TPU v7x, 32 devices: a whole 2x2x4 slice. The times are simulated.
32 devices in a mesh: cuts: 8 (over y, x, core), frame: 4 (over z).
Axes of the slice: x: 2, y: 2, z: 4, core: 2. Of those that a mesh axis runs over, the one named last changes fastest.
Arguments:
- basis: bfloat16 [2, 32, 128, 4, 256], P(None, None, 'cuts', 'frame'), may hold values from -6 to 6
- coil_maps: bfloat16 [2, 12, 128, 4, 256], P(None, None, 'cuts', 'frame'), may hold values from -3 to 3
- factors: bfloat16 [2, 32, 64], P(None, None, 'frame'), may hold values from -0.75 to 0.75
- lines: int32 [64, 16], P(None, 'cuts'), may hold values from 0 to 4095
- kdata: bfloat16 [2, 64, 16, 12, 4], P(None, None, 'cuts', None, 'frame'), may hold values from -6 to 6
Outputs:
- basis_grad: float32 [2, 32, 128, 4, 256], P(None, None, 'cuts', 'frame')
- factor_grad: float32 [2, 32, 64], P(None, None, 'frame')
Inputs may be any that keep to these rules, and one draw needn't show every extreme that they name: lines[t, j] = (ky - (j // 2) * 32) * 128 + kz for a position (ky, kz) sampled in frame t whose ky lies in the rows (j // 2) * 32 to (j // 2 + 1) * 32 - 1; positions may repeat over frames.
All inputs are finite; a program needn't handle non-finite values.
Results may differ from a plain program's by a relative error of at most 0.011.
Values may be sent and summed in bfloat16 or wider, within the bound.
No kernel may reach another device: no remote copies, remote signals or barrier semaphores. Data moves between devices by JAX's collectives and lax.ppermute only.
A program may use at most 64 MiB of HBM per device.

v0:
```python
import math

import jax
import jax.numpy as jnp
from jax import lax
from jax.sharding import PartitionSpec as P

HIGH = lax.Precision.HIGHEST


def twiddle(product, size):
    angle = product.astype(jnp.float32) * (2.0 * math.pi / size)
    factor = 1.0 / math.sqrt(size)
    return (
        (jnp.cos(angle) * factor).astype(jnp.bfloat16),
        (jnp.sin(angle) * factor).astype(jnp.bfloat16),
    )


def dft_table(size, inverse):
    index = jnp.arange(size, dtype=jnp.int32)
    product = index[:, None] * index[None, :] % size
    cosine, sine = twiddle(product, size)
    imag = sine if inverse else -sine
    return jnp.stack([jnp.stack([cosine, imag]), jnp.stack([-imag, cosine])])


def body(basis, coil_maps, factors, lines, kdata):
    n_cuts = lax.axis_size("cuts")
    cut_index = lax.axis_index("cuts")
    slab = basis.shape[2]
    readout = basis.shape[3]
    width = basis.shape[4]
    depth = slab * n_cuts
    ky_rows = width // n_cuts
    lines_dev = lines.shape[1]
    scale = 1.0 / math.sqrt(
        coil_maps.shape[1] * lines_dev * n_cuts * readout * lax.axis_size("frame")
    )
    fwd_y = dft_table(width, False)
    inv_y = dft_table(width, True)
    every = lax.all_gather(factors, "frame", axis=2, tiled=True)
    frames = every.shape[2]
    v_re = every[0]
    v_im = every[1]
    v_re32 = v_re.astype(jnp.float32)
    v_im32 = v_im.astype(jnp.float32)
    b_re = basis[0].astype(jnp.float32)
    b_im = basis[1].astype(jnp.float32)

    def forward_hybrid(maps):
        m_re = maps[0].astype(jnp.float32)[None]
        m_im = maps[1].astype(jnp.float32)[None]
        image = jnp.stack([m_re * b_re - m_im * b_im, m_re * b_im + m_im * b_re]).astype(
            jnp.bfloat16
        )
        return jnp.einsum(
            "plzxy,pqwy->qlzxw", image, fwd_y, preferred_element_type=jnp.float32
        ).astype(jnp.bfloat16)

    def finish(back, maps, grad_acc):
        imgrad = jnp.einsum("plzxw,pqyw->qlzxy", back, inv_y, preferred_element_type=jnp.float32)
        m_re = maps[0].astype(jnp.float32)[None]
        m_im = maps[1].astype(jnp.float32)[None]
        g_re = imgrad[0]
        g_im = imgrad[1]
        return grad_acc + jnp.stack([m_re * g_re + m_im * g_im, m_re * g_im - m_im * g_re])

    all_lines = lax.all_gather(lines, "cuts", axis=1, tiled=True)
    column = jnp.arange(all_lines.shape[1], dtype=jnp.int32) // lines_dev
    ky_all = column[None, :] * ky_rows + all_lines // depth
    kz_all = all_lines % depth
    z_global = cut_index * slab + jnp.arange(slab, dtype=jnp.int32)
    tw_cos, tw_sin = twiddle(kz_all[:, :, None] * z_global[None, None, :] % depth, depth)
    tw_cos = tw_cos.astype(jnp.float32)
    tw_sin = tw_sin.astype(jnp.float32)
    row_index = jnp.arange(frames, dtype=jnp.int32)[:, None] * width + ky_all

    def coil_step(carry, inputs):
        grad_acc, factor_acc = carry
        maps, data = inputs
        hybrid = forward_hybrid(maps)
        h_re = hybrid[0]
        h_im = hybrid[1]
        m_re = jnp.einsum(
            "lzxy,lt->tyzx", h_re, v_re, preferred_element_type=jnp.float32
        ) - jnp.einsum("lzxy,lt->tyzx", h_im, v_im, preferred_element_type=jnp.float32)
        m_im = jnp.einsum(
            "lzxy,lt->tyzx", h_re, v_im, preferred_element_type=jnp.float32
        ) + jnp.einsum("lzxy,lt->tyzx", h_im, v_re, preferred_element_type=jnp.float32)
        table_rows = jnp.stack([m_re, m_im], axis=2).reshape(frames * width, 2 * slab * readout)
        index = row_index
        cos_part = tw_cos[..., None]
        sin_part = tw_sin[..., None]
        fetched = jnp.take(table_rows, index.reshape(-1), axis=0).reshape(
            frames, lax.axis_size("cuts") * lines_dev, 2, slab, readout
        )
        part_re = jnp.sum(cos_part * fetched[:, :, 0] + sin_part * fetched[:, :, 1], axis=2)
        part_im = jnp.sum(cos_part * fetched[:, :, 1] - sin_part * fetched[:, :, 0], axis=2)
        predicted = lax.psum_scatter(
            jnp.stack([part_re, part_im]).transpose(2, 0, 1, 3),
            "cuts",
            scatter_dimension=0,
            tiled=True,
        ).transpose(1, 2, 0, 3)
        resid = (predicted - data.astype(jnp.float32)).astype(jnp.bfloat16)
        empty = jnp.zeros((frames * width, 2 * slab * readout), jnp.float32)
        piece = lax.all_gather(resid, "cuts", axis=2, tiled=True)
        count = piece.shape[2]
        index = row_index
        cos_part = tw_cos[..., None]
        sin_part = tw_sin[..., None]
        r_re = piece[0].astype(jnp.float32)[:, :, None, :]
        r_im = piece[1].astype(jnp.float32)[:, :, None, :]
        values = jnp.stack(
            [cos_part * r_re - sin_part * r_im, cos_part * r_im + sin_part * r_re], axis=2
        )
        spread = empty.at[index.reshape(-1)].add(values.reshape(frames * count, 2 * slab * readout))
        spread = spread.reshape(frames, width, 2, slab, readout)
        e_re = spread[:, :, 0]
        e_im = spread[:, :, 1]
        h_re32 = h_re.astype(jnp.float32)
        h_im32 = h_im.astype(jnp.float32)
        gv_re = jnp.einsum("lzxy,tyzx->lt", h_re32, e_re, precision=HIGH) + jnp.einsum(
            "lzxy,tyzx->lt", h_im32, e_im, precision=HIGH
        )
        gv_im = jnp.einsum("lzxy,tyzx->lt", h_re32, e_im, precision=HIGH) - jnp.einsum(
            "lzxy,tyzx->lt", h_im32, e_re, precision=HIGH
        )
        zg_re = jnp.einsum("tyzx,lt->lzxy", e_re, v_re32, precision=HIGH) + jnp.einsum(
            "tyzx,lt->lzxy", e_im, v_im32, precision=HIGH
        )
        zg_im = jnp.einsum("tyzx,lt->lzxy", e_im, v_re32, precision=HIGH) - jnp.einsum(
            "tyzx,lt->lzxy", e_re, v_im32, precision=HIGH
        )
        back = jnp.stack([zg_re, zg_im]).astype(jnp.bfloat16)
        return ((finish(back, maps, grad_acc), factor_acc + jnp.stack([gv_re, gv_im])), None)

    start_state = (
        jnp.zeros(basis.shape, jnp.float32),
        jnp.zeros((2, basis.shape[1], frames), jnp.float32),
    )
    inputs = (coil_maps.transpose(1, 0, 2, 3, 4), kdata.transpose(3, 0, 1, 2, 4))
    (grad_acc, factor_acc), unused = lax.scan(coil_step, start_state, inputs)
    shared = lax.psum_scatter(factor_acc * scale, "frame", scatter_dimension=2, tiled=True)
    factor_grad = lax.psum(shared, "cuts")
    return (grad_acc, factor_grad)


def solution(mesh):
    placed = (
        P(None, None, "cuts", "frame", None),
        P(None, None, "cuts", "frame", None),
        P(None, None, "frame"),
        P(None, "cuts"),
        P(None, None, "cuts", None, "frame"),
    )
    return jax.shard_map(
        body,
        mesh=mesh,
        in_specs=placed,
        out_specs=(P(None, None, "cuts", "frame", None), P(None, None, "frame")),
        check_vma=False,
    )
```

profile of v0, /device:TPU:0, one launch (start us, length us, event | category | flops | bytes accessed | tf_op | source)
XLA Modules:
  0.0 1078.8 jit_solution(455958249287394084)
XLA Ops:
  9.6 14.8 %all_gather.10 = bf16[2,32,64]{1,0,2:T(2,128)(2,1)S(1)} all-gather(bf16[2,32,16]{1,0,2:T(2,128)(2,1)S(1)} %copy.232), channel_id=1, replica_groups=mesh['cuts'=8,'frame'=4] {'frame'}, dimensions={2}, use_global_device_ids=true | all-gather | bytes 10240 | tf_op jit(solution)/shard_map/all_gather | solution.py:42
  24.7 8.9 all-gather
  36.3 991.8 %while.16 = (s32[]{:T(128)}, f32[2,32,16,1,256]{4,2,0,1,3:T(8,128)}, f32[2,32,64]{2,1,0:T(8,128)S(1)}, bf16[12,2,16,1,256]{4,2,3,1,0:T(8,128)(2,1)S(1)}, s32[64,...) while((s32[]{:T(128)}, ...), condition=%wide.wide.region_5.6_spmd.clone.clone.clone, body=%wide.wide.region_0.5_spmd.clone.clone.clone.sunk | while | flops 1416108800 | bytes 72538176 | solution.py:144
  45.7 6.2 gather_fusion
  55.4 23.5 %all-reduce.3 = f32[16,2,64,1]{2,1,3,0:T(2,128)S(1)} all-reduce(f32[16,2,64,1]{2,1,3,0:T(2,128)S(1)} %copy.322), channel_id=2, replica_groups=mesh['cuts'=8,'frame'=4] {'cuts'}, use_global_device_ids=true, to_apply=%region_3.3.clone | all-reduce | flops 2048 | bytes 16384 | tf_op jit(solution)/shard_map/while
  80.9 8.9 all_gather.16
  93.1 9.7 scatter_custom_fusion.10
  102.8 6.3 copy.326
  128.8 6.2 gather_fusion
  138.5 23.5 %all-reduce.3 = f32[16,2,64,1]{2,1,3,0:T(2,128)S(1)} all-reduce(f32[16,2,64,1]{2,1,3,0:T(2,128)S(1)} %copy.322), channel_id=2, replica_groups=mesh['cuts'=8,'frame'=4] {'cuts'}, use_global_device_ids=true, to_apply=%region_3.3.clone | all-reduce | flops 2048 | bytes 16384 | tf_op jit(solution)/shard_map/while
  164.0 7.9 all_gather.16
  175.2 9.7 scatter_custom_fusion.10
  185.0 6.3 copy.326
  211.0 6.2 gather_fusion
  220.7 23.6 %all-reduce.3 = f32[16,2,64,1]{2,1,3,0:T(2,128)S(1)} all-reduce(f32[16,2,64,1]{2,1,3,0:T(2,128)S(1)} %copy.322), channel_id=2, replica_groups=mesh['cuts'=8,'frame'=4] {'cuts'}, use_global_device_ids=true, to_apply=%region_3.3.clone | all-reduce | flops 2048 | bytes 16384 | tf_op jit(solution)/shard_map/while
  246.2 8.9 all_gather.16
  258.4 9.7 scatter_custom_fusion.10
  268.1 6.3 copy.326
  294.1 6.2 gather_fusion
  303.8 23.6 %all-reduce.3 = f32[16,2,64,1]{2,1,3,0:T(2,128)S(1)} all-reduce(f32[16,2,64,1]{2,1,3,0:T(2,128)S(1)} %copy.322), channel_id=2, replica_groups=mesh['cuts'=8,'frame'=4] {'cuts'}, use_global_device_ids=true, to_apply=%region_3.3.clone | all-reduce | flops 2048 | bytes 16384 | tf_op jit(solution)/shard_map/while
  329.3 7.9 all_gather.16
  340.6 9.7 scatter_custom_fusion.10
  350.3 6.3 copy.326
  376.3 6.2 gather_fusion
  386.0 23.5 %all-reduce.3 = f32[16,2,64,1]{2,1,3,0:T(2,128)S(1)} all-reduce(f32[16,2,64,1]{2,1,3,0:T(2,128)S(1)} %copy.322), channel_id=2, replica_groups=mesh['cuts'=8,'frame'=4] {'cuts'}, use_global_device_ids=true, to_apply=%region_3.3.clone | all-reduce | flops 2048 | bytes 16384 | tf_op jit(solution)/shard_map/while
  411.5 8.9 all_gather.16
  423.7 9.7 scatter_custom_fusion.10
  433.4 6.3 copy.326
  459.5 6.2 gather_fusion
  469.1 23.5 %all-reduce.3 = f32[16,2,64,1]{2,1,3,0:T(2,128)S(1)} all-reduce(f32[16,2,64,1]{2,1,3,0:T(2,128)S(1)} %copy.322), channel_id=2, replica_groups=mesh['cuts'=8,'frame'=4] {'cuts'}, use_global_device_ids=true, to_apply=%region_3.3.clone | all-reduce | flops 2048 | bytes 16384 | tf_op jit(solution)/shard_map/while
  494.6 7.9 all_gather.16
  505.9 9.7 scatter_custom_fusion.10
  515.6 6.3 copy.326
  541.6 6.2 gather_fusion
  551.3 23.6 %all-reduce.3 = f32[16,2,64,1]{2,1,3,0:T(2,128)S(1)} all-reduce(f32[16,2,64,1]{2,1,3,0:T(2,128)S(1)} %copy.322), channel_id=2, replica_groups=mesh['cuts'=8,'frame'=4] {'cuts'}, use_global_device_ids=true, to_apply=%region_3.3.clone | all-reduce | flops 2048 | bytes 16384 | tf_op jit(solution)/shard_map/while
  576.8 8.9 all_gather.16
  589.0 9.7 scatter_custom_fusion.10
  598.7 6.3 copy.326
  624.8 6.2 gather_fusion
  634.4 23.6 %all-reduce.3 = f32[16,2,64,1]{2,1,3,0:T(2,128)S(1)} all-reduce(f32[16,2,64,1]{2,1,3,0:T(2,128)S(1)} %copy.322), channel_id=2, replica_groups=mesh['cuts'=8,'frame'=4] {'cuts'}, use_global_device_ids=true, to_apply=%region_3.3.clone | all-reduce | flops 2048 | bytes 16384 | tf_op jit(solution)/shard_map/while
  659.9 7.9 all_gather.16
  671.2 9.7 scatter_custom_fusion.10
  680.9 6.3 copy.326
  706.9 6.2 gather_fusion
  716.6 23.5 %all-reduce.3 = f32[16,2,64,1]{2,1,3,0:T(2,128)S(1)} all-reduce(f32[16,2,64,1]{2,1,3,0:T(2,128)S(1)} %copy.322), channel_id=2, replica_groups=mesh['cuts'=8,'frame'=4] {'cuts'}, use_global_device_ids=true, to_apply=%region_3.3.clone | all-reduce | flops 2048 | bytes 16384 | tf_op jit(solution)/shard_map/while
  742.1 8.9 all_gather.16
  754.3 9.7 scatter_custom_fusion.10
  764.0 6.3 copy.326
  790.1 6.2 gather_fusion
  799.7 23.5 %all-reduce.3 = f32[16,2,64,1]{2,1,3,0:T(2,128)S(1)} all-reduce(f32[16,2,64,1]{2,1,3,0:T(2,128)S(1)} %copy.322), channel_id=2, replica_groups=mesh['cuts'=8,'frame'=4] {'cuts'}, use_global_device_ids=true, to_apply=%region_3.3.clone | all-reduce | flops 2048 | bytes 16384 | tf_op jit(solution)/shard_map/while
  825.2 7.9 all_gather.16
  836.5 9.7 scatter_custom_fusion.10
  846.2 6.3 copy.326
  872.2 6.2 gather_fusion
  881.9 23.6 %all-reduce.3 = f32[16,2,64,1]{2,1,3,0:T(2,128)S(1)} all-reduce(f32[16,2,64,1]{2,1,3,0:T(2,128)S(1)} %copy.322), channel_id=2, replica_groups=mesh['cuts'=8,'frame'=4] {'cuts'}, use_global_device_ids=true, to_apply=%region_3.3.clone | all-reduce | flops 2048 | bytes 16384 | tf_op jit(solution)/shard_map/while
  907.4 8.9 all_gather.16
  919.6 9.7 scatter_custom_fusion.10
  929.3 6.3 copy.326
  965.0 23.6 %all-reduce.3 = f32[16,2,64,1]{2,1,3,0:T(2,128)S(1)} all-reduce(f32[16,2,64,1]{2,1,3,0:T(2,128)S(1)} %copy.322), channel_id=2, replica_groups=mesh['cuts'=8,'frame'=4] {'cuts'}, use_global_device_ids=true, to_apply=%region_3.3.clone | all-reduce | flops 2048 | bytes 16384 | tf_op jit(solution)/shard_map/while
  990.5 7.9 all_gather.16
  1001.8 9.7 scatter_custom_fusion.10
  1011.5 6.3 copy.326
  1032.2 15.9 %reduce-scatter.4.cloned.1.call-done = f32[16,64]{1,0:T(8,128)} async-done(((f32[64,64]{1,0:T(8,128)}), f32[16,64]{1,0:T(8,128)}) %reduce-scatter.4.cloned.1.call-update) | async-done | bytes 4112
  1049.0 22.3 %psum.7 = f32[2,32,16]{2,1,0:T(8,128)S(1)} all-reduce(f32[2,32,16]{2,1,0:T(8,128)S(1)} %copy.247), channel_id=1, replica_groups=mesh['cuts'=8,'frame'=4] {'cuts'}, use_global_device_ids=true, to_apply=%region_7.8 | all-reduce | flops 1024 | bytes 8192 | tf_op jit(solution)/shard_map/psum | solution.py:146
  (692 shorter events, 348.1 us)
Async XLA Ops:
  7.2 2.5 copy-start.8
  7.2 17.5 %copy-start.9 = (s32[64,2]{0,1:T(2,128)S(1)}, s32[64,2]{0,1:T(2,128)}, u32[]{:S(2)}) copy-start(s32[64,2]{0,1:T(2,128)} %param.10) | copy-start | bytes 1540
  7.2 1040.9 %reduce-scatter.4.cloned.1.call-start = ((), (), s32[]{:S(2)}) async-start(), calls=%async_computation.1 | async-start | bytes 40960
  8.3 25.5 %copy-start.3 = (bf16[2,32,16,1,256]{4,2,3,1,0:T(8,128)(2,1)S(1)}, bf16[2,32,16,1,256]{4,2,3,1,0:T(8,128)(2,1)}, u32[]{:S(2)}) copy-start(bf16[2,32,16,1,256]{4,2,3,1,0:T(8,128)(2,1)} %param.7) | copy-start | bytes 1572868
  9.5 25.3 %copy-start.6 = (bf16[2,12,16,1,256]{4,2,3,1,0:T(8,128)(2,1)S(1)}, bf16[2,12,16,1,256]{4,2,3,1,0:T(8,128)(2,1)}, u32[]{:S(2)}) copy-start(bf16[2,12,16,1,256]{4,2,3,1,0:T(8,128)(2,1)} %param.8) | copy-start | bytes 589828
  9.5 25.3 %copy-start.7 = (bf16[2,64,2,12,1]{1,2,4,3,0:T(2,128)(2,1)S(1)}, bf16[2,64,2,12,1]{1,2,4,3,0:T(2,128)(2,1)}, u32[]{:S(2)}) copy-start(bf16[2,64,2,12,1]{1,2,4,3,0:T(2,128)(2,1)} %param.11) | copy-start | bytes 18436
  9.6 26.7 %copy-start.10 = (u32[32]{0:T(128)S(1)}, u32[32]{0:T(128)}, u32[]{:S(2)}) copy-start(u32[32]{0:T(128)} %constant.280) | copy-start | bytes 388
  36.3 1.9 copy-start.4
  115.4 1.5 copy-start.2
  116.8 1.2 copy-start
  117.5 1.9 copy-start.5
  118.4 1.0 copy-start.1
  119.4 1.9 copy-start.4
  197.5 1.5 copy-start.2
  199.0 1.2 copy-start
  199.7 1.9 copy-start.5
  200.6 1.0 copy-start.1
  201.6 1.9 copy-start.4
  280.7 1.5 copy-start.2
  282.1 1.2 copy-start
  282.8 1.9 copy-start.5
  283.7 1.0 copy-start.1
  284.7 1.9 copy-start.4
  362.9 1.5 copy-start.2
  364.3 1.2 copy-start
  365.0 1.9 copy-start.5
  365.9 1.0 copy-start.1
  366.9 1.9 copy-start.4
  446.0 1.5 copy-start.2
  447.5 1.2 copy-start
  448.1 1.9 copy-start.5
  449.0 1.0 copy-start.1
  450.0 1.9 copy-start.4
  528.2 1.5 copy-start.2
  529.6 1.2 copy-start
  530.3 1.9 copy-start.5
  531.2 1.0 copy-start.1
  532.2 1.9 copy-start.4
  611.3 1.5 copy-start.2
  612.8 1.2 copy-start
  613.4 1.9 copy-start.5
  614.3 1.0 copy-start.1
  615.3 1.9 copy-start.4
  693.5 1.5 copy-start.2
  694.9 1.2 copy-start
  695.6 1.9 copy-start.5
  697.5 1.9 copy-start.4
  776.6 1.5 copy-start.2
  778.1 1.2 copy-start
  778.7 1.9 copy-start.5
  779.6 1.0 copy-start.1
  780.6 1.9 copy-start.4
  858.8 1.5 copy-start.2
  860.2 1.2 copy-start
  860.9 1.9 copy-start.5
  862.8 1.9 copy-start.4
  941.9 1.5 copy-start.2
  943.4 1.2 copy-start
  944.0 1.9 copy-start.5
  944.9 1.0 copy-start.1
  945.9 1.9 copy-start.4
  1024.1 1.5 copy-start.2
  1025.5 1.2 copy-start
  1026.2 1.9 copy-start.5
  (3 other events, 3.0 us)
Sparse Core Ops, SparseCore 0:
  1029.1 18.9 reduce-scatter.3
where the time goes:
time: 1080 us
  blocking collectives  429 us (40%)
  local copies, waits for them, and re-layouts  299 us (28%)
  other arithmetic  217 us (20%)
  matrix products  92.2 us (9%)
  waiting for transfers between devices  15.9 us (1%)
  between operations  14.2 us (1%)
  loops' own time  11.3 us (1%)
    while x12, blocking collectives  283 us
    scatter-add x12, other arithmetic, coil_step(): empty.at[index.reshape(-1)]  117 us
    all_gather x12, blocking collectives, coil_step(): piece = lax.all_gather(resid, 'cuts', axis=2, tiled=True)  101 us
    gather x36, local copies, waits for them, and re-layouts, coil_step(): jnp.take(table_rows, index.reshape(-1), axis=0)  80.7 us
    scatter-add x12, local copies, waits for them, and re-layouts, coil_step(): empty.at[index.reshape(-1)]  75.3 us
    while x156, local copies, waits for them, and re-layouts  67.4 us
    reshape x12, local copies, waits for them, and re-layouts, coil_step(): jnp.stack([m_re, m_im], axis=2).reshape(frames * width, 2 * slab * readout)  55.8 us
    reduce_sum x12, other arithmetic, coil_step(): jnp.sum(cos_part * fetched[:, :, 0] + sin_part * fetched[:, :, 1], axis=2)  31.8 us
  transfers between devices with their start and end apart: 1, of which 1 were waited for; matrix products, arithmetic and copies ran while one was open for 0% of the time, Pallas kernels for 0%

commit v1 on v0

v1 whole, which is shorter than its diff:
```python
import functools
import math

import jax
import jax.numpy as jnp
import numpy as np
from jax import lax
from jax.experimental import pallas as pl
from jax.experimental.pallas import tpu as pltpu
from jax.sharding import PartitionSpec as P

F32 = jnp.float32
BF16 = jnp.bfloat16
LANES = 128
TILE = 16


def dft_parts(size):
    index = np.arange(size, dtype=np.int64)
    angle = ((index[:, None] * index[None, :]) % size).astype(np.float64) * (2.0 * math.pi / size)
    factor = 1.0 / math.sqrt(size)
    return (np.cos(angle) * factor).astype(BF16), (np.sin(angle) * factor).astype(BF16)


def nn(a, b):
    return lax.dot_general(a, b, (((1,), (0,)), ((), ())), preferred_element_type=F32)


def nt(a, b):
    return lax.dot_general(a, b, (((1,), (1,)), ((), ())), preferred_element_type=F32)


def tn(a, b):
    return lax.dot_general(a, b, (((0,), (0,)), ((), ())), preferred_element_type=F32)


def total(refs):
    value = refs[0][...].astype(F32)
    for ref in refs[1:]:
        value = value + ref[...].astype(F32)
    return value


def factor_matrix(refs):
    v = total(refs)
    rank = v.shape[1] // 2
    v_re, v_im = v[:, :rank], v[:, rank:]
    top = jnp.concatenate([v_re, -v_im], axis=1)
    bottom = jnp.concatenate([v_im, v_re], axis=1)
    return jnp.concatenate([top, bottom], axis=0).astype(BF16)


def predict_kernel(n_v, n_line, frames, slab, *refs):
    v_refs, refs = refs[:n_v], refs[n_v:]
    line_refs, refs = refs[:n_line], refs[n_line:]
    (b_ref, m_ref, taby_ref, tabz_ref, coil_ref, kd_ref, pred_ref, w_ref, fz_ref, i_ref, x_ref) = refs
    width = b_ref.shape[2]
    rows = m_ref.shape[1]
    pad = x_ref.shape[1]
    depth = tabz_ref.shape[0]
    samples = w_ref.shape[0]
    per = samples // frames
    coils = rows // slab

    pos = total(line_refs)
    groups = pos.shape[0] // 2
    ky = pos[:groups].T
    kz = pos[groups:].T
    at_y = lax.broadcasted_iota(jnp.int32, (LANES, width), 1).astype(F32)
    at_z = lax.broadcasted_iota(jnp.int32, (LANES, depth), 1).astype(F32)
    for g in range(groups):
        hot_y = jnp.where(at_y == ky[:, g : g + 1], 1.0, 0.0).astype(BF16)
        w_ref[g * LANES : (g + 1) * LANES, :] = nn(hot_y, taby_ref[...]).astype(BF16)
        hot_z = jnp.where(at_z == kz[:, g : g + 1], 1.0, 0.0).astype(BF16)
        fz_ref[g * LANES : (g + 1) * LANES, :] = nn(hot_z, tabz_ref[...]).astype(BF16)

    v = factor_matrix(v_refs)
    halves = width // LANES
    for z in range(slab):
        image = nn(v, b_ref[z])
        for h in range(halves):
            i_ref[h, z * 2 * frames : (z + 1) * 2 * frames, :] = image[
                :, h * LANES : (h + 1) * LANES
            ]

    m_re = m_ref[0].reshape(coils, slab, width)
    m_im = m_ref[1].reshape(coils, slab, width)

    def frame(t, carry):
        i_re, i_im = (
            jnp.concatenate(
                [i_ref[h, pl.ds(at, slab, stride=2 * frames), :] for h in range(halves)], axis=1
            ).astype(BF16)[None]
            for at in (t, frames + t)
        )
        p_re = (m_re * i_re - m_im * i_im).reshape(rows, width)
        p_im = (m_re * i_im + m_im * i_re).reshape(rows, width)
        at = pl.ds(pl.multiple_of(t * per, TILE), per)
        w = w_ref[at, :]
        lhs = jnp.concatenate([w[:, : 2 * width], w[:, 2 * width :]], axis=0)
        y = nt(lhs[:, :width], p_re) + nt(lhs[:, width:], p_im)
        y_re, y_im = y[:per], y[per:]
        f = fz_ref[at, :].astype(F32)
        f_cos, f_sin = f[:, :rows], f[:, pad : pad + rows]
        x_re = y_re * f_cos + y_im * f_sin
        x_im = y_im * f_cos - y_re * f_sin
        base = pl.multiple_of(t * 2 * per, TILE)
        x_ref[pl.ds(base, 2 * per), :rows] = jnp.concatenate([x_re, x_im], axis=0).astype(BF16)
        return carry

    lax.fori_loop(0, frames, frame, 0, unroll=2)
    chunk = min(512, 2 * samples)
    for s in range(0, 2 * samples, chunk):
        part = nt(coil_ref[:, :rows], x_ref[s : s + chunk, :rows])
        pred_ref[:, s : s + chunk] = (part - kd_ref[:, s : s + chunk].astype(F32)).astype(BF16)


def gradient_kernel(n_v, n_r, frames, slab, scale, *refs):
    v_refs, refs = refs[:n_v], refs[n_v:]
    r_refs, refs = refs[:n_r], refs[n_r:]
    (b_ref, m_ref, coil_ref, w_ref, fz_ref, grad_ref, fg_ref, g_ref, r_ref, mf_ref) = refs
    width = b_ref.shape[2]
    rows = m_ref.shape[1]
    pad = coil_ref.shape[1]
    samples = w_ref.shape[0]
    per = samples // frames
    coils = rows // slab

    resid = total(r_refs).astype(BF16)
    chunk = min(512, 2 * samples)
    for s in range(0, 2 * samples, chunk):
        r_ref[s : s + chunk, :] = tn(resid[:, s : s + chunk], coil_ref[...])
    mf_ref[...] = m_ref[...].astype(F32)
    halves = width // LANES

    def frame(t, carry):
        at = pl.ds(pl.multiple_of(t * per, TILE), per)
        w = w_ref[at, :]
        rhs = jnp.concatenate([w[:, : 2 * width], w[:, 2 * width :]], axis=0)
        f = fz_ref[at, :].astype(F32)
        f_cos, f_sin = f[:, :pad], f[:, pad:]
        base = pl.multiple_of(t * 2 * per, TILE)
        r = r_ref[pl.ds(base, 2 * per), :]
        r_re, r_im = r[:per], r[per:]
        q = jnp.concatenate([r_re * f_cos - r_im * f_sin, r_im * f_cos + r_re * f_sin], axis=0)
        u = tn(q[:, :rows].astype(BF16), rhs)
        u_re = u[:, :width].reshape(coils, slab, width)
        u_im = u[:, width:].reshape(coils, slab, width)
        m_re = mf_ref[0].reshape(coils, slab, width)
        m_im = mf_ref[1].reshape(coils, slab, width)
        g_re = jnp.sum(m_re * u_re + m_im * u_im, axis=0)
        g_im = jnp.sum(m_re * u_im - m_im * u_re, axis=0)
        for h in range(halves):
            lanes = slice(h * LANES, (h + 1) * LANES)
            g_ref[h, pl.ds(t, slab, stride=2 * frames), :] = g_re[:, lanes]
            g_ref[h, pl.ds(frames + t, slab, stride=2 * frames), :] = g_im[:, lanes]
        return carry

    lax.fori_loop(0, frames, frame, 0, unroll=2)
    v = factor_matrix(v_refs)
    rank = v.shape[1] // 2
    acc = jnp.zeros((2 * frames, 2 * rank), F32)
    for z in range(slab):
        at = pl.ds(z * 2 * frames, 2 * frames)
        g = jnp.concatenate([g_ref[h, at, :] for h in range(halves)], axis=1).astype(BF16)
        acc = acc + nt(g, b_ref[z])
        grad = tn(v, g)
        for h in range(halves):
            grad_ref[pl.ds(z * halves + h, 2 * rank, stride=slab * halves), :] = grad[
                :, h * LANES : (h + 1) * LANES
            ]
    top, bottom = acc[:frames], acc[frames:]
    g_re = top[:, :rank] + bottom[:, rank:]
    g_im = bottom[:, :rank] - top[:, rank:]
    fg_ref[...] = jnp.concatenate([g_re, g_im], axis=1) * scale


def stages(size):
    steps, stride = [], 1
    if (size.bit_length() - 1) % 2:
        steps.append((1, 2))
        stride = 2
    while stride < size:
        steps.append((stride, 4))
        stride *= 4
    return steps


def swap(value, axis, distance):
    size = lax.axis_size(axis)
    return lax.ppermute(value, axis, [(i, i ^ distance) for i in range(size)])


def shares(value, axis):
    steps = stages(lax.axis_size(axis))
    for number, (stride, radix) in enumerate(steps):
        terms = [value] + [swap(value, axis, stride * d) for d in range(1, radix)]
        if number + 1 < len(steps):
            value = functools.reduce(
                lambda a, b: a + b, [term.astype(F32) for term in terms]
            ).astype(value.dtype)
    return terms


def call(kernel, outs, scratch, flops, *operands):
    nbytes = sum(math.prod(x.shape) * x.dtype.itemsize for x in operands)
    return pl.pallas_call(
        kernel,
        out_shape=outs,
        scratch_shapes=scratch,
        compiler_params=pltpu.CompilerParams(vmem_limit_bytes=56 * 1024 * 1024),
        cost_estimate=pl.CostEstimate(flops=flops, bytes_accessed=nbytes, transcendentals=0),
    )(*operands)


def one_position(basis, coil_maps, factors, lines, kdata, scale):
    n_cuts, n_frame = lax.axis_size("cuts"), lax.axis_size("frame")
    cut, part = lax.axis_index("cuts"), lax.axis_index("frame")
    rank, slab, width = basis.shape[1:]
    coils = coil_maps.shape[1]
    own = lines.shape[1]
    frames = lines.shape[0]
    per = own * n_cuts
    samples = frames * per
    depth = slab * n_cuts
    ky_rows = width // n_cuts

    spread = max(1, TILE // slab)
    tall = spread * slab
    coil_groups = -(-coils // spread)
    rows = coil_groups * tall
    pad = -(-rows // LANES) * LANES
    coil_rows = -(-coils // TILE) * TILE

    kind = BF16 if max(width, depth) <= 256 else F32
    mine = jnp.stack([cut * ky_rows + lines // depth, lines % depth])
    column_owner = jnp.arange(per, dtype=jnp.int32) // own == cut
    placed = jnp.where(column_owner, jnp.tile(mine, (1, 1, n_cuts)), 0)
    line_terms = shares(placed.astype(kind).reshape(2 * samples // LANES, LANES), "cuts")
    turned = factors.transpose(2, 0, 1).reshape(factors.shape[2], 2 * rank)
    row_owner = jnp.arange(frames, dtype=jnp.int32)[:, None] // factors.shape[2] == part
    v_terms = shares(
        jnp.where(row_owner, jnp.tile(turned, (n_frame, 1)), jnp.zeros((), BF16)), "frame"
    )

    tab_cos, tab_sin = dft_parts(width)
    taby = jnp.asarray(np.concatenate([tab_cos, tab_sin, -tab_sin, tab_cos], axis=1))
    z_cos, z_sin = dft_parts(depth)
    tabz = lax.dynamic_slice_in_dim(jnp.asarray(np.stack([z_cos, z_sin])), cut * slab, slab, axis=2)
    tabz = jnp.pad(jnp.tile(tabz, (1, 1, rows // slab)), ((0, 0), (0, 0), (0, pad - rows)))
    tabz = jnp.concatenate([tabz[0], tabz[1]], axis=1)
    row_coil = np.arange(pad) // slab
    coil_of = jnp.asarray(
        ((row_coil[None] == np.arange(coil_rows)[:, None]) & (row_coil[None] < coils)).astype(BF16)
    )

    b_rows = jnp.tile(basis.reshape(2 * rank, slab, width).transpose(1, 0, 2), (spread, 1, 1))
    m_rows = jnp.pad(coil_maps, ((0, 0), (0, coil_groups * spread - coils), (0, 0), (0, 0)))
    m_rows = m_rows.reshape(2, rows, width)
    kd = jnp.tile(kdata.transpose(3, 1, 0, 2), (1, 1, 1, n_cuts))
    kd = jnp.where(column_owner, kd, jnp.zeros((), BF16)).reshape(coils, 2 * samples)
    kd = jnp.pad(kd, ((0, coil_rows - coils), (0, 0)))

    flops = 2 * frames * 2 * per * rows * 2 * width
    predicted, w, fz = call(
        functools.partial(predict_kernel, len(v_terms), len(line_terms), frames, tall),
        (
            jax.ShapeDtypeStruct((coil_rows, 2 * samples), BF16),
            jax.ShapeDtypeStruct((samples, 4 * width), BF16),
            jax.ShapeDtypeStruct((samples, 2 * pad), BF16),
        ),
        [pltpu.VMEM((width // LANES, tall * 2 * frames, LANES), F32), pltpu.VMEM((2 * samples, pad), BF16)],
        flops,
        *v_terms, *line_terms, b_rows, m_rows, taby, tabz, coil_of, kd,
    )
    resid_terms = shares(predicted, "cuts")
    grad, fg = call(
        functools.partial(
            gradient_kernel, len(v_terms), len(resid_terms), frames, tall, scale
        ),
        (
            jax.ShapeDtypeStruct((2 * rank * tall * width // LANES, LANES), F32),
            jax.ShapeDtypeStruct((frames, 2 * rank), F32),
        ),
        [
            pltpu.VMEM((width // LANES, tall * 2 * frames, LANES), F32),
            pltpu.VMEM((2 * samples, pad), F32),
            pltpu.VMEM((2, rows, width), F32),
        ],
        flops,
        *v_terms, *resid_terms, b_rows, m_rows, coil_of, w, fz,
    )
    if spread > 1:
        grad = jnp.sum(grad.reshape(2, rank, spread, slab, width), axis=2)
    return grad.reshape(2, rank, slab, width), fg


def body(basis, coil_maps, factors, lines, kdata):
    n_cuts, n_frame = lax.axis_size("cuts"), lax.axis_size("frame")
    readout = basis.shape[3]
    rank = basis.shape[1]
    own = factors.shape[2]
    scale = 1.0 / math.sqrt(coil_maps.shape[1] * lines.shape[1] * n_cuts * readout * n_frame)
    grads, fg = [], 0.0
    for x in range(readout):
        grad, term = one_position(
            basis[:, :, :, x], coil_maps[:, :, :, x], factors, lines, kdata[..., x], scale
        )
        grads.append(grad)
        fg = fg + term
    basis_grad = grads[0][:, :, :, None] if readout == 1 else jnp.stack(grads, axis=3)
    pieces = jnp.broadcast_to(
        fg.reshape(1, n_frame, own, 2 * rank), (n_cuts, n_frame, own, 2 * rank)
    ).reshape(n_cuts * n_frame, own, 2 * rank)
    gathered = lax.all_to_all(pieces, ("cuts", "frame"), 0, 0, tiled=True)
    factor_grad = jnp.sum(gathered, axis=0).reshape(own, 2, rank).transpose(1, 2, 0)
    return basis_grad, factor_grad


def solution(mesh):
    placed = (
        P(None, None, "cuts", "frame", None),
        P(None, None, "cuts", "frame", None),
        P(None, None, "frame"),
        P(None, "cuts"),
        P(None, None, "cuts", None, "frame"),
    )
    return jax.shard_map(
        body,
        mesh=mesh,
        in_specs=placed,
        out_specs=(P(None, None, "cuts", "frame", None), P(None, None, "frame")),
        check_vma=False,
    )
```

time: 1080 us -> 76.9 us (0.07)
  blocking collectives: 429 us -> 13.3 us
  local copies, waits for them, and re-layouts: 299 us -> 8.77 us
  other arithmetic: 217 us -> 3.33 us
  matrix products: 92.2 us -> 0 us
  Pallas kernels: 0 us -> 29.7 us
  starting transfers between devices: 0.04 us -> 15.3 us
  between operations: 14.2 us -> 0.88 us
  loops' own time: 11.3 us -> 0 us
    while x12 -> x0, blocking collectives: 283 us -> none
    all_gather x14 -> x0, blocking collectives: 124 us -> none  [the longest x12 101 us: coil_step(): piece = lax.all_gather(resid, 'cuts', axis=2, tiled=True)]
    scatter-add x12 -> x0, other arithmetic: 117 us -> none  [coil_step(): empty.at[index.reshape(-1)]]
    dot_general x168 -> x0, matrix products: 92.2 us -> none  [the longest x12 8.25 us: coil_step(): jnp.einsum('tyzx,lt->lzxy', e_im, v_im32, precision=HIGH)]
    gather x36 -> x0, local copies, waits for them, and re-layouts: 80.7 us -> none  [coil_step(): jnp.take(table_rows, index.reshape(-1), axis=0)]
    scatter-add x12 -> x0, local copies, waits for them, and re-layouts: 75.3 us -> none  [coil_step(): empty.at[index.reshape(-1)]]
    while x156 -> x0, local copies, waits for them, and re-layouts: 67.4 us -> none
    reshape x37 -> x1, local copies, waits for them, and re-layouts: 65.7 us -> 0.08 us  [body(): jnp.sum(gathered, axis=0).reshape(own, 2, rank).transpose(1, 2, 0)]
  transfers between devices with their start and end apart: 1 -> 11, of which waited for: 1 -> 5; matrix products, arithmetic and copies ran while one was open for 0% -> 8% of each run, Pallas kernels for 0% -> 0%
where the time goes in v1:
time: 76.9 us; the launch traced here: 76.5 us
  Pallas kernels  29.7 us (39%)
  starting transfers between devices  15.3 us (20%)
  blocking collectives  13.3 us (17%)
  local copies, waits for them, and re-layouts  8.77 us (11%)
  waiting for transfers between devices  5.29 us (7%)
  other arithmetic  3.33 us (4%)
  between operations  0.88 us (1%)
    pallas_call x2, Pallas kernels, call(): pl.pallas_call(kernel, out_shape=outs, scratch_shapes=scratch, compiler_p...  29.7 us
    ppermute x11, starting transfers between devices, swap(): return lax.ppermute(value, axis, [(i, i ^ distance) for i in range(size)])  15.3 us
    all_to_all x1, blocking collectives, body(): gathered = lax.all_to_all(pieces, ('cuts', 'frame'), 0, 0, tiled=True)  13.3 us
    ppermute x11, waiting for transfers between devices, swap(): return lax.ppermute(value, axis, [(i, i ^ distance) for i in range(size)])  5.29 us
    unnamed x30, local copies, waits for them, and re-layouts  3.08 us
  transfers between devices with their start and end apart: 11, of which 5 were waited for; matrix products, arithmetic and copies ran while one was open for 8% of the time, Pallas kernels for 0%

profile of v1, /device:TPU:0, one launch (start us, length us, event | category | flops | bytes accessed | tf_op | source)
XLA Modules:
  0.0 76.5 jit_solution(10108918170699174293)
XLA Ops:
  0.6 0.0 copy-start
  0.7 0.8 copy.22
  1.4 0.1 tile.18
  1.5 0.1 bitcast_select_fusion.refs_0_
  1.6 3.1 %collective-permute-start = (bf16[64,64]{1,0:T(8,128)(2,1)S(1)}, bf16[64,64]{1,0:T(8,128)(2,1)S(1)}, u32[]{:S(2)}, u32[]{:S(2)}) collective-permute-start(bf16[64,64]{1,0:T(8,128)(2,1)S(1)} %bitcast_select_fusion.refs_0_), channel_id=1, source_target_pairs={{0,1},{1,0},{2,3},{3,2},{4,5},{5,4},{6,7},{7,6},{8,9},{9,8},{10,11... | collective-permute-start | bytes 24584 | tf_op jit(solution)/shard_map/ppermute | solution.py:191
  4.7 2.6 %collective-permute-start.1 = (bf16[64,64]{1,0:T(8,128)(2,1)S(1)}, bf16[64,64]{1,0:T(8,128)(2,1)S(1)}, u32[]{:S(2)}, u32[]{:S(2)}) collective-permute-start(bf16[64,64]{1,0:T(8,128)(2,1)S(1)} %bitcast_select_fusion.refs_0_), channel_id=1, source_target_pairs={{0,2},{1,3},{2,0},{3,1},{4,6},{5,7},{6,4},{7,5},{8,10},{9,11},{10,... | collective-permute-start | bytes 24584 | tf_op jit(solution)/shard_map/ppermute | solution.py:191
  7.3 0.0 collective-permute-start.2
  7.3 0.7 add_bitcast_fusion
  8.0 0.1 copy.23
  8.1 0.3 tile.41
  8.4 0.1 broadcast_in_dim.45
  8.5 0.1 collective-permute-start.3
  8.6 0.1 broadcast_in_dim.48
  8.7 0.8 %copy.26 = bf16[12,64,2,2]{0,3,2,1:T(2,128)(2,1)S(1)} copy(bf16[12,64,2,2]{1,3,0,2:T(2,128)(2,1)} %bitcast.37) | data formatting | bytes 12288 | tf_op jit(solution)/shard_map/transpose | solution.py:260
  9.6 0.3 tile.44
  9.9 0.2 copy.27
  10.1 0.7 constant_dynamic-slice_fusion
  10.8 0.1 copy.25
  10.9 0.0 collective-permute-done.3
  11.0 0.0 copy-start.9
  11.0 1.8 %collective-permute-start.4 = (bf16[16,128]{1,0:T(8,128)(2,1)S(1)}, bf16[16,128]{1,0:T(8,128)(2,1)S(1)}, u32[]{:S(2)}, u32[]{:S(2)}) collective-permute-start(bf16[16,128]{1,0:T(8,128)(2,1)S(1)} %add_convert_fusion.1.refs_4_), channel_id=1, source_target_pairs={{0,8},{4,12},{8,0},{12,4},{16,24},{20,28},{24,16},{28,20},{1,9},{5... | collective-permute-start | bytes 12296 | tf_op jit(solution)/shard_map/ppermute | solution.py:191
  12.8 1.6 %collective-permute-start.5 = (bf16[16,128]{1,0:T(8,128)(2,1)S(1)}, bf16[16,128]{1,0:T(8,128)(2,1)S(1)}, u32[]{:S(2)}, u32[]{:S(2)}) collective-permute-start(bf16[16,128]{1,0:T(8,128)(2,1)S(1)} %add_convert_fusion.1.refs_4_), channel_id=1, source_target_pairs={{0,16},{4,20},{8,24},{12,28},{16,0},{20,4},{24,8},{28,12},{1,17},{... | collective-permute-start | bytes 12296 | tf_op jit(solution)/shard_map/ppermute | solution.py:191
  14.4 0.3 collective-permute-done.4.refs_5_
  14.7 2.7 %collective-permute-start.6 = (bf16[16,128]{1,0:T(8,128)(2,1)S(1)}, bf16[16,128]{1,0:T(8,128)(2,1)S(1)}, u32[]{:S(2)}, u32[]{:S(2)}) collective-permute-start(bf16[16,128]{1,0:T(8,128)(2,1)S(1)} %add_convert_fusion.1.refs_4_), channel_id=1, source_target_pairs={{0,24},{4,28},{8,16},{12,20},{16,8},{20,12},{24,0},{28,4},{1,25},{... | collective-permute-start | bytes 12296 | tf_op jit(solution)/shard_map/ppermute | solution.py:191
  17.3 0.7 pad_maximum_fusion.refs_11_
  18.0 0.0 copy-done
  18.0 1.0 %copy.24 = bf16[2,32,16,1,256]{4,1,0,2,3:T(8,128)(2,1)} copy(bf16[2,32,16,1,256]{4,2,3,1,0:T(8,128)(2,1)S(1)} %copy-done) | data formatting | bytes 1048576 | tf_op args[0]
  18.9 0.0 copy-done.2
  18.9 0.6 pad.9.refs_13_
  19.6 0.0 collective-permute-done.5.refs_6_
  19.6 0.0 collective-permute-done.6.refs_7_
  19.6 0.0 copy-start.12
  19.6 0.0 collective-permute-done.refs_1_
  19.6 0.0 collective-permute-done.1.refs_2_
  19.6 0.0 copy-start.7
  19.6 0.0 collective-permute-done.2.refs_3_
  19.7 0.5 copy-done.11
  20.2 0.0 copy-done.12
  20.2 0.0 copy-done.6
  20.2 0.0 copy-done.7
  20.2 0.0 copy-done.8
  20.3 13.7 %shard_map.95 = (bf16[16,2048]{1,0:T(8,128)(2,1)}, bf16[1024,1024]{1,0:T(8,128)(2,1)}, bf16[1024,512]{1,0:T(8,128)(2,1)}) custom-call(bf16[64,64]{1,0:T(8,128)(2,1)} %copy-done.2, bf16[64,64]{1,0:T(8,128)(2,1)} %copy-done.6, bf16[64,64]{1,0:T(8,128)(2,1)} %copy-done.7, bf16[64,64]{1,0:T(8,128)(2,1)} %copy-done.8, bf16[16,128]{1,0:T(8,128)(2,1)} %copy-done.9, ...), custom_call_target="tpu_custom_call" | custom-call | flops 402653184 | bytes 1499136 | tf_op jit(solution)/shard_map/pallas_call | solution.py:207
  33.9 0.0 collective-permute-start.7
  33.9 1.5 %collective-permute-done.7 = bf16[16,2048]{1,0:T(8,128)(2,1)S(1)} collective-permute-done((bf16[16,2048]{1,0:T(8,128)(2,1)}, bf16[16,2048]{1,0:T(8,128)(2,1)S(1)}, u32[]{:S(2)}, u32[]{:S(2)}) %collective-permute-start.7) | collective-permute-done | bytes 65568 | tf_op jit(solution)/shard_map/ppermute | solution.py:191
  35.4 0.9 %add_convert_fusion.refs_4_ = bf16[16,2048]{1,0:T(8,128)(2,1)S(1)} fusion(bf16[16,2048]{1,0:T(8,128)(2,1)S(1)} %collective-permute-done.7, bf16[16,2048]{1,0:T(8,128)(2,1)} %get-tuple-element.7), kind=kLoop, calls=%fused_computation.1 | loop fusion | flops 131072 | bytes 196608 | tf_op jit(solution)/shard_map/convert_element_type | solution.py:201
  36.2 0.0 copy-start.1
  36.2 2.3 %collective-permute-start.10 = (bf16[16,2048]{1,0:T(8,128)(2,1)S(1)}, bf16[16,2048]{1,0:T(8,128)(2,1)S(1)}, u32[]{:S(2)}, u32[]{:S(2)}) collective-permute-start(bf16[16,2048]{1,0:T(8,128)(2,1)S(1)} %add_convert_fusion.refs_4_), channel_id=1, source_target_pairs={{0,24},{4,28},{8,16},{12,20},{16,8},{20,12},{24,0},{28,4},{1,25},{... | collective-permute-start | bytes 196616 | tf_op jit(solution)/shard_map/ppermute | solution.py:191
  38.5 0.5 collective-permute-start.8
  39.1 0.7 collective-permute-start.9
  39.8 2.2 %collective-permute-done.10.refs_7_ = bf16[16,2048]{1,0:T(8,128)(2,1)S(1)} collective-permute-done((bf16[16,2048]{1,0:T(8,128)(2,1)S(1)}, bf16[16,2048]{1,0:T(8,128)(2,1)S(1)}, u32[]{:S(2)}, u32[]{:S(2)}) %collective-permute-start.10) | collective-permute-done | bytes 65568 | tf_op jit(solution)/shard_map/ppermute | solution.py:191
  42.0 0.8 collective-permute-done.8.refs_5_
  42.8 0.5 collective-permute-done.9.refs_6_
  43.3 0.0 copy-done.1
  43.3 0.1 copy-done.4
  43.4 0.6 copy-done.5
  44.0 16.0 %shard_map.96 = (f32[2048,128]{1,0:T(8,128)}, f32[64,64]{1,0:T(8,128)}) custom-call(bf16[64,64]{1,0:T(8,128)(2,1)} %copy-done.2, bf16[64,64]{1,0:T(8,128)(2,1)} %copy-done.6, bf16[64,64]{1,0:T(8,128)(2,1)} %copy-done.7, bf16[64,64]{1,0:T(8,128)(2,1)} %copy-done.8, bf16[16,2048]{1,0:T(8,128)(2,1)} %copy-done.1, bf16[16,2048]{1,0:T(8,128)(2,1)} %copy-done.4, ...), custom_call_target="tpu_custom_call" | custom-call | flops 402653184 | bytes 4169728 | tf_op jit(solution)/shard_map/pallas_call | solution.py:207
  60.0 0.8 %broadcast_in_dim.52 = f32[8,4,16,64]{3,2,1,0:T(8,128)S(1)} broadcast(f32[4,16,64]{2,1,0:T(8,128)} %bitcast.36), dimensions={1,2,3} | broadcast | bytes 147456 | tf_op jit(solution)/shard_map/broadcast_in_dim | solution.py:312
  60.8 0.2 reshape.80
  61.0 13.3 %all_to_all.5 = f32[32,1,1024]{2,1,0:T(1,128)S(1)} all-to-all(f32[32,1,1024]{2,1,0:T(1,128)S(1)} %reshape.80), channel_id=1, replica_groups=mesh['cuts'=8,'frame'=4] {'cuts','frame'}, dimensions={0} | all-to-all | bytes 262144 | tf_op jit(solution)/shard_map/all_to_all | solution.py:315
  74.2 0.5 broadcast.105
  74.7 0.9 %reduce = f32[32,1024]{1,0:T(8,128)S(1)} reduce(f32[32,1,1024]{2,1,0:T(1,128)S(1)} %all_to_all.5, f32[]{:T(128)} %broadcast.105), dimensions={1}, to_apply=%all_to_all.3.reduce_sub_computation | reduce | bytes 262148 | tf_op jit(solution)/shard_map/all_to_all | solution.py:315
  75.7 0.1 reshape.81
  75.8 0.1 reshape.79
  75.9 0.6 copy.29
  (23 shorter events, 0.2 us)
Async XLA Ops:
  0.6 17.4 %copy-start = (bf16[2,32,16,1,256]{4,2,3,1,0:T(8,128)(2,1)S(1)}, bf16[2,32,16,1,256]{4,2,3,1,0:T(8,128)(2,1)}, u32[]{:S(2)}) copy-start(bf16[2,32,16,1,256]{4,2,3,1,0:T(8,128)(2,1)} %param.8) | copy-start | bytes 1572868
  1.6 17.4 %copy-start.2 = (bf16[64,64]{1,0:T(8,128)(2,1)}, bf16[64,64]{1,0:T(8,128)(2,1)S(1)}, u32[]{:S(2)}) copy-start(bf16[64,64]{1,0:T(8,128)(2,1)S(1)} %bitcast_select_fusion.refs_0_) | copy-start | bytes 24580
  1.6 18.0 %collective-permute-start = (bf16[64,64]{1,0:T(8,128)(2,1)S(1)}, bf16[64,64]{1,0:T(8,128)(2,1)S(1)}, u32[]{:S(2)}, u32[]{:S(2)}) collective-permute-start(bf16[64,64]{1,0:T(8,128)(2,1)S(1)} %bitcast_select_fusion.refs_0_), channel_id=1, source_target_pairs={{0,1},{1,0},{2,3},{3,2},{4,5},{5,4},{6,7},{7,6},{8,9},{9,8},{10,11... | collective-permute-start | bytes 24584 | tf_op jit(solution)/shard_map/ppermute | solution.py:191
  4.7 14.9 %collective-permute-start.1 = (bf16[64,64]{1,0:T(8,128)(2,1)S(1)}, bf16[64,64]{1,0:T(8,128)(2,1)S(1)}, u32[]{:S(2)}, u32[]{:S(2)}) collective-permute-start(bf16[64,64]{1,0:T(8,128)(2,1)S(1)} %bitcast_select_fusion.refs_0_), channel_id=1, source_target_pairs={{0,2},{1,3},{2,0},{3,1},{4,6},{5,7},{6,4},{7,5},{8,10},{9,11},{10,... | collective-permute-start | bytes 24584 | tf_op jit(solution)/shard_map/ppermute | solution.py:191
  7.3 12.4 %collective-permute-start.2 = (bf16[64,64]{1,0:T(8,128)(2,1)S(1)}, bf16[64,64]{1,0:T(8,128)(2,1)S(1)}, u32[]{:S(2)}, u32[]{:S(2)}) collective-permute-start(bf16[64,64]{1,0:T(8,128)(2,1)S(1)} %bitcast_select_fusion.refs_0_), channel_id=1, source_target_pairs={{0,3},{1,2},{2,1},{3,0},{4,7},{5,6},{6,5},{7,4},{8,11},{9,10},{10,... | collective-permute-start | bytes 24584 | tf_op jit(solution)/shard_map/ppermute | solution.py:191
  8.5 2.4 %collective-permute-start.3 = (bf16[16,128]{1,0:T(8,128)(2,1)S(1)}, bf16[16,128]{1,0:T(8,128)(2,1)S(1)}, u32[]{:S(2)}, u32[]{:S(2)}) collective-permute-start(bf16[16,128]{1,0:T(8,128)(2,1)S(1)} %select_convert_fusion), channel_id=1, source_target_pairs={{0,4},{4,0},{8,12},{12,8},{16,20},{20,16},{24,28},{28,24},{1,5},{5... | collective-permute-start | bytes 12296 | tf_op jit(solution)/shard_map/ppermute | solution.py:191
  11.0 8.7 %copy-start.9 = (bf16[16,128]{1,0:T(8,128)(2,1)}, bf16[16,128]{1,0:T(8,128)(2,1)S(1)}, u32[]{:S(2)}) copy-start(bf16[16,128]{1,0:T(8,128)(2,1)S(1)} %add_convert_fusion.1.refs_4_) | copy-start | bytes 12292
  11.0 3.7 %collective-permute-start.4 = (bf16[16,128]{1,0:T(8,128)(2,1)S(1)}, bf16[16,128]{1,0:T(8,128)(2,1)S(1)}, u32[]{:S(2)}, u32[]{:S(2)}) collective-permute-start(bf16[16,128]{1,0:T(8,128)(2,1)S(1)} %add_convert_fusion.1.refs_4_), channel_id=1, source_target_pairs={{0,8},{4,12},{8,0},{12,4},{16,24},{20,28},{24,16},{28,20},{1,9},{5... | collective-permute-start | bytes 12296 | tf_op jit(solution)/shard_map/ppermute | solution.py:191
  12.8 6.8 %collective-permute-start.5 = (bf16[16,128]{1,0:T(8,128)(2,1)S(1)}, bf16[16,128]{1,0:T(8,128)(2,1)S(1)}, u32[]{:S(2)}, u32[]{:S(2)}) collective-permute-start(bf16[16,128]{1,0:T(8,128)(2,1)S(1)} %add_convert_fusion.1.refs_4_), channel_id=1, source_target_pairs={{0,16},{4,20},{8,24},{12,28},{16,0},{20,4},{24,8},{28,12},{1,17},{... | collective-permute-start | bytes 12296 | tf_op jit(solution)/shard_map/ppermute | solution.py:191
  14.7 5.0 %copy-start.10 = (bf16[16,128]{1,0:T(8,128)(2,1)}, bf16[16,128]{1,0:T(8,128)(2,1)S(1)}, u32[]{:S(2)}) copy-start(bf16[16,128]{1,0:T(8,128)(2,1)S(1)} %collective-permute-done.4.refs_5_) | copy-start | bytes 12292
  14.7 4.9 %collective-permute-start.6 = (bf16[16,128]{1,0:T(8,128)(2,1)S(1)}, bf16[16,128]{1,0:T(8,128)(2,1)S(1)}, u32[]{:S(2)}, u32[]{:S(2)}) collective-permute-start(bf16[16,128]{1,0:T(8,128)(2,1)S(1)} %add_convert_fusion.1.refs_4_), channel_id=1, source_target_pairs={{0,24},{4,28},{8,16},{12,20},{16,8},{20,12},{24,0},{28,4},{1,25},{... | collective-permute-start | bytes 12296 | tf_op jit(solution)/shard_map/ppermute | solution.py:191
  19.6 0.6 copy-start.11
  19.6 0.6 copy-start.12
  19.6 0.6 copy-start.6
  19.6 0.6 copy-start.7
  19.7 0.6 copy-start.8
  33.9 1.5 %collective-permute-start.7 = (bf16[16,2048]{1,0:T(8,128)(2,1)}, bf16[16,2048]{1,0:T(8,128)(2,1)S(1)}, u32[]{:S(2)}, u32[]{:S(2)}) collective-permute-start(bf16[16,2048]{1,0:T(8,128)(2,1)} %get-tuple-element.7), channel_id=1, source_target_pairs={{0,4},{4,0},{8,12},{12,8},{16,20},{20,16},{24,28},{28,24},{1,5},{5... | collective-permute-start | bytes 196616 | tf_op jit(solution)/shard_map/ppermute | solution.py:191
  36.2 7.1 %copy-start.1 = (bf16[16,2048]{1,0:T(8,128)(2,1)}, bf16[16,2048]{1,0:T(8,128)(2,1)S(1)}, u32[]{:S(2)}) copy-start(bf16[16,2048]{1,0:T(8,128)(2,1)S(1)} %add_convert_fusion.refs_4_) | copy-start | bytes 196612
  36.2 5.8 %collective-permute-start.10 = (bf16[16,2048]{1,0:T(8,128)(2,1)S(1)}, bf16[16,2048]{1,0:T(8,128)(2,1)S(1)}, u32[]{:S(2)}, u32[]{:S(2)}) collective-permute-start(bf16[16,2048]{1,0:T(8,128)(2,1)S(1)} %add_convert_fusion.refs_4_), channel_id=1, source_target_pairs={{0,24},{4,28},{8,16},{12,20},{16,8},{20,12},{24,0},{28,4},{1,25},{... | collective-permute-start | bytes 196616 | tf_op jit(solution)/shard_map/ppermute | solution.py:191
  38.5 4.3 %collective-permute-start.8 = (bf16[16,2048]{1,0:T(8,128)(2,1)S(1)}, bf16[16,2048]{1,0:T(8,128)(2,1)S(1)}, u32[]{:S(2)}, u32[]{:S(2)}) collective-permute-start(bf16[16,2048]{1,0:T(8,128)(2,1)S(1)} %add_convert_fusion.refs_4_), channel_id=1, source_target_pairs={{0,8},{4,12},{8,0},{12,4},{16,24},{20,28},{24,16},{28,20},{1,9},{5... | collective-permute-start | bytes 196616 | tf_op jit(solution)/shard_map/ppermute | solution.py:191
  39.1 4.3 %collective-permute-start.9 = (bf16[16,2048]{1,0:T(8,128)(2,1)S(1)}, bf16[16,2048]{1,0:T(8,128)(2,1)S(1)}, u32[]{:S(2)}, u32[]{:S(2)}) collective-permute-start(bf16[16,2048]{1,0:T(8,128)(2,1)S(1)} %add_convert_fusion.refs_4_), channel_id=1, source_target_pairs={{0,16},{4,20},{8,24},{12,28},{16,0},{20,4},{24,8},{28,12},{1,17},{... | collective-permute-start | bytes 196616 | tf_op jit(solution)/shard_map/ppermute | solution.py:191
  42.0 1.3 %copy-start.3 = (bf16[16,2048]{1,0:T(8,128)(2,1)}, bf16[16,2048]{1,0:T(8,128)(2,1)S(1)}, u32[]{:S(2)}) copy-start(bf16[16,2048]{1,0:T(8,128)(2,1)S(1)} %collective-permute-done.10.refs_7_) | copy-start | bytes 196612
  42.8 0.6 copy-start.4
  43.3 0.6 copy-start.5

commit v2 on v1

--- a/solution.py
+++ b/solution.py
@@ -13,6 +13,7 @@
 BF16 = jnp.bfloat16
 LANES = 128
 TILE = 16
+PITCH = 8
 
 
 def dft_parts(size):
@@ -50,7 +51,21 @@
     return jnp.concatenate([top, bottom], axis=0).astype(BF16)
 
 
-def predict_kernel(n_v, n_line, frames, slab, *refs):
+def adjoint_pair(w):
+    half = w.shape[1] // 2
+    return jnp.concatenate([w, jnp.concatenate([-w[:, half:], w[:, :half]], axis=1)], axis=0)
+
+
+def tree(value):
+    terms = [value[i] for i in range(value.shape[0])]
+    while len(terms) > 1:
+        odd = [terms[-1]] if len(terms) % 2 else []
+        terms = [a + b for a, b in zip(terms[::2], terms[1::2])] + odd
+    return terms[0].astype(F32)
+
+
+def predict_kernel(n_v, n_line, frames, slab, real, *refs):
+    cut = lax.axis_index("cuts")
     v_refs, refs = refs[:n_v], refs[n_v:]
     line_refs, refs = refs[:n_line], refs[n_line:]
     (b_ref, m_ref, taby_ref, tabz_ref, coil_ref, kd_ref, pred_ref, w_ref, fz_ref, i_ref, x_ref) = refs
@@ -61,6 +76,8 @@
     samples = w_ref.shape[0]
     per = samples // frames
     coils = rows // slab
+    halves = width // LANES
+    pitch = 2 * frames + PITCH
 
     pos = total(line_refs)
     groups = pos.shape[0] // 2
@@ -68,18 +85,22 @@
     kz = pos[groups:].T
     at_y = lax.broadcasted_iota(jnp.int32, (LANES, width), 1).astype(F32)
     at_z = lax.broadcasted_iota(jnp.int32, (LANES, depth), 1).astype(F32)
+    slice_of = lax.broadcasted_iota(jnp.int32, (depth, pad), 1) % real + cut * real
+    own = (lax.broadcasted_iota(jnp.int32, (depth, pad), 0) == slice_of).astype(F32).astype(BF16)
+    tabz = jnp.concatenate(
+        [nn(tabz_ref[:, :depth], own), nn(tabz_ref[:, depth:], own)], axis=1
+    ).astype(BF16)
     for g in range(groups):
         hot_y = jnp.where(at_y == ky[:, g : g + 1], 1.0, 0.0).astype(BF16)
         w_ref[g * LANES : (g + 1) * LANES, :] = nn(hot_y, taby_ref[...]).astype(BF16)
         hot_z = jnp.where(at_z == kz[:, g : g + 1], 1.0, 0.0).astype(BF16)
-        fz_ref[g * LANES : (g + 1) * LANES, :] = nn(hot_z, tabz_ref[...]).astype(BF16)
+        fz_ref[g * LANES : (g + 1) * LANES, :] = nn(hot_z, tabz).astype(BF16)
 
     v = factor_matrix(v_refs)
-    halves = width // LANES
     for z in range(slab):
         image = nn(v, b_ref[z])
         for h in range(halves):
-            i_ref[h, z * 2 * frames : (z + 1) * 2 * frames, :] = image[
+            i_ref[h, z * pitch : z * pitch + 2 * frames, :] = image[
                 :, h * LANES : (h + 1) * LANES
             ]
 
@@ -89,7 +110,7 @@
     def frame(t, carry):
         i_re, i_im = (
             jnp.concatenate(
-                [i_ref[h, pl.ds(at, slab, stride=2 * frames), :] for h in range(halves)], axis=1
+                [i_ref[h, pl.ds(at, slab, stride=pitch), :] for h in range(halves)], axis=1
             ).astype(BF16)[None]
             for at in (t, frames + t)
         )
@@ -97,7 +118,7 @@
         p_im = (m_re * i_im + m_im * i_re).reshape(rows, width)
         at = pl.ds(pl.multiple_of(t * per, TILE), per)
         w = w_ref[at, :]
-        lhs = jnp.concatenate([w[:, : 2 * width], w[:, 2 * width :]], axis=0)
+        lhs = adjoint_pair(w)
         y = nt(lhs[:, :width], p_re) + nt(lhs[:, width:], p_im)
         y_re, y_im = y[:per], y[per:]
         f = fz_ref[at, :].astype(F32)
@@ -108,7 +129,7 @@
         x_ref[pl.ds(base, 2 * per), :rows] = jnp.concatenate([x_re, x_im], axis=0).astype(BF16)
         return carry
 
-    lax.fori_loop(0, frames, frame, 0, unroll=2)
+    lax.fori_loop(0, frames, frame, 0, unroll=math.gcd(frames, 16))
     chunk = min(512, 2 * samples)
     for s in range(0, 2 * samples, chunk):
         part = nt(coil_ref[:, :rows], x_ref[s : s + chunk, :rows])
@@ -118,7 +139,7 @@
 def gradient_kernel(n_v, n_r, frames, slab, scale, *refs):
     v_refs, refs = refs[:n_v], refs[n_v:]
     r_refs, refs = refs[:n_r], refs[n_r:]
-    (b_ref, m_ref, coil_ref, w_ref, fz_ref, grad_ref, fg_ref, g_ref, r_ref, mf_ref) = refs
+    (b_ref, m_ref, coil_ref, w_ref, fz_ref, grad_ref, fg_ref, g_ref, r_ref) = refs
     width = b_ref.shape[2]
     rows = m_ref.shape[1]
     pad = coil_ref.shape[1]
@@ -130,38 +151,38 @@
     chunk = min(512, 2 * samples)
     for s in range(0, 2 * samples, chunk):
         r_ref[s : s + chunk, :] = tn(resid[:, s : s + chunk], coil_ref[...])
-    mf_ref[...] = m_ref[...].astype(F32)
     halves = width // LANES
+    pitch = 2 * frames + PITCH
 
     def frame(t, carry):
         at = pl.ds(pl.multiple_of(t * per, TILE), per)
         w = w_ref[at, :]
-        rhs = jnp.concatenate([w[:, : 2 * width], w[:, 2 * width :]], axis=0)
+        rhs = adjoint_pair(w)
         f = fz_ref[at, :].astype(F32)
         f_cos, f_sin = f[:, :pad], f[:, pad:]
         base = pl.multiple_of(t * 2 * per, TILE)
         r = r_ref[pl.ds(base, 2 * per), :]
         r_re, r_im = r[:per], r[per:]
         q = jnp.concatenate([r_re * f_cos - r_im * f_sin, r_im * f_cos + r_re * f_sin], axis=0)
-        u = tn(q[:, :rows].astype(BF16), rhs)
+        u = tn(q[:, :rows].astype(BF16), rhs).astype(BF16)
         u_re = u[:, :width].reshape(coils, slab, width)
         u_im = u[:, width:].reshape(coils, slab, width)
-        m_re = mf_ref[0].reshape(coils, slab, width)
-        m_im = mf_ref[1].reshape(coils, slab, width)
-        g_re = jnp.sum(m_re * u_re + m_im * u_im, axis=0)
-        g_im = jnp.sum(m_re * u_im - m_im * u_re, axis=0)
+        m_re = m_ref[0].reshape(coils, slab, width)
+        m_im = m_ref[1].reshape(coils, slab, width)
+        g_re = tree(m_re * u_re + m_im * u_im)
+        g_im = tree(m_re * u_im - m_im * u_re)
         for h in range(halves):
             lanes = slice(h * LANES, (h + 1) * LANES)
-            g_ref[h, pl.ds(t, slab, stride=2 * frames), :] = g_re[:, lanes]
-            g_ref[h, pl.ds(frames + t, slab, stride=2 * frames), :] = g_im[:, lanes]
+            g_ref[h, pl.ds(t, slab, stride=pitch), :] = g_re[:, lanes]
+            g_ref[h, pl.ds(frames + t, slab, stride=pitch), :] = g_im[:, lanes]
         return carry
 
-    lax.fori_loop(0, frames, frame, 0, unroll=2)
+    lax.fori_loop(0, frames, frame, 0, unroll=math.gcd(frames, 16))
     v = factor_matrix(v_refs)
     rank = v.shape[1] // 2
     acc = jnp.zeros((2 * frames, 2 * rank), F32)
     for z in range(slab):
-        at = pl.ds(z * 2 * frames, 2 * frames)
+        at = pl.ds(z * pitch, 2 * frames)
         g = jnp.concatenate([g_ref[h, at, :] for h in range(halves)], axis=1).astype(BF16)
         acc = acc + nt(g, b_ref[z])
         grad = tn(v, g)
@@ -172,7 +193,14 @@
     top, bottom = acc[:frames], acc[frames:]
     g_re = top[:, :rank] + bottom[:, rank:]
     g_im = bottom[:, :rank] - top[:, rank:]
-    fg_ref[...] = jnp.concatenate([g_re, g_im], axis=1) * scale
+    fg = jnp.concatenate([g_re, g_im], axis=1) * scale
+    n_frame, n_rows, n_lanes = fg_ref.shape[1:]
+    own, fold = frames // n_frame, n_lanes // (2 * rank)
+    for f in range(n_frame):
+        piece = [fg[f * own + k * n_rows : f * own + (k + 1) * n_rows] for k in range(fold)]
+        fg_ref[:, f] = jnp.broadcast_to(
+            jnp.concatenate(piece, axis=1)[None], (fg_ref.shape[0], n_rows, n_lanes)
+        )
 
 
 def stages(size):
@@ -203,12 +231,18 @@
 
 
 def call(kernel, outs, scratch, flops, *operands):
-    nbytes = sum(math.prod(x.shape) * x.dtype.itemsize for x in operands)
+    def size(x):
+        rows = [-(-x.shape[-2] // TILE) * TILE, -(-x.shape[-1] // LANES) * LANES]
+        return math.prod(x.shape[:-2]) * math.prod(rows) * jnp.dtype(x.dtype).itemsize
+
+    nbytes = sum(size(x) for x in operands)
+    held = nbytes + sum(size(x) for x in (*outs, *scratch))
+    limit = min(56, 10 + held * 5 // (4 * 1024 * 1024)) * 1024 * 1024
     return pl.pallas_call(
         kernel,
         out_shape=outs,
         scratch_shapes=scratch,
-        compiler_params=pltpu.CompilerParams(vmem_limit_bytes=56 * 1024 * 1024),
+        compiler_params=pltpu.CompilerParams(vmem_limit_bytes=limit),
         cost_estimate=pl.CostEstimate(flops=flops, bytes_accessed=nbytes, transcendentals=0),
     )(*operands)
 
@@ -243,12 +277,8 @@
         jnp.where(row_owner, jnp.tile(turned, (n_frame, 1)), jnp.zeros((), BF16)), "frame"
     )
 
-    tab_cos, tab_sin = dft_parts(width)
-    taby = jnp.asarray(np.concatenate([tab_cos, tab_sin, -tab_sin, tab_cos], axis=1))
-    z_cos, z_sin = dft_parts(depth)
-    tabz = lax.dynamic_slice_in_dim(jnp.asarray(np.stack([z_cos, z_sin])), cut * slab, slab, axis=2)
-    tabz = jnp.pad(jnp.tile(tabz, (1, 1, rows // slab)), ((0, 0), (0, 0), (0, pad - rows)))
-    tabz = jnp.concatenate([tabz[0], tabz[1]], axis=1)
+    taby = jnp.asarray(np.concatenate(dft_parts(width), axis=1))
+    tabz = jnp.asarray(np.concatenate(dft_parts(depth), axis=1))
     row_coil = np.arange(pad) // slab
     coil_of = jnp.asarray(
         ((row_coil[None] == np.arange(coil_rows)[:, None]) & (row_coil[None] < coils)).astype(BF16)
@@ -261,15 +291,16 @@
     kd = jnp.where(column_owner, kd, jnp.zeros((), BF16)).reshape(coils, 2 * samples)
     kd = jnp.pad(kd, ((0, coil_rows - coils), (0, 0)))
 
+    fold = max(1, LANES // (2 * rank))
     flops = 2 * frames * 2 * per * rows * 2 * width
     predicted, w, fz = call(
-        functools.partial(predict_kernel, len(v_terms), len(line_terms), frames, tall),
+        functools.partial(predict_kernel, len(v_terms), len(line_terms), frames, tall, slab),
         (
             jax.ShapeDtypeStruct((coil_rows, 2 * samples), BF16),
-            jax.ShapeDtypeStruct((samples, 4 * width), BF16),
+            jax.ShapeDtypeStruct((samples, 2 * width), BF16),
             jax.ShapeDtypeStruct((samples, 2 * pad), BF16),
         ),
-        [pltpu.VMEM((width // LANES, tall * 2 * frames, LANES), F32), pltpu.VMEM((2 * samples, pad), BF16)],
+        [pltpu.VMEM((width // LANES, tall * (2 * frames + PITCH), LANES), F32), pltpu.VMEM((2 * samples, pad), BF16)],
         flops,
         *v_terms, *line_terms, b_rows, m_rows, taby, tabz, coil_of, kd,
     )
@@ -280,12 +311,11 @@
         ),
         (
             jax.ShapeDtypeStruct((2 * rank * tall * width // LANES, LANES), F32),
-            jax.ShapeDtypeStruct((frames, 2 * rank), F32),
+            jax.ShapeDtypeStruct((n_cuts, n_frame, frames // n_frame // fold, 2 * rank * fold), F32),
         ),
         [
-            pltpu.VMEM((width // LANES, tall * 2 * frames, LANES), F32),
+            pltpu.VMEM((width // LANES, tall * (2 * frames + PITCH), LANES), F32),
             pltpu.VMEM((2 * samples, pad), F32),
-            pltpu.VMEM((2, rows, width), F32),
         ],
         flops,
         *v_terms, *resid_terms, b_rows, m_rows, coil_of, w, fz,
@@ -309,11 +339,10 @@
         grads.append(grad)
         fg = fg + term
     basis_grad = grads[0][:, :, :, None] if readout == 1 else jnp.stack(grads, axis=3)
-    pieces = jnp.broadcast_to(
-        fg.reshape(1, n_frame, own, 2 * rank), (n_cuts, n_frame, own, 2 * rank)
-    ).reshape(n_cuts * n_frame, own, 2 * rank)
-    gathered = lax.all_to_all(pieces, ("cuts", "frame"), 0, 0, tiled=True)
-    factor_grad = jnp.sum(gathered, axis=0).reshape(own, 2, rank).transpose(1, 2, 0)
+    pieces = fg.reshape((n_cuts * n_frame,) + fg.shape[2:])
+    gathered = jnp.sum(lax.all_to_all(pieces, ("cuts", "frame"), 0, 0, tiled=True), axis=0)
+    folded = gathered.reshape(gathered.shape[0], -1, 2, rank)
+    factor_grad = folded.transpose(2, 3, 1, 0).reshape(2, rank, own)
     return basis_grad, factor_grad
 
 

time: 76.9 us -> 52.1 us (0.68)
  Pallas kernels: 29.7 us -> 12.8 us
  local copies, waits for them, and re-layouts: 8.77 us -> 3.58 us
  other arithmetic: 3.33 us -> 0.19 us
  waiting for transfers between devices: 5.29 us -> 7.22 us
  starting transfers between devices: 15.3 us -> 13.4 us
    pallas_call x2, Pallas kernels: 29.7 us -> 12.8 us  [call(): pl.pallas_call(kernel, out_shape=outs, scratch_shapes=scratch, compiler_p...]
    ppermute x11, starting transfers between devices: 15.3 us -> 13.4 us  [swap(): return lax.ppermute(value, axis, [(i, i ^ distance) for i in range(size)])]
    ppermute x11, waiting for transfers between devices: 5.29 us -> 7.22 us  [swap(): return lax.ppermute(value, axis, [(i, i ^ distance) for i in range(size)])]
    unnamed x30 -> x17, local copies, waits for them, and re-layouts: 3.08 us -> 1.52 us
    all_to_all x1 -> x0, other arithmetic: 0.95 us -> none  [body(): gathered = lax.all_to_all(pieces, ('cuts', 'frame'), 0, 0, tiled=True)]
    convert_element_type x2, other arithmetic: 0.87 us -> 0.02 us  [shares(): value = functools.reduce(lambda a, b: a + b, [term.astype(F32) for term i...]
    broadcast_in_dim x1 -> x0, local copies, waits for them, and re-layouts: 0.78 us -> none  [body(): jnp.broadcast_to(fg.reshape(1, n_frame, own, 2 * rank), (n_cuts, n_frame,...]
  transfers between devices with their start and end apart: 11 -> 11, of which waited for: 5 -> 7; matrix products, arithmetic and copies ran while one was open for 8% -> 2% of each run, Pallas kernels for 0% -> 0%
where the time goes in v2:
time: 52.1 us; the launch traced here: 51.8 us
  blocking collectives  13.8 us (26%)
  starting transfers between devices  13.4 us (26%)
  Pallas kernels  12.8 us (25%)
  waiting for transfers between devices  7.22 us (14%)
  local copies, waits for them, and re-layouts  3.58 us (7%)
  between operations  0.84 us (2%)
    all_to_all x1, blocking collectives, body(): lax.all_to_all(pieces, ('cuts', 'frame'), 0, 0, tiled=True)  13.8 us
    ppermute x11, starting transfers between devices, swap(): return lax.ppermute(value, axis, [(i, i ^ distance) for i in range(size)])  13.4 us
    pallas_call x2, Pallas kernels, call(): pl.pallas_call(kernel, out_shape=outs, scratch_shapes=scratch, compiler_p...  12.8 us
    ppermute x11, waiting for transfers between devices, swap(): return lax.ppermute(value, axis, [(i, i ^ distance) for i in range(size)])  7.22 us
    unnamed x17, local copies, waits for them, and re-layouts  1.52 us
  transfers between devices with their start and end apart: 11, of which 7 were waited for; matrix products, arithmetic and copies ran while one was open for 2% of the time, Pallas kernels for 0%

profile of v2, /device:TPU:0, one launch (start us, length us, event | category | flops | bytes accessed | tf_op | source)
XLA Modules:
  0.0 51.8 jit_solution(6797519372333990462)
XLA Ops:
  0.7 0.0 copy-start.7
  0.7 0.1 broadcast_in_dim.38
  0.8 0.6 %copy-done.7 = s32[64,2]{0,1:T(2,128)S(1)} copy-done((s32[64,2]{0,1:T(2,128)S(1)}, s32[64,2]{0,1:T(2,128)}, u32[]{:S(2)}) %copy-start.7) | copy-done | bytes 536
  1.4 0.1 copy.21
  1.5 0.3 tile.32
  1.8 0.0 copy-start.6
  1.8 0.5 collective-permute-start.3
  2.3 0.2 copy-done.6
  2.5 0.1 tile.28
  2.6 0.1 bitcast_select_fusion.refs_0_
  2.7 5.1 %collective-permute-start.2 = (bf16[64,64]{1,0:T(8,128)(2,1)S(1)}, bf16[64,64]{1,0:T(8,128)(2,1)S(1)}, u32[]{:S(2)}, u32[]{:S(2)}) collective-permute-start(bf16[64,64]{1,0:T(8,128)(2,1)S(1)} %bitcast_select_fusion.refs_0_), channel_id=1, source_target_pairs={{0,3},{1,2},{2,1},{3,0},{4,7},{5,6},{6,5},{7,4},{8,11},{9,10},{10,... | collective-permute-start | bytes 24584 | tf_op jit(solution)/shard_map/ppermute | solution.py:219
  7.7 0.0 collective-permute-start.1
  7.8 0.6 %collective-permute-start = (bf16[64,64]{1,0:T(8,128)(2,1)S(1)}, bf16[64,64]{1,0:T(8,128)(2,1)S(1)}, u32[]{:S(2)}, u32[]{:S(2)}) collective-permute-start(bf16[64,64]{1,0:T(8,128)(2,1)S(1)} %bitcast_select_fusion.refs_0_), channel_id=1, source_target_pairs={{0,1},{1,0},{2,3},{3,2},{4,5},{5,4},{6,7},{7,6},{8,9},{9,8},{10,11... | collective-permute-start | bytes 24584 | tf_op jit(solution)/shard_map/ppermute | solution.py:219
  8.4 0.0 copy-start.5
  8.4 0.1 broadcast_in_dim.41
  8.5 0.6 %copy-done.5 = bf16[2,64,2,12,1]{1,2,4,3,0:T(2,128)(2,1)S(1)} copy-done((bf16[2,64,2,12,1]{1,2,4,3,0:T(2,128)(2,1)S(1)}, bf16[2,64,2,12,1]{1,2,4,3,0:T(2,128)(2,1)}, u32[]{:S(2)}) %copy-start.5) | copy-done | bytes 6168
  9.1 0.1 copy.23
  9.3 0.0 copy-start.4
  9.3 0.3 tile.33
  9.5 0.2 copy.24
  9.8 0.0 collective-permute-done.3
  9.8 2.7 %collective-permute-start.6 = (bf16[16,128]{1,0:T(8,128)(2,1)S(1)}, bf16[16,128]{1,0:T(8,128)(2,1)S(1)}, u32[]{:S(2)}, u32[]{:S(2)}) collective-permute-start(bf16[16,128]{1,0:T(8,128)(2,1)S(1)} %add_convert_fusion.1.refs_4_), channel_id=1, source_target_pairs={{0,24},{4,28},{8,16},{12,20},{16,8},{20,12},{24,0},{28,4},{1,25},{... | collective-permute-start | bytes 12296 | tf_op jit(solution)/shard_map/ppermute | solution.py:219
  12.4 0.5 collective-permute-start.5
  12.9 0.0 collective-permute-done.2.refs_3_
  13.0 0.4 collective-permute-start.4
  13.4 0.0 copy-done.4
  13.4 0.0 copy-start
  13.4 0.0 copy-start.2
  13.4 0.2 copy.22
  13.6 0.0 copy-start.1
  13.6 0.0 copy-start.3
  13.6 0.0 collective-permute-done.1.refs_2_
  13.6 0.0 collective-permute-done.refs_1_
  13.6 0.7 %collective-permute-done.6.refs_7_ = bf16[16,128]{1,0:T(8,128)(2,1)S(1)} collective-permute-done((bf16[16,128]{1,0:T(8,128)(2,1)S(1)}, bf16[16,128]{1,0:T(8,128)(2,1)S(1)}, u32[]{:S(2)}, u32[]{:S(2)}) %collective-permute-start.6) | collective-permute-done | bytes 4128 | tf_op jit(solution)/shard_map/ppermute | solution.py:219
  14.4 1.7 %collective-permute-done.5.refs_6_ = bf16[16,128]{1,0:T(8,128)(2,1)S(1)} collective-permute-done((bf16[16,128]{1,0:T(8,128)(2,1)S(1)}, bf16[16,128]{1,0:T(8,128)(2,1)S(1)}, u32[]{:S(2)}, u32[]{:S(2)}) %collective-permute-start.5) | collective-permute-done | bytes 4128 | tf_op jit(solution)/shard_map/ppermute | solution.py:219
  16.0 0.5 collective-permute-done.4.refs_5_
  16.6 0.0 copy-done
  16.6 0.0 copy-done.2
  16.6 0.0 copy-done.1
  16.6 0.0 copy-done.3
  16.6 6.0 %shard_map.95 = (bf16[16,2048]{1,0:T(8,128)(2,1)S(1)}, bf16[1024,512]{1,0:T(8,128)(2,1)S(1)}, bf16[1024,512]{1,0:T(8,128)(2,1)S(1)}) custom-call(bf16[64,64]{1,0:T(8,128)(2,1)S(1)} %bitcast_select_fusion.refs_0_, bf16[64,64]{1,0:T(8,128)(2,1)S(1)} %collective-permute-done.refs_1_, bf16[64,64]{1,0:T(8,128)(2,1)S(1)} %collective-permute-done.1.refs_2_, ...), custom_call_target="tpu_custom_call" | custom-call | flops 402653184 | bytes 1204224 | tf_op jit(solution)/shard_map/pallas_call | solution.py:241
  22.6 0.0 collective-permute-start.7
  22.7 1.2 %collective-permute-done.7 = bf16[16,2048]{1,0:T(8,128)(2,1)S(1)} collective-permute-done((bf16[16,2048]{1,0:T(8,128)(2,1)S(1)}, bf16[16,2048]{1,0:T(8,128)(2,1)S(1)}, u32[]{:S(2)}, u32[]{:S(2)}) %collective-permute-start.7) | collective-permute-done | bytes 65568 | tf_op jit(solution)/shard_map/ppermute | solution.py:219
  23.9 1.5 %collective-permute-start.10 = (bf16[16,2048]{1,0:T(8,128)(2,1)S(1)}, bf16[16,2048]{1,0:T(8,128)(2,1)S(1)}, u32[]{:S(2)}, u32[]{:S(2)}) collective-permute-start(bf16[16,2048]{1,0:T(8,128)(2,1)S(1)} %add_convert_fusion.refs_4_), channel_id=1, source_target_pairs={{0,24},{4,28},{8,16},{12,20},{16,8},{20,12},{24,0},{28,4},{1,25},{... | collective-permute-start | bytes 196616 | tf_op jit(solution)/shard_map/ppermute | solution.py:219
  25.5 0.4 collective-permute-start.9
  25.9 1.6 %collective-permute-start.8 = (bf16[16,2048]{1,0:T(8,128)(2,1)S(1)}, bf16[16,2048]{1,0:T(8,128)(2,1)S(1)}, u32[]{:S(2)}, u32[]{:S(2)}) collective-permute-start(bf16[16,2048]{1,0:T(8,128)(2,1)S(1)} %add_convert_fusion.refs_4_), channel_id=1, source_target_pairs={{0,8},{4,12},{8,0},{12,4},{16,24},{20,28},{24,16},{28,20},{1,9},{5... | collective-permute-start | bytes 196616 | tf_op jit(solution)/shard_map/ppermute | solution.py:219
  27.5 1.8 %collective-permute-done.10.refs_7_ = bf16[16,2048]{1,0:T(8,128)(2,1)S(1)} collective-permute-done((bf16[16,2048]{1,0:T(8,128)(2,1)S(1)}, bf16[16,2048]{1,0:T(8,128)(2,1)S(1)}, u32[]{:S(2)}, u32[]{:S(2)}) %collective-permute-start.10) | collective-permute-done | bytes 65568 | tf_op jit(solution)/shard_map/ppermute | solution.py:219
  29.2 1.2 %collective-permute-done.9.refs_6_ = bf16[16,2048]{1,0:T(8,128)(2,1)S(1)} collective-permute-done((bf16[16,2048]{1,0:T(8,128)(2,1)S(1)}, bf16[16,2048]{1,0:T(8,128)(2,1)S(1)}, u32[]{:S(2)}, u32[]{:S(2)}) %collective-permute-start.9) | collective-permute-done | bytes 65568 | tf_op jit(solution)/shard_map/ppermute | solution.py:219
  30.5 0.1 collective-permute-done.8.refs_5_
  30.5 6.8 %shard_map.96 = (f32[2048,128]{1,0:T(8,128)}, f32[8,4,8,128]{3,2,1,0:T(8,128)S(1)}) custom-call(bf16[64,64]{1,0:T(8,128)(2,1)S(1)} %bitcast_select_fusion.refs_0_, bf16[64,64]{1,0:T(8,128)(2,1)S(1)} %collective-permute-done.refs_1_, bf16[64,64]{1,0:T(8,128)(2,1)S(1)} %collective-permute-done.1.refs_2_, bf16[64,64]{1,0:T(8,128)(2,1)S(1)} %collective-permute-done.2.refs_3_, ...), custom_call_target="tpu_custom_call" | custom-call | flops 402653184 | bytes 3153920 | tf_op jit(solution)/shard_map/pallas_call | solution.py:241
  37.3 13.8 %all_to_all.5 = f32[32,8,128]{2,1,0:T(8,128)S(1)} all-to-all(f32[32,8,128]{2,1,0:T(8,128)S(1)} %bitcast.29), channel_id=1, replica_groups=mesh['cuts'=8,'frame'=4] {'cuts','frame'}, dimensions={0} | all-to-all | bytes 262144 | tf_op jit(solution)/shard_map/all_to_all | solution.py:343
  51.1 0.1 reshape.76
  51.2 0.6 %copy.28 = f32[2,32,2,8]{1,3,2,0:T(8,128)} copy(f32[2,32,2,8]{1,0,2,3:T(2,128)S(1)} %bitcast.31) | data formatting | bytes 8192 | tf_op jit(solution)/shard_map/transpose | solution.py:345
  (14 shorter events, 0.2 us)
Async XLA Ops:
  0.7 0.7 %copy-start.7 = (s32[64,2]{0,1:T(2,128)S(1)}, s32[64,2]{0,1:T(2,128)}, u32[]{:S(2)}) copy-start(s32[64,2]{0,1:T(2,128)} %param.11) | copy-start | bytes 1540
  1.8 0.7 %copy-start.6 = (bf16[2,32,16]{1,2,0:T(8,128)(2,1)S(1)}, bf16[2,32,16]{1,2,0:T(8,128)(2,1)}, u32[]{:S(2)}) copy-start(bf16[2,32,16]{1,2,0:T(8,128)(2,1)} %param.10) | copy-start | bytes 6148
  1.8 8.0 %collective-permute-start.3 = (bf16[16,128]{1,0:T(8,128)(2,1)S(1)}, bf16[16,128]{1,0:T(8,128)(2,1)S(1)}, u32[]{:S(2)}, u32[]{:S(2)}) collective-permute-start(bf16[16,128]{1,0:T(8,128)(2,1)S(1)} %select_convert_fusion), channel_id=1, source_target_pairs={{0,4},{4,0},{8,12},{12,8},{16,20},{20,16},{24,28},{28,24},{1,5},{5... | collective-permute-start | bytes 12296 | tf_op jit(solution)/shard_map/ppermute | solution.py:219
  2.7 10.3 %collective-permute-start.2 = (bf16[64,64]{1,0:T(8,128)(2,1)S(1)}, bf16[64,64]{1,0:T(8,128)(2,1)S(1)}, u32[]{:S(2)}, u32[]{:S(2)}) collective-permute-start(bf16[64,64]{1,0:T(8,128)(2,1)S(1)} %bitcast_select_fusion.refs_0_), channel_id=1, source_target_pairs={{0,3},{1,2},{2,1},{3,0},{4,7},{5,6},{6,5},{7,4},{8,11},{9,10},{10,... | collective-permute-start | bytes 24584 | tf_op jit(solution)/shard_map/ppermute | solution.py:219
  7.7 5.9 %collective-permute-start.1 = (bf16[64,64]{1,0:T(8,128)(2,1)S(1)}, bf16[64,64]{1,0:T(8,128)(2,1)S(1)}, u32[]{:S(2)}, u32[]{:S(2)}) collective-permute-start(bf16[64,64]{1,0:T(8,128)(2,1)S(1)} %bitcast_select_fusion.refs_0_), channel_id=1, source_target_pairs={{0,2},{1,3},{2,0},{3,1},{4,6},{5,7},{6,4},{7,5},{8,10},{9,11},{10,... | collective-permute-start | bytes 24584 | tf_op jit(solution)/shard_map/ppermute | solution.py:219
  7.8 5.9 %collective-permute-start = (bf16[64,64]{1,0:T(8,128)(2,1)S(1)}, bf16[64,64]{1,0:T(8,128)(2,1)S(1)}, u32[]{:S(2)}, u32[]{:S(2)}) collective-permute-start(bf16[64,64]{1,0:T(8,128)(2,1)S(1)} %bitcast_select_fusion.refs_0_), channel_id=1, source_target_pairs={{0,1},{1,0},{2,3},{3,2},{4,5},{5,4},{6,7},{7,6},{8,9},{9,8},{10,11... | collective-permute-start | bytes 24584 | tf_op jit(solution)/shard_map/ppermute | solution.py:219
  8.4 0.7 %copy-start.5 = (bf16[2,64,2,12,1]{1,2,4,3,0:T(2,128)(2,1)S(1)}, bf16[2,64,2,12,1]{1,2,4,3,0:T(2,128)(2,1)}, u32[]{:S(2)}) copy-start(bf16[2,64,2,12,1]{1,2,4,3,0:T(2,128)(2,1)} %param.12) | copy-start | bytes 18436
  9.3 4.1 %copy-start.4 = (bf16[2,32,16,1,256]{4,2,3,1,0:T(8,128)(2,1)S(1)}, bf16[2,32,16,1,256]{4,2,3,1,0:T(8,128)(2,1)}, u32[]{:S(2)}) copy-start(bf16[2,32,16,1,256]{4,2,3,1,0:T(8,128)(2,1)} %param.8) | copy-start | bytes 1572868
  9.8 4.6 %collective-permute-start.6 = (bf16[16,128]{1,0:T(8,128)(2,1)S(1)}, bf16[16,128]{1,0:T(8,128)(2,1)S(1)}, u32[]{:S(2)}, u32[]{:S(2)}) collective-permute-start(bf16[16,128]{1,0:T(8,128)(2,1)S(1)} %add_convert_fusion.1.refs_4_), channel_id=1, source_target_pairs={{0,24},{4,28},{8,16},{12,20},{16,8},{20,12},{24,0},{28,4},{1,25},{... | collective-permute-start | bytes 12296 | tf_op jit(solution)/shard_map/ppermute | solution.py:219
  12.4 3.6 %collective-permute-start.5 = (bf16[16,128]{1,0:T(8,128)(2,1)S(1)}, bf16[16,128]{1,0:T(8,128)(2,1)S(1)}, u32[]{:S(2)}, u32[]{:S(2)}) collective-permute-start(bf16[16,128]{1,0:T(8,128)(2,1)S(1)} %add_convert_fusion.1.refs_4_), channel_id=1, source_target_pairs={{0,16},{4,20},{8,24},{12,28},{16,0},{20,4},{24,8},{28,12},{1,17},{... | collective-permute-start | bytes 12296 | tf_op jit(solution)/shard_map/ppermute | solution.py:219
  13.0 3.6 %collective-permute-start.4 = (bf16[16,128]{1,0:T(8,128)(2,1)S(1)}, bf16[16,128]{1,0:T(8,128)(2,1)S(1)}, u32[]{:S(2)}, u32[]{:S(2)}) collective-permute-start(bf16[16,128]{1,0:T(8,128)(2,1)S(1)} %add_convert_fusion.1.refs_4_), channel_id=1, source_target_pairs={{0,8},{4,12},{8,0},{12,4},{16,24},{20,28},{24,16},{28,20},{1,9},{5... | collective-permute-start | bytes 12296 | tf_op jit(solution)/shard_map/ppermute | solution.py:219
  13.4 3.2 %copy-start = (bf16[2,12,16,1,256]{4,2,3,1,0:T(8,128)(2,1)S(1)}, bf16[2,12,16,1,256]{4,2,3,1,0:T(8,128)(2,1)}, u32[]{:S(2)}) copy-start(bf16[2,12,16,1,256]{4,2,3,1,0:T(8,128)(2,1)} %param.9) | copy-start | bytes 589828
  13.4 3.2 %copy-start.2 = (bf16[256,512]{1,0:T(8,128)(2,1)S(1)}, bf16[256,512]{1,0:T(8,128)(2,1)}, u32[]{:S(2)}) copy-start(bf16[256,512]{1,0:T(8,128)(2,1)} %constant.79.clone.refs_10_) | copy-start | bytes 786436
  13.6 3.0 %copy-start.1 = (bf16[16,256]{1,0:T(8,128)(2,1)S(1)}, bf16[16,256]{1,0:T(8,128)(2,1)}, u32[]{:S(2)}) copy-start(bf16[16,256]{1,0:T(8,128)(2,1)} %constant.81.clone.refs_12_.refs_10_) | copy-start | bytes 24580
  13.6 3.0 %copy-start.3 = (bf16[128,256]{1,0:T(8,128)(2,1)S(1)}, bf16[128,256]{1,0:T(8,128)(2,1)}, u32[]{:S(2)}) copy-start(bf16[128,256]{1,0:T(8,128)(2,1)} %constant.80.clone.refs_11_) | copy-start | bytes 196612
  22.6 1.3 %collective-permute-start.7 = (bf16[16,2048]{1,0:T(8,128)(2,1)S(1)}, bf16[16,2048]{1,0:T(8,128)(2,1)S(1)}, u32[]{:S(2)}, u32[]{:S(2)}) collective-permute-start(bf16[16,2048]{1,0:T(8,128)(2,1)S(1)} %get-tuple-element.7), channel_id=1, source_target_pairs={{0,4},{4,0},{8,12},{12,8},{16,20},{20,16},{24,28},{28,24},{1,5},{5... | collective-permute-start | bytes 196616 | tf_op jit(solution)/shard_map/ppermute | solution.py:219
  23.9 5.3 %collective-permute-start.10 = (bf16[16,2048]{1,0:T(8,128)(2,1)S(1)}, bf16[16,2048]{1,0:T(8,128)(2,1)S(1)}, u32[]{:S(2)}, u32[]{:S(2)}) collective-permute-start(bf16[16,2048]{1,0:T(8,128)(2,1)S(1)} %add_convert_fusion.refs_4_), channel_id=1, source_target_pairs={{0,24},{4,28},{8,16},{12,20},{16,8},{20,12},{24,0},{28,4},{1,25},{... | collective-permute-start | bytes 196616 | tf_op jit(solution)/shard_map/ppermute | solution.py:219
  25.5 5.0 %collective-permute-start.9 = (bf16[16,2048]{1,0:T(8,128)(2,1)S(1)}, bf16[16,2048]{1,0:T(8,128)(2,1)S(1)}, u32[]{:S(2)}, u32[]{:S(2)}) collective-permute-start(bf16[16,2048]{1,0:T(8,128)(2,1)S(1)} %add_convert_fusion.refs_4_), channel_id=1, source_target_pairs={{0,16},{4,20},{8,24},{12,28},{16,0},{20,4},{24,8},{28,12},{1,17},{... | collective-permute-start | bytes 196616 | tf_op jit(solution)/shard_map/ppermute | solution.py:219
  25.9 4.7 %collective-permute-start.8 = (bf16[16,2048]{1,0:T(8,128)(2,1)S(1)}, bf16[16,2048]{1,0:T(8,128)(2,1)S(1)}, u32[]{:S(2)}, u32[]{:S(2)}) collective-permute-start(bf16[16,2048]{1,0:T(8,128)(2,1)S(1)} %add_convert_fusion.refs_4_), channel_id=1, source_target_pairs={{0,8},{4,12},{8,0},{12,4},{16,24},{20,28},{24,16},{28,20},{1,9},{5... | collective-permute-start | bytes 196616 | tf_op jit(solution)/shard_map/ppermute | solution.py:219

commit v3 on v2

v3 whole, which is shorter than its diff:
```python
import functools
import math

import jax
import jax.numpy as jnp
import numpy as np
from jax import lax
from jax.experimental import pallas as pl
from jax.experimental.pallas import tpu as pltpu
from jax.sharding import PartitionSpec as P

F32 = jnp.float32
BF16 = jnp.bfloat16
LANES = 128
TILE = 16
PITCH = 8


def dft_parts(size):
    index = np.arange(size, dtype=np.int64)
    angle = ((index[:, None] * index[None, :]) % size).astype(np.float64) * (2.0 * math.pi / size)
    factor = 1.0 / math.sqrt(size)
    return (np.cos(angle) * factor).astype(BF16), (np.sin(angle) * factor).astype(BF16)


def nn(a, b):
    return lax.dot_general(a, b, (((1,), (0,)), ((), ())), preferred_element_type=F32)


def nt(a, b):
    return lax.dot_general(a, b, (((1,), (1,)), ((), ())), preferred_element_type=F32)


def tn(a, b):
    return lax.dot_general(a, b, (((0,), (0,)), ((), ())), preferred_element_type=F32)


def total(refs):
    terms = [ref[...].astype(F32) for ref in refs]
    while len(terms) > 1:
        odd = [terms[-1]] if len(terms) % 2 else []
        terms = [a + b for a, b in zip(terms[::2], terms[1::2])] + odd
    return terms[0]


def arrived(sent_ref, got_ref):
    sent, got = sent_ref[...].astype(F32), got_ref[...].astype(F32)
    even = lax.axis_index("cuts") % 2 == 0
    return jnp.where(even, sent, got), jnp.where(even, got, sent)


def factor_matrix(v_re, v_im):
    top = jnp.concatenate([v_re, -v_im], axis=1)
    bottom = jnp.concatenate([v_im, v_re], axis=1)
    return jnp.concatenate([top, bottom], axis=0).astype(BF16)


def own_and_rest(v_ref, others):
    _, own, rank = v_ref.shape
    v = v_ref[...].astype(F32)
    starts = range(0, rank * (lax.axis_size("frame") - 1), rank)
    rest = [
        jnp.concatenate([others[p * own : (p + 1) * own, a : a + rank] for a in starts], axis=0)
        for p in range(2)
    ]
    return (v[0], v[1]), rest


def adjoint_pair(w):
    half = w.shape[1] // 2
    return jnp.concatenate([w, jnp.concatenate([-w[:, half:], w[:, :half]], axis=1)], axis=0)


def tree(value):
    terms = [value[i] for i in range(value.shape[0])]
    while len(terms) > 1:
        odd = [terms[-1]] if len(terms) % 2 else []
        terms = [a + b for a, b in zip(terms[::2], terms[1::2])] + odd
    return terms[0].astype(F32)


def frame_of(step, own):
    return ((step // own) ^ lax.axis_index("frame")) * own + step % own


def stage_kernel(real, coils, after_ref, table_ref, b_ref, *refs):
    del after_ref
    taby_out, tabz_out, coil_out, b_out, turn_ref = refs
    width, depth, pad = taby_out.shape[0], tabz_out.shape[0], coil_out.shape[1]
    taby_out[...] = table_ref[:width, : 2 * width].astype(BF16)
    table = table_ref[width : width + depth, : 2 * depth].astype(BF16)
    column = lax.broadcasted_iota(jnp.int32, coil_out.shape, 1) // real
    row = lax.broadcasted_iota(jnp.int32, coil_out.shape, 0)
    coil_out[...] = ((row == column) & (row < coils)).astype(F32).astype(BF16)
    slice_of = lax.broadcasted_iota(jnp.int32, (depth, pad), 1) % real
    slice_of = slice_of + lax.axis_index("cuts") * real
    own = (lax.broadcasted_iota(jnp.int32, (depth, pad), 0) == slice_of).astype(F32).astype(BF16)
    tabz_out[...] = jnp.concatenate(
        [nn(table[:, :depth], own), nn(table[:, depth:], own)], axis=1
    ).astype(BF16)
    images, slab, width = b_ref.shape
    pitch = turn_ref.shape[1] // images
    for h in range(width // LANES):
        lanes = slice(h * LANES, (h + 1) * LANES)
        for n in range(images):
            turn_ref[h, n * pitch : n * pitch + slab, :] = b_ref[n, :, lanes].astype(F32)
        for z in range(slab):
            rows = turn_ref[h, pl.ds(z, images, stride=pitch), :].astype(BF16)
            for k in range(z, b_out.shape[0], slab):
                b_out[k, :, lanes] = rows


def write_tables(pos, taby_ref, tabz_ref, w_ref, fz_ref):
    per, frames = pos.shape[0] // 2, pos.shape[1]
    at_y = lax.broadcasted_iota(jnp.int32, (per, taby_ref.shape[0]), 1).astype(F32)
    at_z = lax.broadcasted_iota(jnp.int32, (per, tabz_ref.shape[0]), 1).astype(F32)
    group = max(1, 128 // per)
    for g in range(0, frames, group):
        hot_y, hot_z = (
            jnp.concatenate(
                [
                    jnp.where(iota == pos[first : first + per, t : t + 1], 1.0, 0.0)
                    for t in range(g, g + group)
                ],
                axis=0,
            ).astype(BF16)
            for iota, first in ((at_y, 0), (at_z, per))
        )
        rows = slice(g * per, (g + group) * per)
        w_ref[rows, :] = nn(hot_y, taby_ref[...]).astype(BF16)
        fz_ref[rows, :] = nn(hot_z, tabz_ref[...]).astype(BF16)


def samples_step(x_ref, frames, per):
    return x_ref.shape[1] // (2 * per)


def predict_kernel(own, frames, slab, *refs):
    sent_ref, got_ref, v_ref, taby_ref, tabz_ref, coil_ref, b_ref, m_ref, kd_ref = refs[:9]
    pred_ref, w_ref, fz_ref, x_ref, i_ref = refs[9:]
    steps = frames
    width = b_ref.shape[2]
    rows = m_ref.shape[1]
    pad = fz_ref.shape[1] // 2
    per = w_ref.shape[0] // frames
    coils = rows // slab
    halves = width // LANES
    pitch = 2 * steps + PITCH
    stride = samples_step(x_ref, frames, per)

    pos, others = arrived(sent_ref, got_ref)
    write_tables(pos[: 2 * per, :frames], taby_ref, tabz_ref, w_ref, fz_ref)
    mine, rest = own_and_rest(v_ref, others)
    v = factor_matrix(*(jnp.concatenate(both, axis=0) for both in zip(mine, rest)))
    for z in range(slab):
        image = nn(v, b_ref[z])
        for h in range(halves):
            i_ref[h, z * pitch : z * pitch + 2 * steps, :] = image[:, h * LANES : (h + 1) * LANES]

    m_re = m_ref[0].reshape(coils, slab, width)
    m_im = m_ref[1].reshape(coils, slab, width)

    def frame(step, carry):
        t = frame_of(step, own)
        i_re, i_im = (
            jnp.concatenate(
                [i_ref[h, pl.ds(at, slab, stride=pitch), :] for h in range(halves)], axis=1
            ).astype(BF16)[None]
            for at in (step, steps + step)
        )
        p_re = (m_re * i_re - m_im * i_im).reshape(rows, width)
        p_im = (m_re * i_im + m_im * i_re).reshape(rows, width)
        at = pl.ds(pl.multiple_of(t * per, TILE), per)
        lhs = adjoint_pair(w_ref[at, :])
        y = nt(lhs[:, :width], p_re) + nt(lhs[:, width:], p_im)
        y_re, y_im = y[:per], y[per:]
        f = fz_ref[at, :].astype(F32)
        f_cos, f_sin = f[:, :rows], f[:, pad : pad + rows]
        x = jnp.concatenate([y_re * f_cos + y_im * f_sin, y_im * f_cos - y_re * f_sin], axis=0)
        for h in range(x_ref.shape[0]):
            lanes = min(LANES, rows - h * LANES)
            x_ref[h, pl.ds(t, 2 * per, stride=stride), :lanes] = x[:, h * LANES : h * LANES + lanes]
        return carry

    lax.fori_loop(0, steps, frame, 0, unroll=math.gcd(steps, 16))
    blocks = max(1, min(8, 512 // frames))
    for s in range(0, 2 * per, blocks):
        x = jnp.concatenate(
            [
                jnp.concatenate(
                    [x_ref[h, k * stride : k * stride + frames, :] for h in range(x_ref.shape[0])],
                    axis=1,
                )[:, :rows]
                for k in range(s, s + blocks)
            ],
            axis=0,
        )
        pred_ref[:, s * frames : (s + blocks) * frames] = nt(
            coil_ref[:, :rows], x.astype(BF16)
        ).astype(BF16)
    size = kd_ref.shape[2]
    for part in range(2):
        at = part * per * frames + lax.axis_index("cuts") * size
        at = pl.ds(pl.multiple_of(at, LANES), size)
        pred_ref[:, at] = (pred_ref[:, at].astype(F32) - kd_ref[part].astype(F32)).astype(BF16)


def gradient_kernel(first, steps, own, frames, slab, scale, n_r, *refs):
    r_refs, refs = refs[:n_r], refs[n_r:]
    if n_r:
        b_ref, m_ref, w_ref, fz_ref, coil_ref, fg_ref, gz_ref, r_ref, g_ref = refs
    else:
        b_ref, m_ref, w_ref, fz_ref, r_ref, fg_ref, gz_ref, g_ref = refs
    width = b_ref.shape[2]
    rank = b_ref.shape[1] // 2
    rows = m_ref.shape[1]
    pad = fz_ref.shape[1] // 2
    per = w_ref.shape[0] // frames
    coils = rows // slab
    halves = width // LANES
    pitch = 2 * steps + PITCH
    stride = samples_step(r_ref, frames, per)

    if n_r:
        resid = total(r_refs).astype(BF16)
        blocks = max(1, min(8, 512 // frames))
        for s in range(0, 2 * per, blocks):
            r = tn(resid[:, s * frames : (s + blocks) * frames], coil_ref[...])
            for k in range(blocks):
                at = slice((s + k) * stride, (s + k) * stride + frames)
                for h in range(r_ref.shape[0]):
                    r_ref[h, at, :] = r[
                        k * frames : (k + 1) * frames, h * LANES : (h + 1) * LANES
                    ]

    m_re = m_ref[0].reshape(coils, slab, width)
    m_im = m_ref[1].reshape(coils, slab, width)

    def frame(step, carry):
        t = frame_of(first + step, own)
        at = pl.ds(pl.multiple_of(t * per, TILE), per)
        rhs = adjoint_pair(w_ref[at, :])
        f = fz_ref[at, :].astype(F32)
        f_cos, f_sin = f[:, :pad], f[:, pad:]
        r = jnp.concatenate(
            [r_ref[h, pl.ds(t, 2 * per, stride=stride), :] for h in range(r_ref.shape[0])], axis=1
        )
        r_re, r_im = r[:per], r[per:]
        q = jnp.concatenate([r_re * f_cos - r_im * f_sin, r_im * f_cos + r_re * f_sin], axis=0)
        u = tn(q[:, :rows].astype(BF16), rhs).astype(BF16)
        u_re = u[:, :width].reshape(coils, slab, width)
        u_im = u[:, width:].reshape(coils, slab, width)
        g_re = tree(m_re * u_re + m_im * u_im)
        g_im = tree(m_re * u_im - m_im * u_re)
        for h in range(halves):
            lanes = slice(h * LANES, (h + 1) * LANES)
            g_ref[h, pl.ds(step, slab, stride=pitch), :] = g_re[:, lanes]
            g_ref[h, pl.ds(steps + step, slab, stride=pitch), :] = g_im[:, lanes]
        return carry

    lax.fori_loop(0, steps, frame, 0, unroll=math.gcd(steps, 16))
    acc = jnp.zeros((2 * steps, 2 * rank), F32)
    for z in range(slab):
        at = pl.ds(z * pitch, 2 * steps)
        g = jnp.concatenate([g_ref[h, at, :] for h in range(halves)], axis=1).astype(BF16)
        gz_ref[z] = g
        acc = acc + nt(g, b_ref[z])
    top, bottom = acc[:steps], acc[steps:]
    fg = jnp.concatenate(
        [top[:, :rank] + bottom[:, rank:], bottom[:, :rank] - top[:, rank:]], axis=1
    )
    fg_ref[...] = (fg * scale).reshape(fg_ref.shape)


def basis_kernel(sent_ref, got_ref, v_ref, rest_ref, own_ref, grad_ref):
    slab, _, width = own_ref.shape
    mine, rest = own_and_rest(v_ref, arrived(sent_ref, got_ref)[1])
    v_own, v_rest = factor_matrix(*mine), factor_matrix(*rest)
    halves = width // LANES
    for z in range(slab):
        grad = tn(v_own, own_ref[z]) + tn(v_rest, rest_ref[z])
        for h in range(halves):
            grad_ref[pl.ds(z * halves + h, grad.shape[0], stride=slab * halves), :] = grad[
                :, h * LANES : (h + 1) * LANES
            ]


def stages(size):
    steps, stride = [(1, 2)], 2
    if (size // stride).bit_length() % 2 == 0:
        steps.append((stride, 2))
        stride *= 2
    while stride < size:
        steps.append((stride, 4))
        stride *= 4
    return steps


def swap(value, axis, distance):
    size = lax.axis_size(axis)
    return lax.ppermute(value, axis, [(i, i ^ distance) for i in range(size)])


def shares(value, axis, last=1):
    steps = stages(lax.axis_size(axis))
    for number, (stride, radix) in enumerate(steps):
        if number + last == len(steps) + 1:
            return value
        terms = [value] + [swap(value, axis, stride * d) for d in range(1, radix)]
        if number + 1 < len(steps):
            value = pairs([term.astype(F32) for term in terms]).astype(value.dtype)
    return terms


def grown(value, rows, lanes):
    return jnp.pad(value, ((0, rows - value.shape[0]), (0, lanes - value.shape[1])))


def collect(positions, v_own, meanwhile):
    n_cuts, n_frame = lax.axis_size("cuts"), lax.axis_size("frame")
    even = lax.axis_index("cuts") % 2 == 0
    stride, radix = stages(n_cuts)[-1]
    near = shares(positions, "cuts", last=2)
    rank = v_own.shape[2]
    rows = max(near.shape[0], math.prod(v_own.shape[:2]))
    lanes = max(near.shape[1], rank)
    v_packet = grown(v_own.reshape(-1, rank).astype(near.dtype), rows, lanes)
    near, v_packet = lax.optimization_barrier((near, v_packet))
    packet = jnp.where(even, grown(near, rows, lanes), v_packet)
    got = []
    for d in range(1, max(radix, n_frame)):
        route = []
        for c in range(n_cuts):
            for f in range(n_frame):
                if c % 2 == 0 and d < radix:
                    route.append((c * n_frame + f, (c ^ stride * d) * n_frame + f))
                if c % 2 == 1 and d < n_frame:
                    route.append((c * n_frame + f, c * n_frame + (f ^ d)))
        got.append(lax.ppermute(packet, ("cuts", "frame"), route))
    staged = meanwhile(packet)
    got, staged = lax.optimization_barrier((got, staged))
    joined = pairs([x.astype(F32) for x in (packet, *got[: radix - 1])]).astype(near.dtype)
    others = jnp.concatenate([x[:, :rank] for x in got[: n_frame - 1]], axis=1)
    lanes = max(lanes, others.shape[1])
    sent = jnp.where(even, grown(joined, rows, lanes), grown(others, rows, lanes))
    return sent, swap(sent, "cuts", 1), staged


def call(kernel, outs, scratch, flops, *operands, limit=0):
    def size(x):
        rows = [-(-x.shape[-2] // TILE) * TILE, -(-x.shape[-1] // LANES) * LANES]
        return math.prod(x.shape[:-2]) * math.prod(rows) * jnp.dtype(x.dtype).itemsize

    nbytes = sum(size(x) for x in operands)
    held = nbytes + sum(size(x) for x in (*outs, *scratch))
    limit = limit or min(56, 10 + held * 5 // (4 * 1024 * 1024))
    return pl.pallas_call(
        kernel,
        out_shape=outs,
        scratch_shapes=scratch,
        compiler_params=pltpu.CompilerParams(vmem_limit_bytes=limit * 1024 * 1024),
        cost_estimate=pl.CostEstimate(flops=flops, bytes_accessed=nbytes, transcendentals=0),
    )(*operands)


def one_position(basis, coil_maps, factors, lines, kdata, scale):
    n_cuts, n_frame = lax.axis_size("cuts"), lax.axis_size("frame")
    cut = lax.axis_index("cuts")
    rank, slab, width = basis.shape[1:]
    coils = coil_maps.shape[1]
    columns = lines.shape[1]
    frames = lines.shape[0]
    own = factors.shape[2]
    rest = frames - own
    per = columns * n_cuts
    samples = frames * per
    depth = slab * n_cuts
    ky_rows = width // n_cuts

    spread = max(1, TILE // slab)
    tall = spread * slab
    coil_groups = -(-coils // spread)
    rows = coil_groups * tall
    pad = -(-rows // LANES) * LANES
    coil_rows = -(-coils // TILE) * TILE

    kind = BF16 if max(width, depth) <= 256 else F32
    turned = lines.T
    mine = jnp.stack([cut * ky_rows + turned // depth, turned % depth])
    owner = jnp.arange(n_cuts, dtype=jnp.int32)[None, :, None, None] == cut
    placed = jnp.where(owner, mine[:, None], 0).astype(kind).reshape(2 * per, frames)
    v_own = factors.transpose(0, 2, 1)
    table_y = np.concatenate(dft_parts(width), axis=1).astype(np.float32)
    table_z = np.concatenate(dft_parts(depth), axis=1).astype(np.float32)
    lanes = max(table_y.shape[1], table_z.shape[1])
    tables = jnp.asarray(
        np.concatenate([np.pad(x, ((0, 0), (0, lanes - x.shape[1]))) for x in (table_y, table_z)])
    )
    m_rows = jnp.pad(coil_maps, ((0, 0), (0, coil_groups * spread - coils), (0, 0), (0, 0)))
    m_rows = m_rows.reshape(2, rows, width)
    kd = kdata.transpose(0, 3, 2, 1).reshape(2, coils, columns * frames)
    kd = jnp.pad(kd, ((0, 0), (0, coil_rows - coils), (0, 0)))

    flops = 2 * 2 * per * rows * 2 * width * 8
    halves = width // LANES
    x_shape = jax.ShapeDtypeStruct((pad // LANES, 2 * per * (frames + PITCH), LANES), F32)

    def images(steps):
        return pltpu.VMEM((halves, tall * (2 * steps + PITCH), LANES), F32)

    def stage(packet):
        return call(
            functools.partial(stage_kernel, slab, coils),
            (
                jax.ShapeDtypeStruct((width, 2 * width), BF16),
                jax.ShapeDtypeStruct((depth, 2 * pad), BF16),
                jax.ShapeDtypeStruct((coil_rows, pad), BF16),
                jax.ShapeDtypeStruct((tall, 2 * rank, width), BF16),
            ),
            [pltpu.VMEM((halves, 2 * rank * (-(-slab // 8) * 8 + PITCH), LANES), F32)],
            2 * 1024 * 1024 * 1024,
            packet, tables, basis.reshape(2 * rank, slab, width),
        )

    sent, got, (taby, tabz, coil_of, b_rows) = collect(placed, v_own, stage)
    predicted, w, fz = call(
        functools.partial(predict_kernel, own, frames, tall),
        (
            jax.ShapeDtypeStruct((coil_rows, 2 * samples), BF16),
            jax.ShapeDtypeStruct((samples, 2 * width), BF16),
            jax.ShapeDtypeStruct((samples, 2 * pad), BF16),
        ),
        [pltpu.VMEM(x_shape.shape, F32), images(frames)],
        flops * frames,
        sent, got, v_own, taby, tabz, coil_of, b_rows, m_rows, kd,
    )
    resid_terms = shares(predicted, "cuts")

    def gradient(first, steps, n_r, *operands):
        outs = [
            jax.ShapeDtypeStruct((steps // own, own, 2 * rank), F32),
            jax.ShapeDtypeStruct((tall, 2 * steps, width), BF16),
        ] + ([x_shape] if n_r else [])
        return call(
            functools.partial(gradient_kernel, first, steps, own, frames, tall, scale, n_r),
            tuple(outs),
            [images(steps)],
            flops * steps,
            *operands,
        )

    fg_rest, g_rest, r = gradient(
        own, rest, len(resid_terms), *resid_terms, b_rows, m_rows, w, fz, coil_of
    )
    others = [swap(fg_rest[d - 1], "frame", d) for d in range(1, n_frame)]
    fg_own, g_own = gradient(0, own, 0, b_rows, m_rows, w, fz, r)
    (grad,) = call(
        basis_kernel,
        (jax.ShapeDtypeStruct((2 * rank * tall * halves, LANES), F32),),
        [],
        2 * 2 * rank * 2 * frames * tall * width * 8,
        sent, got, v_own, g_rest, g_own,
    )
    if spread > 1:
        grad = jnp.sum(grad.reshape(2, rank, spread, slab, width), axis=2)
    return grad.reshape(2, rank, slab, width), pairs([fg_own[0], *others])


def pairs(terms):
    while len(terms) > 1:
        odd = [terms[-1]] if len(terms) % 2 else []
        terms = [a + b for a, b in zip(terms[::2], terms[1::2])] + odd
    return terms[0]


def body(basis, coil_maps, factors, lines, kdata):
    n_cuts, n_frame = lax.axis_size("cuts"), lax.axis_size("frame")
    readout = basis.shape[3]
    rank = basis.shape[1]
    own = factors.shape[2]
    scale = 1.0 / math.sqrt(coil_maps.shape[1] * lines.shape[1] * n_cuts * readout * n_frame)
    grads, fg = [], 0.0
    for x in range(readout):
        grad, term = one_position(
            basis[:, :, :, x], coil_maps[:, :, :, x], factors, lines, kdata[..., x], scale
        )
        grads.append(grad)
        fg = fg + term
    basis_grad = grads[0][:, :, :, None] if readout == 1 else jnp.stack(grads, axis=3)
    summed = pairs(shares(fg, "cuts"))
    return basis_grad, summed.reshape(own, 2, rank).transpose(1, 2, 0)


def solution(mesh):
    placed = (
        P(None, None, "cuts", "frame", None),
        P(None, None, "cuts", "frame", None),
        P(None, None, "frame"),
        P(None, "cuts"),
        P(None, None, "cuts", None, "frame"),
    )
    return jax.shard_map(
        body,
        mesh=mesh,
        in_specs=placed,
        out_specs=(P(None, None, "cuts", "frame", None), P(None, None, "frame")),
        check_vma=False,
    )
```

time: 52.1 us -> 47.1 us (0.904)
  blocking collectives: 13.8 us -> 0 us
  starting transfers between devices: 13.4 us -> 17.1 us
  waiting for transfers between devices: 7.22 us -> 10 us
  Pallas kernels: 12.8 us -> 14.1 us
  other arithmetic: 0.19 us -> 0.99 us
    all_to_all x1 -> x0, blocking collectives: 13.8 us -> none  [body(): lax.all_to_all(pieces, ('cuts', 'frame'), 0, 0, tiled=True)]
    ppermute x0 -> x3, starting transfers between devices: none -> 4.49 us  [collect(): got.append(lax.ppermute(packet, ('cuts', 'frame'), route))]
    ppermute x11 -> x13, waiting for transfers between devices: 7.22 us -> 9.04 us  [swap(): return lax.ppermute(value, axis, [(i, i ^ distance) for i in range(size)])]
    pallas_call x2 -> x5, Pallas kernels: 12.8 us -> 14.1 us  [call(): pl.pallas_call(kernel, out_shape=outs, scratch_shapes=scratch, compiler_p...]
    another operation x6 -> x0, local copies, waits for them, and re-layouts: 0.99 us -> none  [the longest x2 0.5 us: one_position(): kd = jnp.tile(kdata.transpose(3, 1, 0, 2), (1, 1, 1, n_cuts))]
    ppermute x0 -> x3, waiting for transfers between devices: none -> 0.98 us  [collect(): got.append(lax.ppermute(packet, ('cuts', 'frame'), route))]
    transpose x3 -> x0, local copies, waits for them, and re-layouts: 0.74 us -> none  [the longest x1 0.61 us: body(): factor_grad = folded.transpose(2, 3, 1, 0).reshape(2, rank, own)]
    ppermute x11 -> x13, starting transfers between devices: 13.4 us -> 12.7 us  [swap(): return lax.ppermute(value, axis, [(i, i ^ distance) for i in range(size)])]
  transfers between devices with their start and end apart: 11 -> 16, of which waited for: 7 -> 12; matrix products, arithmetic and copies ran while one was open for 2% -> 2% of each run, Pallas kernels for 0% -> 8%
where the time goes in v3:
time: 47.1 us; the launch traced here: 46.9 us
  starting transfers between devices  17.1 us (36%)
  Pallas kernels  14.1 us (30%)
  waiting for transfers between devices  10 us (21%)
  local copies, waits for them, and re-layouts  3.86 us (8%)
  other arithmetic  0.99 us (2%)
  between operations  0.72 us (2%)
    pallas_call x5, Pallas kernels, call(): pl.pallas_call(kernel, out_shape=outs, scratch_shapes=scratch, compiler_p...  14.1 us
    ppermute x13, starting transfers between devices, swap(): return lax.ppermute(value, axis, [(i, i ^ distance) for i in range(size)])  12.7 us
    ppermute x13, waiting for transfers between devices, swap(): return lax.ppermute(value, axis, [(i, i ^ distance) for i in range(size)])  9.04 us
    ppermute x3, starting transfers between devices, collect(): got.append(lax.ppermute(packet, ('cuts', 'frame'), route))  4.49 us
    unnamed x10, local copies, waits for them, and re-layouts  2.18 us
    ppermute x3, waiting for transfers between devices, collect(): got.append(lax.ppermute(packet, ('cuts', 'frame'), route))  0.98 us
  transfers between devices with their start and end apart: 16, of which 12 were waited for; matrix products, arithmetic and copies ran while one was open for 2% of the time, Pallas kernels for 8%

profile of v3, /device:TPU:0, one launch (start us, length us, event | category | flops | bytes accessed | tf_op | source)
XLA Modules:
  0.0 46.9 jit_solution(14726260931805949382)
XLA Ops:
  0.6 0.1 broadcast_in_dim.28
  0.7 0.1 broadcast_in_dim.29
  0.8 0.7 %add_bitcast_fusion = (s32[1,2,64]{2,1,0:T(2,128)S(1)}, s32[1,2,64]{2,1,0:T(2,128)S(1)}) fusion(s32[64,2]{0,1:T(2,128)} %param.9, s32[]{:T(128)S(6)} %mul.3), kind=kLoop, calls=%fused_computation.22 | loop fusion | flops 2560 | bytes 1540 | tf_op jit(solution)/shard_map/stack | solution.py:389
  1.5 0.1 select_convert_fusion
  1.6 0.5 collective-permute-start
  2.1 0.7 %pad.12 = bf16[32,64]{1,0:T(8,128)(2,1)S(1)} pad(bf16[32,32]{1,0:T(8,128)(2,1)} %bitcast.55, bf16[]{:T(256)} %constant.51.clone.1), padding=0_0x0_32 | pad | bytes 6146 | tf_op jit(solution)/shard_map/jit(_pad)/pad | solution.py:316
  2.8 0.1 collective-permute-done
  2.9 0.1 add_convert_fusion.2
  3.0 3.8 %collective-permute-start.3 = (bf16[32,64]{1,0:T(8,128)(2,1)S(1)}, bf16[32,64]{1,0:T(8,128)(2,1)S(1)}, u32[]{:S(2)}, u32[]{:S(2)}) collective-permute-start(bf16[32,64]{1,0:T(8,128)(2,1)S(1)} %broadcast_select_fusion.after_ref), channel_id=1, source_target_pairs={{0,24},{1,25},{2,26},{3,27},{4,7},{5,6},{6,5},{7,4},{8,16},{9,17},... | collective-permute-start | bytes 12296 | tf_op jit(solution)/shard_map/ppermute | solution.py:339
  6.8 0.5 %collective-permute-start.2 = (bf16[32,64]{1,0:T(8,128)(2,1)S(1)}, bf16[32,64]{1,0:T(8,128)(2,1)S(1)}, u32[]{:S(2)}, u32[]{:S(2)}) collective-permute-start(bf16[32,64]{1,0:T(8,128)(2,1)S(1)} %broadcast_select_fusion.after_ref), channel_id=1, source_target_pairs={{0,16},{1,17},{2,18},{3,19},{4,6},{5,7},{6,4},{7,5},{8,24},{9,25},... | collective-permute-start | bytes 12296 | tf_op jit(solution)/shard_map/ppermute | solution.py:339
  7.3 0.1 collective-permute-start.1
  7.5 0.0 copy-start.2
  7.5 1.0 %copy-done.2 = bf16[2,32,16,1,256]{4,2,3,1,0:T(8,128)(2,1)S(1)} copy-done((bf16[2,32,16,1,256]{4,2,3,1,0:T(8,128)(2,1)S(1)}, bf16[2,32,16,1,256]{4,2,3,1,0:T(8,128)(2,1)}, u32[]{:S(2)}) %copy-start.2) | copy-done | bytes 524312
  8.5 0.0 copy-start.3
  8.5 1.1 %copy-done.3 = f32[384,512]{1,0:T(8,128)S(1)} copy-done((f32[384,512]{1,0:T(8,128)S(1)}, f32[384,512]{1,0:T(8,128)}, u32[]{:S(2)}) %copy-start.3) | copy-done | bytes 786456
  9.6 0.0 copy-start.4
  9.7 0.0 copy-start
  9.7 0.0 copy-start.1
  9.7 0.3 shard_map.77
  10.0 0.0 collective-permute-done.3
  10.0 0.5 %collective-permute-done.2 = bf16[32,64]{1,0:T(8,128)(2,1)S(1)} collective-permute-done((bf16[32,64]{1,0:T(8,128)(2,1)S(1)}, bf16[32,64]{1,0:T(8,128)(2,1)S(1)}, u32[]{:S(2)}, u32[]{:S(2)}) %collective-permute-start.2) | collective-permute-done | bytes 4128 | tf_op jit(solution)/shard_map/ppermute | solution.py:339
  10.5 0.5 %collective-permute-done.1 = bf16[32,64]{1,0:T(8,128)(2,1)S(1)} collective-permute-done((bf16[32,64]{1,0:T(8,128)(2,1)S(1)}, bf16[32,64]{1,0:T(8,128)(2,1)S(1)}, u32[]{:S(2)}, u32[]{:S(2)}) %collective-permute-start.1) | collective-permute-done | bytes 4128 | tf_op jit(solution)/shard_map/ppermute | solution.py:339
  11.0 0.1 maximum_select_fusion.refs_0_.sent_ref
  11.1 0.3 collective-permute-start.4
  11.4 0.0 copy-done.4
  11.4 0.1 reshape.30
  11.5 0.8 %collective-permute-done.4.refs_1_.got_ref = bf16[32,96]{1,0:T(8,128)(2,1)S(1)} collective-permute-done((bf16[32,96]{1,0:T(8,128)(2,1)S(1)}, bf16[32,96]{1,0:T(8,128)(2,1)S(1)}, u32[]{:S(2)}, u32[]{:S(2)}) %collective-permute-start.4) | collective-permute-done | bytes 6176 | tf_op jit(solution)/shard_map/ppermute | solution.py:301
  12.3 0.0 copy-done
  12.3 0.0 copy-done.1
  12.3 6.0 %shard_map.78 = (bf16[16,2048]{1,0:T(8,128)(2,1)S(1)}, bf16[1024,512]{1,0:T(8,128)(2,1)S(1)}, bf16[1024,512]{1,0:T(8,128)(2,1)S(1)}) custom-call(bf16[32,96]{1,0:T(8,128)(2,1)S(1)} %maximum_select_fusion.refs_0_.sent_ref, bf16[32,96]{1,0:T(8,128)(2,1)S(1)} %collective-permute-done.4.refs_1_.got_ref, bf16[2,16,32]{2,1,0:T(8,128)(2,1)S(1)} %bitcast.56, ...), custom_call_target="tpu_custom_call" | custom-call | flops 3221225472 | bytes 1155072 | tf_op jit(solution)/shard_map/pallas_call | solution.py:357
  18.3 0.3 collective-permute-start.5
  18.6 1.0 %collective-permute-done.5 = bf16[16,2048]{1,0:T(8,128)(2,1)S(1)} collective-permute-done((bf16[16,2048]{1,0:T(8,128)(2,1)S(1)}, bf16[16,2048]{1,0:T(8,128)(2,1)S(1)}, u32[]{:S(2)}, u32[]{:S(2)}) %collective-permute-start.5) | collective-permute-done | bytes 65568 | tf_op jit(solution)/shard_map/ppermute | solution.py:301
  19.7 2.4 %collective-permute-start.8 = (bf16[16,2048]{1,0:T(8,128)(2,1)S(1)}, bf16[16,2048]{1,0:T(8,128)(2,1)S(1)}, u32[]{:S(2)}, u32[]{:S(2)}) collective-permute-start(bf16[16,2048]{1,0:T(8,128)(2,1)S(1)} %add_convert_fusion.refs_0_), channel_id=1, source_target_pairs={{0,24},{4,28},{8,16},{12,20},{16,8},{20,12},{24,0},{28,4},{1,25},{... | collective-permute-start | bytes 196616 | tf_op jit(solution)/shard_map/ppermute | solution.py:301
  22.1 0.5 %collective-permute-start.7 = (bf16[16,2048]{1,0:T(8,128)(2,1)S(1)}, bf16[16,2048]{1,0:T(8,128)(2,1)S(1)}, u32[]{:S(2)}, u32[]{:S(2)}) collective-permute-start(bf16[16,2048]{1,0:T(8,128)(2,1)S(1)} %add_convert_fusion.refs_0_), channel_id=1, source_target_pairs={{0,16},{4,20},{8,24},{12,28},{16,0},{20,4},{24,8},{28,12},{1,17},{... | collective-permute-start | bytes 196616 | tf_op jit(solution)/shard_map/ppermute | solution.py:301
  22.6 0.6 %collective-permute-start.6 = (bf16[16,2048]{1,0:T(8,128)(2,1)S(1)}, bf16[16,2048]{1,0:T(8,128)(2,1)S(1)}, u32[]{:S(2)}, u32[]{:S(2)}) collective-permute-start(bf16[16,2048]{1,0:T(8,128)(2,1)S(1)} %add_convert_fusion.refs_0_), channel_id=1, source_target_pairs={{0,8},{4,12},{8,0},{12,4},{16,24},{20,28},{24,16},{28,20},{1,9},{5... | collective-permute-start | bytes 196616 | tf_op jit(solution)/shard_map/ppermute | solution.py:301
  23.2 1.7 %collective-permute-done.8.refs_3_ = bf16[16,2048]{1,0:T(8,128)(2,1)S(1)} collective-permute-done((bf16[16,2048]{1,0:T(8,128)(2,1)S(1)}, bf16[16,2048]{1,0:T(8,128)(2,1)S(1)}, u32[]{:S(2)}, u32[]{:S(2)}) %collective-permute-start.8) | collective-permute-done | bytes 65568 | tf_op jit(solution)/shard_map/ppermute | solution.py:301
  24.9 1.5 %collective-permute-done.7.refs_2_ = bf16[16,2048]{1,0:T(8,128)(2,1)S(1)} collective-permute-done((bf16[16,2048]{1,0:T(8,128)(2,1)S(1)}, bf16[16,2048]{1,0:T(8,128)(2,1)S(1)}, u32[]{:S(2)}, u32[]{:S(2)}) %collective-permute-start.7) | collective-permute-done | bytes 65568 | tf_op jit(solution)/shard_map/ppermute | solution.py:301
  26.4 0.5 %collective-permute-done.6.refs_1_ = bf16[16,2048]{1,0:T(8,128)(2,1)S(1)} collective-permute-done((bf16[16,2048]{1,0:T(8,128)(2,1)S(1)}, bf16[16,2048]{1,0:T(8,128)(2,1)S(1)}, u32[]{:S(2)}, u32[]{:S(2)}) %collective-permute-start.6) | collective-permute-done | bytes 65568 | tf_op jit(solution)/shard_map/ppermute | solution.py:301
  26.9 4.1 %shard_map.79 = (f32[3,16,64]{2,1,0:T(8,128)S(1)}, bf16[16,96,256]{2,1,0:T(8,128)(2,1)S(1)}, f32[2,2304,128]{2,1,0:T(8,128)S(1)}) custom-call(bf16[16,2048]{1,0:T(8,128)(2,1)S(1)} %add_convert_fusion.refs_0_, bf16[16,2048]{1,0:T(8,128)(2,1)S(1)} %collective-permute-done.6.refs_1_, bf16[16,2048]{1,0:T(8,128)(2,1)S(1)} %collective-permute-done.7.refs_2_, ...), custom_call_target="tpu_custom_call" | custom-call | flops 2415919104 | bytes 3088384 | tf_op jit(solution)/shard_map/pallas_call | solution.py:357
  31.0 3.2 %collective-permute-start.11 = (f32[16,64]{1,0:T(8,128)S(1)}, f32[16,64]{1,0:T(8,128)S(1)}, u32[]{:S(2)}, u32[]{:S(2)}) collective-permute-start(f32[16,64]{1,0:T(8,128)S(1)} %get-tuple-element.48), channel_id=1, source_target_pairs={{0,3},{1,2},{2,1},{3,0},{4,7},{5,6},{6,5},{7,4},{8,11},{9,10},{10,... | collective-permute-start | bytes 12296 | tf_op jit(solution)/shard_map/ppermute | solution.py:301
  34.2 0.0 collective-permute-start.10
  34.2 1.3 %collective-permute-start.9 = (f32[16,64]{1,0:T(8,128)S(1)}, f32[16,64]{1,0:T(8,128)S(1)}, u32[]{:S(2)}, u32[]{:S(2)}) collective-permute-start(f32[16,64]{1,0:T(8,128)S(1)} %get-tuple-element.50), channel_id=1, source_target_pairs={{0,1},{1,0},{2,3},{3,2},{4,5},{5,4},{6,7},{7,6},{8,9},{9,8},{10,11... | collective-permute-start | bytes 12296 | tf_op jit(solution)/shard_map/ppermute | solution.py:301
  35.4 1.7 %shard_map.80 = (f32[1,16,64]{2,1,0:T(8,128)S(1)}, bf16[16,32,256]{2,1,0:T(8,128)(2,1)S(1)}) custom-call(bf16[16,64,256]{2,1,0:T(8,128)(2,1)S(1)} %get-tuple-element.35.refs_6_.refs_4_.refs_0_, bf16[2,192,256]{2,1,0:T(8,128)(2,1)S(1)} %bitcast.54, bf16[1024,512]{1,0:T(8,128)(2,1)S(1)} %get-tuple-element.37.refs_6_.refs_2_, ...), custom_call_target="tpu_custom_call" | custom-call | flops 805306368 | bytes 5177344 | tf_op jit(solution)/shard_map/pallas_call | solution.py:357
  37.1 0.0 collective-permute-done.11
  37.1 1.6 %collective-permute-done.10 = f32[16,64]{1,0:T(8,128)S(1)} collective-permute-done((f32[16,64]{1,0:T(8,128)S(1)}, f32[16,64]{1,0:T(8,128)S(1)}, u32[]{:S(2)}, u32[]{:S(2)}) %collective-permute-start.10) | collective-permute-done | bytes 4128 | tf_op jit(solution)/shard_map/ppermute | solution.py:301
  38.7 0.0 collective-permute-done.9
  38.7 0.1 collective-permute-start.12
  38.8 1.2 %collective-permute-done.12 = f32[16,64]{1,0:T(8,128)S(1)} collective-permute-done((f32[16,64]{1,0:T(8,128)S(1)}, f32[16,64]{1,0:T(8,128)S(1)}, u32[]{:S(2)}, u32[]{:S(2)}) %collective-permute-start.12) | collective-permute-done | bytes 4128 | tf_op jit(solution)/shard_map/ppermute | solution.py:301
  40.0 2.0 %collective-permute-start.15 = (f32[16,64]{1,0:T(8,128)S(1)}, f32[16,64]{1,0:T(8,128)S(1)}, u32[]{:S(2)}, u32[]{:S(2)}) collective-permute-start(f32[16,64]{1,0:T(8,128)S(1)} %add.71), channel_id=1, source_target_pairs={{0,24},{4,28},{8,16},{12,20},{16,8},{20,12},{24,0},{28,4},{1,25},{... | collective-permute-start | bytes 12296 | tf_op jit(solution)/shard_map/ppermute | solution.py:301
  42.0 0.5 %collective-permute-start.14 = (f32[16,64]{1,0:T(8,128)S(1)}, f32[16,64]{1,0:T(8,128)S(1)}, u32[]{:S(2)}, u32[]{:S(2)}) collective-permute-start(f32[16,64]{1,0:T(8,128)S(1)} %add.71), channel_id=1, source_target_pairs={{0,16},{4,20},{8,24},{12,28},{16,0},{20,4},{24,8},{28,12},{1,17},{... | collective-permute-start | bytes 12296 | tf_op jit(solution)/shard_map/ppermute | solution.py:301
  42.5 1.0 %collective-permute-start.13 = (f32[16,64]{1,0:T(8,128)S(1)}, f32[16,64]{1,0:T(8,128)S(1)}, u32[]{:S(2)}, u32[]{:S(2)}) collective-permute-start(f32[16,64]{1,0:T(8,128)S(1)} %add.71), channel_id=1, source_target_pairs={{0,8},{4,12},{8,0},{12,4},{16,24},{20,28},{24,16},{28,20},{1,9},{5... | collective-permute-start | bytes 12296 | tf_op jit(solution)/shard_map/ppermute | solution.py:301
  43.5 2.0 %shard_map.81 = f32[2048,128]{1,0:T(8,128)} custom-call(bf16[32,96]{1,0:T(8,128)(2,1)S(1)} %maximum_select_fusion.refs_0_.sent_ref, bf16[32,96]{1,0:T(8,128)(2,1)S(1)} %collective-permute-done.4.refs_1_.got_ref, bf16[2,16,32]{2,1,0:T(8,128)(2,1)S(1)} %bitcast.57, bf16[16,96,256]{2,1,0:T(8,128)(2,1)S(1)} %get-tuple-element.39.rest_ref, ...), custom_call_target="tpu_custom_call" | custom-call | flops 536870912 | bytes 1073152 | tf_op jit(solution)/shard_map/pallas_call | solution.py:357
  45.4 0.0 collective-permute-done.15
  45.4 0.2 collective-permute-done.14
  45.7 0.5 %collective-permute-done.13 = f32[16,64]{1,0:T(8,128)S(1)} collective-permute-done((f32[16,64]{1,0:T(8,128)S(1)}, f32[16,64]{1,0:T(8,128)S(1)}, u32[]{:S(2)}, u32[]{:S(2)}) %collective-permute-start.13) | collective-permute-done | bytes 4128 | tf_op jit(solution)/shard_map/ppermute | solution.py:301
  46.2 0.1 reshape.29
  46.2 0.6 %copy.16 = f32[16,2,32]{2,0,1:T(8,128)} copy(f32[16,2,32]{2,1,0:T(2,128)S(1)} %reshape.29) | data formatting | bytes 8192 | tf_op jit(solution)/shard_map/reshape | solution.py:491
  (11 shorter events, 0.1 us)
Async XLA Ops:
  1.6 1.3 %collective-permute-start = (bf16[32,64]{1,0:T(8,128)(2,1)S(1)}, bf16[32,64]{1,0:T(8,128)(2,1)S(1)}, u32[]{:S(2)}, u32[]{:S(2)}) collective-permute-start(bf16[32,64]{1,0:T(8,128)(2,1)S(1)} %select_convert_fusion), channel_id=1, source_target_pairs={{0,4},{4,0},{8,12},{12,8},{16,20},{20,16},{24,28},{28,24},{1,5},{5... | collective-permute-start | bytes 12296 | tf_op jit(solution)/shard_map/ppermute | solution.py:301
  3.0 7.0 %collective-permute-start.3 = (bf16[32,64]{1,0:T(8,128)(2,1)S(1)}, bf16[32,64]{1,0:T(8,128)(2,1)S(1)}, u32[]{:S(2)}, u32[]{:S(2)}) collective-permute-start(bf16[32,64]{1,0:T(8,128)(2,1)S(1)} %broadcast_select_fusion.after_ref), channel_id=1, source_target_pairs={{0,24},{1,25},{2,26},{3,27},{4,7},{5,6},{6,5},{7,4},{8,16},{9,17},... | collective-permute-start | bytes 12296 | tf_op jit(solution)/shard_map/ppermute | solution.py:339
  6.8 3.7 %collective-permute-start.2 = (bf16[32,64]{1,0:T(8,128)(2,1)S(1)}, bf16[32,64]{1,0:T(8,128)(2,1)S(1)}, u32[]{:S(2)}, u32[]{:S(2)}) collective-permute-start(bf16[32,64]{1,0:T(8,128)(2,1)S(1)} %broadcast_select_fusion.after_ref), channel_id=1, source_target_pairs={{0,16},{1,17},{2,18},{3,19},{4,6},{5,7},{6,4},{7,5},{8,24},{9,25},... | collective-permute-start | bytes 12296 | tf_op jit(solution)/shard_map/ppermute | solution.py:339
  7.3 3.7 %collective-permute-start.1 = (bf16[32,64]{1,0:T(8,128)(2,1)S(1)}, bf16[32,64]{1,0:T(8,128)(2,1)S(1)}, u32[]{:S(2)}, u32[]{:S(2)}) collective-permute-start(bf16[32,64]{1,0:T(8,128)(2,1)S(1)} %broadcast_select_fusion.after_ref), channel_id=1, source_target_pairs={{0,8},{1,9},{2,10},{3,11},{4,5},{5,4},{6,7},{7,6},{8,0},{9,1},{10,... | collective-permute-start | bytes 12296 | tf_op jit(solution)/shard_map/ppermute | solution.py:339
  7.5 1.0 %copy-start.2 = (bf16[2,32,16,1,256]{4,2,3,1,0:T(8,128)(2,1)S(1)}, bf16[2,32,16,1,256]{4,2,3,1,0:T(8,128)(2,1)}, u32[]{:S(2)}) copy-start(bf16[2,32,16,1,256]{4,2,3,1,0:T(8,128)(2,1)} %param.6) | copy-start | bytes 1572868
  8.5 1.1 %copy-start.3 = (f32[384,512]{1,0:T(8,128)S(1)}, f32[384,512]{1,0:T(8,128)}, u32[]{:S(2)}) copy-start(f32[384,512]{1,0:T(8,128)} %constant.52.clone.table_ref) | copy-start | bytes 2359300
  9.6 1.7 %copy-start.4 = (bf16[2,64,2,12,1]{1,2,4,3,0:T(2,128)(2,1)S(1)}, bf16[2,64,2,12,1]{1,2,4,3,0:T(2,128)(2,1)}, u32[]{:S(2)}) copy-start(bf16[2,64,2,12,1]{1,2,4,3,0:T(2,128)(2,1)} %param.10) | copy-start | bytes 18436
  9.7 2.6 %copy-start = (bf16[2,12,16,1,256]{4,2,3,1,0:T(8,128)(2,1)S(1)}, bf16[2,12,16,1,256]{4,2,3,1,0:T(8,128)(2,1)}, u32[]{:S(2)}) copy-start(bf16[2,12,16,1,256]{4,2,3,1,0:T(8,128)(2,1)} %param.7) | copy-start | bytes 589828
  9.7 2.6 %copy-start.1 = (bf16[2,32,16]{1,2,0:T(8,128)(2,1)S(1)}, bf16[2,32,16]{1,2,0:T(8,128)(2,1)}, u32[]{:S(2)}) copy-start(bf16[2,32,16]{1,2,0:T(8,128)(2,1)} %param.8) | copy-start | bytes 6148
  11.1 1.2 %collective-permute-start.4 = (bf16[32,96]{1,0:T(8,128)(2,1)S(1)}, bf16[32,96]{1,0:T(8,128)(2,1)S(1)}, u32[]{:S(2)}, u32[]{:S(2)}) collective-permute-start(bf16[32,96]{1,0:T(8,128)(2,1)S(1)} %maximum_select_fusion.refs_0_.sent_ref), channel_id=1, source_target_pairs={{0,4},{4,0},{8,12},{12,8},{16,20},{20,16},{24,28},{28,24},{1,5},{5... | collective-permute-start | bytes 18440 | tf_op jit(solution)/shard_map/ppermute | solution.py:301
  18.3 1.3 %collective-permute-start.5 = (bf16[16,2048]{1,0:T(8,128)(2,1)S(1)}, bf16[16,2048]{1,0:T(8,128)(2,1)S(1)}, u32[]{:S(2)}, u32[]{:S(2)}) collective-permute-start(bf16[16,2048]{1,0:T(8,128)(2,1)S(1)} %get-tuple-element.36), channel_id=1, source_target_pairs={{0,4},{4,0},{8,12},{12,8},{16,20},{20,16},{24,28},{28,24},{1,5},{5... | collective-permute-start | bytes 196616 | tf_op jit(solution)/shard_map/ppermute | solution.py:301
  19.7 5.2 %collective-permute-start.8 = (bf16[16,2048]{1,0:T(8,128)(2,1)S(1)}, bf16[16,2048]{1,0:T(8,128)(2,1)S(1)}, u32[]{:S(2)}, u32[]{:S(2)}) collective-permute-start(bf16[16,2048]{1,0:T(8,128)(2,1)S(1)} %add_convert_fusion.refs_0_), channel_id=1, source_target_pairs={{0,24},{4,28},{8,16},{12,20},{16,8},{20,12},{24,0},{28,4},{1,25},{... | collective-permute-start | bytes 196616 | tf_op jit(solution)/shard_map/ppermute | solution.py:301
  22.1 4.3 %collective-permute-start.7 = (bf16[16,2048]{1,0:T(8,128)(2,1)S(1)}, bf16[16,2048]{1,0:T(8,128)(2,1)S(1)}, u32[]{:S(2)}, u32[]{:S(2)}) collective-permute-start(bf16[16,2048]{1,0:T(8,128)(2,1)S(1)} %add_convert_fusion.refs_0_), channel_id=1, source_target_pairs={{0,16},{4,20},{8,24},{12,28},{16,0},{20,4},{24,8},{28,12},{1,17},{... | collective-permute-start | bytes 196616 | tf_op jit(solution)/shard_map/ppermute | solution.py:301
  22.6 4.3 %collective-permute-start.6 = (bf16[16,2048]{1,0:T(8,128)(2,1)S(1)}, bf16[16,2048]{1,0:T(8,128)(2,1)S(1)}, u32[]{:S(2)}, u32[]{:S(2)}) collective-permute-start(bf16[16,2048]{1,0:T(8,128)(2,1)S(1)} %add_convert_fusion.refs_0_), channel_id=1, source_target_pairs={{0,8},{4,12},{8,0},{12,4},{16,24},{20,28},{24,16},{28,20},{1,9},{5... | collective-permute-start | bytes 196616 | tf_op jit(solution)/shard_map/ppermute | solution.py:301
  31.0 6.1 %collective-permute-start.11 = (f32[16,64]{1,0:T(8,128)S(1)}, f32[16,64]{1,0:T(8,128)S(1)}, u32[]{:S(2)}, u32[]{:S(2)}) collective-permute-start(f32[16,64]{1,0:T(8,128)S(1)} %get-tuple-element.48), channel_id=1, source_target_pairs={{0,3},{1,2},{2,1},{3,0},{4,7},{5,6},{6,5},{7,4},{8,11},{9,10},{10,... | collective-permute-start | bytes 12296 | tf_op jit(solution)/shard_map/ppermute | solution.py:301
  34.2 4.5 %collective-permute-start.10 = (f32[16,64]{1,0:T(8,128)S(1)}, f32[16,64]{1,0:T(8,128)S(1)}, u32[]{:S(2)}, u32[]{:S(2)}) collective-permute-start(f32[16,64]{1,0:T(8,128)S(1)} %get-tuple-element.49), channel_id=1, source_target_pairs={{0,2},{1,3},{2,0},{3,1},{4,6},{5,7},{6,4},{7,5},{8,10},{9,11},{10,... | collective-permute-start | bytes 12296 | tf_op jit(solution)/shard_map/ppermute | solution.py:301
  34.2 4.5 %collective-permute-start.9 = (f32[16,64]{1,0:T(8,128)S(1)}, f32[16,64]{1,0:T(8,128)S(1)}, u32[]{:S(2)}, u32[]{:S(2)}) collective-permute-start(f32[16,64]{1,0:T(8,128)S(1)} %get-tuple-element.50), channel_id=1, source_target_pairs={{0,1},{1,0},{2,3},{3,2},{4,5},{5,4},{6,7},{7,6},{8,9},{9,8},{10,11... | collective-permute-start | bytes 12296 | tf_op jit(solution)/shard_map/ppermute | solution.py:301
  38.7 1.2 %collective-permute-start.12 = (f32[16,64]{1,0:T(8,128)S(1)}, f32[16,64]{1,0:T(8,128)S(1)}, u32[]{:S(2)}, u32[]{:S(2)}) collective-permute-start(f32[16,64]{1,0:T(8,128)S(1)} %fusion), channel_id=1, source_target_pairs={{0,4},{4,0},{8,12},{12,8},{16,20},{20,16},{24,28},{28,24},{1,5},{5... | collective-permute-start | bytes 12296 | tf_op jit(solution)/shard_map/ppermute | solution.py:301
  40.0 5.5 %collective-permute-start.15 = (f32[16,64]{1,0:T(8,128)S(1)}, f32[16,64]{1,0:T(8,128)S(1)}, u32[]{:S(2)}, u32[]{:S(2)}) collective-permute-start(f32[16,64]{1,0:T(8,128)S(1)} %add.71), channel_id=1, source_target_pairs={{0,24},{4,28},{8,16},{12,20},{16,8},{20,12},{24,0},{28,4},{1,25},{... | collective-permute-start | bytes 12296 | tf_op jit(solution)/shard_map/ppermute | solution.py:301
  42.0 3.7 %collective-permute-start.14 = (f32[16,64]{1,0:T(8,128)S(1)}, f32[16,64]{1,0:T(8,128)S(1)}, u32[]{:S(2)}, u32[]{:S(2)}) collective-permute-start(f32[16,64]{1,0:T(8,128)S(1)} %add.71), channel_id=1, source_target_pairs={{0,16},{4,20},{8,24},{12,28},{16,0},{20,4},{24,8},{28,12},{1,17},{... | collective-permute-start | bytes 12296 | tf_op jit(solution)/shard_map/ppermute | solution.py:301
  42.5 3.7 %collective-permute-start.13 = (f32[16,64]{1,0:T(8,128)S(1)}, f32[16,64]{1,0:T(8,128)S(1)}, u32[]{:S(2)}, u32[]{:S(2)}) collective-permute-start(f32[16,64]{1,0:T(8,128)S(1)} %add.71), channel_id=1, source_target_pairs={{0,8},{4,12},{8,0},{12,4},{16,24},{20,28},{24,16},{28,20},{1,9},{5... | collective-permute-start | bytes 12296 | tf_op jit(solution)/shard_map/ppermute | solution.py:301

commit v4 on v3

--- a/solution.py
+++ b/solution.py
@@ -16,11 +16,24 @@
 PITCH = 8
 
 
-def dft_parts(size):
-    index = np.arange(size, dtype=np.int64)
-    angle = ((index[:, None] * index[None, :]) % size).astype(np.float64) * (2.0 * math.pi / size)
+def trig(product, size):
+    angle = (product % size).astype(F32) * (2.0 * math.pi / size)
+    return jnp.cos(angle), jnp.sin(angle)
+
+
+def write_dft(out_ref, size, index):
+    lanes = index.shape[1]
+    fine = lax.broadcasted_iota(jnp.int32, (TILE, lanes), 0)
+    b_cos, b_sin = trig(fine * index[:TILE], size)
+    coarse = lax.broadcasted_iota(jnp.int32, (size // TILE, lanes), 0) * TILE
+    a_cos, a_sin = trig(coarse * index[: size // TILE], size)
     factor = 1.0 / math.sqrt(size)
-    return (np.cos(angle) * factor).astype(BF16), (np.sin(angle) * factor).astype(BF16)
+    a_cos, a_sin = a_cos * factor, a_sin * factor
+    for a in range(size // TILE):
+        rows = slice(a * TILE, (a + 1) * TILE)
+        p_cos, p_sin = a_cos[a : a + 1], a_sin[a : a + 1]
+        out_ref[rows, :lanes] = (p_cos * b_cos - p_sin * b_sin).astype(BF16)
+        out_ref[rows, lanes:] = (p_sin * b_cos + p_cos * b_sin).astype(BF16)
 
 
 def nn(a, b):
@@ -83,21 +96,21 @@
     return ((step // own) ^ lax.axis_index("frame")) * own + step % own
 
 
-def stage_kernel(real, coils, after_ref, table_ref, b_ref, *refs):
+def tables_kernel(real, coils, after_ref, taby_ref, tabz_ref, coil_ref):
     del after_ref
-    taby_out, tabz_out, coil_out, b_out, turn_ref = refs
-    width, depth, pad = taby_out.shape[0], tabz_out.shape[0], coil_out.shape[1]
-    taby_out[...] = table_ref[:width, : 2 * width].astype(BF16)
-    table = table_ref[width : width + depth, : 2 * depth].astype(BF16)
-    column = lax.broadcasted_iota(jnp.int32, coil_out.shape, 1) // real
-    row = lax.broadcasted_iota(jnp.int32, coil_out.shape, 0)
-    coil_out[...] = ((row == column) & (row < coils)).astype(F32).astype(BF16)
-    slice_of = lax.broadcasted_iota(jnp.int32, (depth, pad), 1) % real
-    slice_of = slice_of + lax.axis_index("cuts") * real
-    own = (lax.broadcasted_iota(jnp.int32, (depth, pad), 0) == slice_of).astype(F32).astype(BF16)
-    tabz_out[...] = jnp.concatenate(
-        [nn(table[:, :depth], own), nn(table[:, depth:], own)], axis=1
-    ).astype(BF16)
+    width, depth, pad = taby_ref.shape[0], tabz_ref.shape[0], coil_ref.shape[2]
+    write_dft(taby_ref, width, lax.broadcasted_iota(jnp.int32, (max(TILE, width // TILE), width), 1))
+    slice_of = lax.broadcasted_iota(jnp.int32, (max(TILE, depth // TILE), pad), 1) % real
+    write_dft(tabz_ref, depth, slice_of + lax.axis_index("cuts") * real)
+    column = lax.broadcasted_iota(jnp.int32, coil_ref.shape[1:], 1) // real
+    row = lax.broadcasted_iota(jnp.int32, coil_ref.shape[1:], 0)
+    for part in range(2):
+        place = (row == column + part * coils) & (column < coils)
+        coil_ref[part] = place.astype(F32).astype(BF16)
+
+
+def turn_kernel(after_ref, b_ref, b_out, turn_ref):
+    del after_ref
     images, slab, width = b_ref.shape
     pitch = turn_ref.shape[1] // images
     for h in range(width // LANES):
@@ -182,35 +195,31 @@
             x_ref[h, pl.ds(t, 2 * per, stride=stride), :lanes] = x[:, h * LANES : h * LANES + lanes]
         return carry
 
-    lax.fori_loop(0, steps, frame, 0, unroll=math.gcd(steps, 16))
-    blocks = max(1, min(8, 512 // frames))
-    for s in range(0, 2 * per, blocks):
-        x = jnp.concatenate(
-            [
-                jnp.concatenate(
-                    [x_ref[h, k * stride : k * stride + frames, :] for h in range(x_ref.shape[0])],
-                    axis=1,
-                )[:, :rows]
-                for k in range(s, s + blocks)
-            ],
-            axis=0,
-        )
-        pred_ref[:, s * frames : (s + blocks) * frames] = nt(
-            coil_ref[:, :rows], x.astype(BF16)
+    lax.fori_loop(0, steps, frame, 0, unroll=math.gcd(steps, 32))
+    blocks = max(1, min(per, 512 // frames))
+
+    def summed(part, first):
+        at = [(part * per + first + k) * stride for k in range(blocks)]
+        halves_of = [
+            jnp.concatenate([x_ref[h, a : a + frames, :] for a in at], axis=0)
+            for h in range(x_ref.shape[0])
+        ]
+        x = jnp.concatenate(halves_of, axis=1)[:, :rows].astype(BF16)
+        return nt(coil_ref[part, :, :rows], x)
+
+    for first in range(0, per, blocks):
+        pred_ref[:, first * frames : (first + blocks) * frames] = (
+            summed(0, first) + summed(1, first)
         ).astype(BF16)
-    size = kd_ref.shape[2]
-    for part in range(2):
-        at = part * per * frames + lax.axis_index("cuts") * size
-        at = pl.ds(pl.multiple_of(at, LANES), size)
-        pred_ref[:, at] = (pred_ref[:, at].astype(F32) - kd_ref[part].astype(F32)).astype(BF16)
-
-
-def gradient_kernel(first, steps, own, frames, slab, scale, n_r, *refs):
+    size = kd_ref.shape[1]
+    at = pl.ds(pl.multiple_of(lax.axis_index("cuts") * size, LANES), size)
+    pred_ref[:, at] = (pred_ref[:, at].astype(F32) - kd_ref[...].astype(F32)).astype(BF16)
+
+
+def gradient_kernel(own, frames, slab, scale, n_r, *refs):
     r_refs, refs = refs[:n_r], refs[n_r:]
-    if n_r:
-        b_ref, m_ref, w_ref, fz_ref, coil_ref, fg_ref, gz_ref, r_ref, g_ref = refs
-    else:
-        b_ref, m_ref, w_ref, fz_ref, r_ref, fg_ref, gz_ref, g_ref = refs
+    b_ref, m_ref, w_ref, fz_ref, coil_ref, fg_ref, gz_ref, r_ref, g_ref = refs
+    steps = frames
     width = b_ref.shape[2]
     rank = b_ref.shape[1] // 2
     rows = m_ref.shape[1]
@@ -221,15 +230,15 @@
     pitch = 2 * steps + PITCH
     stride = samples_step(r_ref, frames, per)
 
-    if n_r:
-        resid = total(r_refs).astype(BF16)
-        blocks = max(1, min(8, 512 // frames))
-        for s in range(0, 2 * per, blocks):
-            r = tn(resid[:, s * frames : (s + blocks) * frames], coil_ref[...])
+    resid = total(r_refs).astype(BF16)
+    blocks = max(1, min(per, 512 // frames))
+    for part in range(2):
+        for first in range(0, per, blocks):
+            r = tn(resid[:, first * frames : (first + blocks) * frames], coil_ref[part])
             for k in range(blocks):
-                at = slice((s + k) * stride, (s + k) * stride + frames)
+                at = (part * per + first + k) * stride
                 for h in range(r_ref.shape[0]):
-                    r_ref[h, at, :] = r[
+                    r_ref[h, at : at + frames, :] = r[
                         k * frames : (k + 1) * frames, h * LANES : (h + 1) * LANES
                     ]
 
@@ -237,7 +246,7 @@
     m_im = m_ref[1].reshape(coils, slab, width)
 
     def frame(step, carry):
-        t = frame_of(first + step, own)
+        t = frame_of(step, own)
         at = pl.ds(pl.multiple_of(t * per, TILE), per)
         rhs = adjoint_pair(w_ref[at, :])
         f = fz_ref[at, :].astype(F32)
@@ -258,7 +267,7 @@
             g_ref[h, pl.ds(steps + step, slab, stride=pitch), :] = g_im[:, lanes]
         return carry
 
-    lax.fori_loop(0, steps, frame, 0, unroll=math.gcd(steps, 16))
+    lax.fori_loop(0, steps, frame, 0, unroll=math.gcd(steps, 32))
     acc = jnp.zeros((2 * steps, 2 * rank), F32)
     for z in range(slab):
         at = pl.ds(z * pitch, 2 * steps)
@@ -269,16 +278,28 @@
     fg = jnp.concatenate(
         [top[:, :rank] + bottom[:, rank:], bottom[:, :rank] - top[:, rank:]], axis=1
     )
-    fg_ref[...] = (fg * scale).reshape(fg_ref.shape)
-
-
-def basis_kernel(sent_ref, got_ref, v_ref, rest_ref, own_ref, grad_ref):
-    slab, _, width = own_ref.shape
+    fg = (fg * scale).astype(fg_ref.dtype)
+    n_cuts, n_frame, n_rows, n_lanes = fg_ref.shape
+    for d in range(n_frame):
+        piece = jnp.concatenate(
+            [
+                fg[d * own + k : d * own + k + n_rows].astype(F32)
+                for k in range(0, own, n_rows)
+            ],
+            axis=1,
+        ).astype(fg_ref.dtype)
+        target = lax.axis_index("frame") ^ d
+        for c in range(n_cuts):
+            fg_ref[c, pl.ds(target, 1)] = piece[None]
+
+
+def basis_kernel(sent_ref, got_ref, v_ref, g_ref, grad_ref):
+    slab, _, width = g_ref.shape
     mine, rest = own_and_rest(v_ref, arrived(sent_ref, got_ref)[1])
-    v_own, v_rest = factor_matrix(*mine), factor_matrix(*rest)
+    v = factor_matrix(*(jnp.concatenate(both, axis=0) for both in zip(mine, rest)))
     halves = width // LANES
     for z in range(slab):
-        grad = tn(v_own, own_ref[z]) + tn(v_rest, rest_ref[z])
+        grad = tn(v, g_ref[z])
         for h in range(halves):
             grad_ref[pl.ds(z * halves + h, grad.shape[0], stride=slab * halves), :] = grad[
                 :, h * LANES : (h + 1) * LANES
@@ -371,7 +392,6 @@
     columns = lines.shape[1]
     frames = lines.shape[0]
     own = factors.shape[2]
-    rest = frames - own
     per = columns * n_cuts
     samples = frames * per
     depth = slab * n_cuts
@@ -382,7 +402,7 @@
     coil_groups = -(-coils // spread)
     rows = coil_groups * tall
     pad = -(-rows // LANES) * LANES
-    coil_rows = -(-coils // TILE) * TILE
+    coil_rows = -(-2 * coils // 8) * 8
 
     kind = BF16 if max(width, depth) <= 256 else F32
     turned = lines.T
@@ -390,17 +410,8 @@
     owner = jnp.arange(n_cuts, dtype=jnp.int32)[None, :, None, None] == cut
     placed = jnp.where(owner, mine[:, None], 0).astype(kind).reshape(2 * per, frames)
     v_own = factors.transpose(0, 2, 1)
-    table_y = np.concatenate(dft_parts(width), axis=1).astype(np.float32)
-    table_z = np.concatenate(dft_parts(depth), axis=1).astype(np.float32)
-    lanes = max(table_y.shape[1], table_z.shape[1])
-    tables = jnp.asarray(
-        np.concatenate([np.pad(x, ((0, 0), (0, lanes - x.shape[1]))) for x in (table_y, table_z)])
-    )
     m_rows = jnp.pad(coil_maps, ((0, 0), (0, coil_groups * spread - coils), (0, 0), (0, 0)))
     m_rows = m_rows.reshape(2, rows, width)
-    kd = kdata.transpose(0, 3, 2, 1).reshape(2, coils, columns * frames)
-    kd = jnp.pad(kd, ((0, 0), (0, coil_rows - coils), (0, 0)))
-
     flops = 2 * 2 * per * rows * 2 * width * 8
     halves = width // LANES
     x_shape = jax.ShapeDtypeStruct((pad // LANES, 2 * per * (frames + PITCH), LANES), F32)
@@ -410,23 +421,33 @@
 
     def stage(packet):
         return call(
-            functools.partial(stage_kernel, slab, coils),
+            functools.partial(tables_kernel, slab, coils),
             (
                 jax.ShapeDtypeStruct((width, 2 * width), BF16),
                 jax.ShapeDtypeStruct((depth, 2 * pad), BF16),
-                jax.ShapeDtypeStruct((coil_rows, pad), BF16),
-                jax.ShapeDtypeStruct((tall, 2 * rank, width), BF16),
+                jax.ShapeDtypeStruct((2, coil_rows, pad), BF16),
             ),
-            [pltpu.VMEM((halves, 2 * rank * (-(-slab // 8) * 8 + PITCH), LANES), F32)],
-            2 * 1024 * 1024 * 1024,
-            packet, tables, basis.reshape(2 * rank, slab, width),
+            [],
+            1024 * 1024 * 1024,
+            packet,
         )
 
-    sent, got, (taby, tabz, coil_of, b_rows) = collect(placed, v_own, stage)
+    sent, got, (taby, tabz, coil_of) = collect(placed, v_own, stage)
+    (b_rows,) = call(
+        turn_kernel,
+        (jax.ShapeDtypeStruct((tall, 2 * rank, width), BF16),),
+        [pltpu.VMEM((halves, 2 * rank * (-(-slab // 8) * 8 + PITCH), LANES), F32)],
+        1024 * 1024 * 1024,
+        sent, basis.reshape(2 * rank, slab, width),
+    )
+    _, kdata = lax.optimization_barrier((sent, kdata))
+    kd = kdata.transpose(0, 3, 2, 1).reshape(2 * coils, columns * frames)
+    kd = jnp.pad(kd, ((0, coil_rows - 2 * coils), (0, 0)))
+
     predicted, w, fz = call(
         functools.partial(predict_kernel, own, frames, tall),
         (
-            jax.ShapeDtypeStruct((coil_rows, 2 * samples), BF16),
+            jax.ShapeDtypeStruct((coil_rows, samples), BF16),
             jax.ShapeDtypeStruct((samples, 2 * width), BF16),
             jax.ShapeDtypeStruct((samples, 2 * pad), BF16),
         ),
@@ -436,34 +457,27 @@
     )
     resid_terms = shares(predicted, "cuts")
 
-    def gradient(first, steps, n_r, *operands):
-        outs = [
-            jax.ShapeDtypeStruct((steps // own, own, 2 * rank), F32),
-            jax.ShapeDtypeStruct((tall, 2 * steps, width), BF16),
-        ] + ([x_shape] if n_r else [])
-        return call(
-            functools.partial(gradient_kernel, first, steps, own, frames, tall, scale, n_r),
-            tuple(outs),
-            [images(steps)],
-            flops * steps,
-            *operands,
-        )
-
-    fg_rest, g_rest, r = gradient(
-        own, rest, len(resid_terms), *resid_terms, b_rows, m_rows, w, fz, coil_of
-    )
-    others = [swap(fg_rest[d - 1], "frame", d) for d in range(1, n_frame)]
-    fg_own, g_own = gradient(0, own, 0, b_rows, m_rows, w, fz, r)
+    fold = max(1, LANES // (2 * rank))
+    pieces, g = call(
+        functools.partial(gradient_kernel, own, frames, tall, scale, len(resid_terms)),
+        (
+            jax.ShapeDtypeStruct((n_cuts, n_frame, own // fold, 2 * rank * fold), BF16),
+            jax.ShapeDtypeStruct((tall, 2 * frames, width), BF16),
+        ),
+        [pltpu.VMEM(x_shape.shape, F32), images(frames)],
+        flops * frames,
+        *resid_terms, b_rows, m_rows, w, fz, coil_of,
+    )
     (grad,) = call(
         basis_kernel,
         (jax.ShapeDtypeStruct((2 * rank * tall * halves, LANES), F32),),
         [],
         2 * 2 * rank * 2 * frames * tall * width * 8,
-        sent, got, v_own, g_rest, g_own,
+        sent, got, v_own, g,
     )
     if spread > 1:
         grad = jnp.sum(grad.reshape(2, rank, spread, slab, width), axis=2)
-    return grad.reshape(2, rank, slab, width), pairs([fg_own[0], *others])
+    return grad.reshape(2, rank, slab, width), pieces
 
 
 def pairs(terms):
@@ -487,8 +501,11 @@
         grads.append(grad)
         fg = fg + term
     basis_grad = grads[0][:, :, :, None] if readout == 1 else jnp.stack(grads, axis=3)
-    summed = pairs(shares(fg, "cuts"))
-    return basis_grad, summed.reshape(own, 2, rank).transpose(1, 2, 0)
+    pieces = fg.reshape((n_cuts * n_frame,) + fg.shape[2:])
+    arriving = lax.all_to_all(pieces, ("cuts", "frame"), 0, 0, tiled=True)
+    summed = jnp.sum(arriving.astype(F32), axis=0)
+    folded = summed.reshape(summed.shape[0], -1, 2, rank)
+    return basis_grad, folded.transpose(2, 3, 1, 0).reshape(2, rank, own)
 
 
 def solution(mesh):

time: 47.1 us -> 45.4 us (0.964)
  waiting for transfers between devices: 10 us -> 13.5 us
  starting transfers between devices: 17.1 us -> 13.9 us
  local copies, waits for them, and re-layouts: 3.86 us -> 2.73 us
  other arithmetic: 0.99 us -> 0.32 us
    ppermute x13 -> x6, starting transfers between devices: 12.7 us -> 4.59 us  [swap(): return lax.ppermute(value, axis, [(i, i ^ distance) for i in range(size)])]
    all_to_all x0 -> x1, waiting for transfers between devices: none -> 5.57 us  [body(): arriving = lax.all_to_all(pieces, ('cuts', 'frame'), 0, 0, tiled=True)]
    all_to_all x0 -> x1, starting transfers between devices: none -> 4.85 us  [body(): arriving = lax.all_to_all(pieces, ('cuts', 'frame'), 0, 0, tiled=True)]
    ppermute x13 -> x6, waiting for transfers between devices: 9.04 us -> 4.77 us  [swap(): return lax.ppermute(value, axis, [(i, i ^ distance) for i in range(size)])]
    ppermute x3, waiting for transfers between devices: 0.98 us -> 3.16 us  [collect(): got.append(lax.ppermute(packet, ('cuts', 'frame'), route))]
    pad x1, local copies, waits for them, and re-layouts: 0.7 us -> 0.01 us  [grown(): jnp.pad(value, ((0, rows - value.shape[0]), (0, lanes - value.shape[1])))]
    another operation x2, other arithmetic: 0.7 us -> 0.02 us  [one_position(): mine = jnp.stack([cut * ky_rows + turned // depth, turned % depth])]
    reshape x3 -> x2, local copies, waits for them, and re-layouts: 0.78 us -> 0.17 us  [the longest x1 0.09 us: one_position(): kd = kdata.transpose(0, 3, 2, 1).reshape(2 * coils, columns * frames)]
  transfers between devices with their start and end apart: 16 -> 10, of which waited for: 12 -> 10; matrix products, arithmetic and copies ran while one was open for 2% -> 0% of each run, Pallas kernels for 8% -> 6%
where the time goes in v4:
time: 45.4 us; the launch traced here: 45.1 us
  starting transfers between devices  13.9 us (31%)
  Pallas kernels  13.9 us (31%)
  waiting for transfers between devices  13.5 us (30%)
  local copies, waits for them, and re-layouts  2.73 us (6%)
  between operations  0.72 us (2%)
    pallas_call x5, Pallas kernels, call(): pl.pallas_call(kernel, out_shape=outs, scratch_shapes=scratch, compiler_p...  13.9 us
    all_to_all x1, waiting for transfers between devices, body(): arriving = lax.all_to_all(pieces, ('cuts', 'frame'), 0, 0, tiled=True)  5.57 us
    all_to_all x1, starting transfers between devices, body(): arriving = lax.all_to_all(pieces, ('cuts', 'frame'), 0, 0, tiled=True)  4.85 us
    ppermute x6, waiting for transfers between devices, swap(): return lax.ppermute(value, axis, [(i, i ^ distance) for i in range(size)])  4.77 us
    ppermute x6, starting transfers between devices, swap(): return lax.ppermute(value, axis, [(i, i ^ distance) for i in range(size)])  4.59 us
    ppermute x3, starting transfers between devices, collect(): got.append(lax.ppermute(packet, ('cuts', 'frame'), route))  4.49 us
    ppermute x3, waiting for transfers between devices, collect(): got.append(lax.ppermute(packet, ('cuts', 'frame'), route))  3.16 us
    unnamed x10, local copies, waits for them, and re-layouts  1.78 us
  transfers between devices with their start and end apart: 10, of which 10 were waited for; matrix products, arithmetic and copies ran while one was open for 0% of the time, Pallas kernels for 6%

profile of v4, /device:TPU:0, one launch (start us, length us, event | category | flops | bytes accessed | tf_op | source)
XLA Modules:
  0.0 45.1 jit_solution(1438021701549131296)
XLA Ops:
  0.6 0.1 broadcast_in_dim.28
  0.7 0.0 copy-start.4
  0.7 0.1 broadcast_in_dim.29
  0.8 0.6 %copy-done.4 = s32[64,2]{0,1:T(2,128)S(1)} copy-done((s32[64,2]{0,1:T(2,128)S(1)}, s32[64,2]{0,1:T(2,128)}, u32[]{:S(2)}) %copy-start.4) | copy-done | bytes 536
  1.4 0.1 select_convert_fusion
  1.5 0.5 %collective-permute-start = (bf16[32,64]{1,0:T(8,128)(2,1)S(1)}, bf16[32,64]{1,0:T(8,128)(2,1)S(1)}, u32[]{:S(2)}, u32[]{:S(2)}) collective-permute-start(bf16[32,64]{1,0:T(8,128)(2,1)S(1)} %select_convert_fusion), channel_id=1, source_target_pairs={{0,4},{4,0},{8,12},{12,8},{16,20},{20,16},{24,28},{28,24},{1,5},{5... | collective-permute-start | bytes 12296 | tf_op jit(solution)/shard_map/ppermute | solution.py:322
  2.0 0.0 copy-start
  2.0 0.7 %copy-done = bf16[2,32,16]{1,2,0:T(8,128)(2,1)S(1)} copy-done((bf16[2,32,16]{1,2,0:T(8,128)(2,1)S(1)}, bf16[2,32,16]{1,2,0:T(8,128)(2,1)}, u32[]{:S(2)}) %copy-start) | copy-done | bytes 2072
  2.7 0.1 collective-permute-done
  2.8 0.1 add_convert_fusion.2
  2.9 0.0 copy-start.1
  2.9 3.9 %collective-permute-start.3 = (bf16[32,64]{1,0:T(8,128)(2,1)S(1)}, bf16[32,64]{1,0:T(8,128)(2,1)S(1)}, u32[]{:S(2)}, u32[]{:S(2)}) collective-permute-start(bf16[32,64]{1,0:T(8,128)(2,1)S(1)} %broadcast_select_fusion.after_ref), channel_id=1, source_target_pairs={{0,24},{1,25},{2,26},{3,27},{4,7},{5,6},{6,5},{7,4},{8,16},{9,17},... | collective-permute-start | bytes 12296 | tf_op jit(solution)/shard_map/ppermute | solution.py:360
  6.8 0.5 %collective-permute-start.2 = (bf16[32,64]{1,0:T(8,128)(2,1)S(1)}, bf16[32,64]{1,0:T(8,128)(2,1)S(1)}, u32[]{:S(2)}, u32[]{:S(2)}) collective-permute-start(bf16[32,64]{1,0:T(8,128)(2,1)S(1)} %broadcast_select_fusion.after_ref), channel_id=1, source_target_pairs={{0,16},{1,17},{2,18},{3,19},{4,6},{5,7},{6,4},{7,5},{8,24},{9,25},... | collective-permute-start | bytes 12296 | tf_op jit(solution)/shard_map/ppermute | solution.py:360
  7.3 0.1 collective-permute-start.1
  7.4 0.4 shard_map.68
  7.7 0.6 %collective-permute-done.3 = bf16[32,64]{1,0:T(8,128)(2,1)S(1)} collective-permute-done((bf16[32,64]{1,0:T(8,128)(2,1)S(1)}, bf16[32,64]{1,0:T(8,128)(2,1)S(1)}, u32[]{:S(2)}, u32[]{:S(2)}) %collective-permute-start.3) | collective-permute-done | bytes 4128 | tf_op jit(solution)/shard_map/ppermute | solution.py:360
  8.4 2.0 %collective-permute-done.2 = bf16[32,64]{1,0:T(8,128)(2,1)S(1)} collective-permute-done((bf16[32,64]{1,0:T(8,128)(2,1)S(1)}, bf16[32,64]{1,0:T(8,128)(2,1)S(1)}, u32[]{:S(2)}, u32[]{:S(2)}) %collective-permute-start.2) | collective-permute-done | bytes 4128 | tf_op jit(solution)/shard_map/ppermute | solution.py:360
  10.4 0.5 %collective-permute-done.1 = bf16[32,64]{1,0:T(8,128)(2,1)S(1)} collective-permute-done((bf16[32,64]{1,0:T(8,128)(2,1)S(1)}, bf16[32,64]{1,0:T(8,128)(2,1)S(1)}, u32[]{:S(2)}, u32[]{:S(2)}) %collective-permute-start.1) | collective-permute-done | bytes 4128 | tf_op jit(solution)/shard_map/ppermute | solution.py:360
  10.9 0.1 maximum_select_fusion.after_ref.refs_0_.sent_ref
  11.0 0.3 collective-permute-start.4
  11.3 0.0 copy-done.1
  11.3 0.0 copy-start.3
  11.3 0.0 copy-start.2
  11.3 0.3 shard_map.69.refs_6_.refs_4_
  11.6 0.4 copy-done.3
  12.0 0.1 reshape.34.refs_8_
  12.1 0.1 collective-permute-done.4.refs_1_.got_ref
  12.2 0.1 copy-done.2
  12.2 5.8 %shard_map.70 = (bf16[24,1024]{1,0:T(8,128)(2,1)S(1)}, bf16[1024,512]{1,0:T(8,128)(2,1)S(1)}, bf16[1024,512]{1,0:T(8,128)(2,1)S(1)}) custom-call(bf16[32,96]{1,0:T(8,128)(2,1)S(1)} %maximum_select_fusion.after_ref.refs_0_.sent_ref, bf16[32,96]{1,0:T(8,128)(2,1)S(1)} %collective-permute-done.4.refs_1_.got_ref, bf16[2,16,32]{2,1,0:T(8,128)(2,1)S(1)} %bitcast.44, ...), custom_call_target="tpu_custom_call" | custom-call | flops 3221225472 | bytes 1179648 | tf_op jit(solution)/shard_map/pallas_call | solution.py:378
  18.1 0.3 collective-permute-start.5
  18.3 1.0 %collective-permute-done.5 = bf16[24,1024]{1,0:T(8,128)(2,1)S(1)} collective-permute-done((bf16[24,1024]{1,0:T(8,128)(2,1)S(1)}, bf16[24,1024]{1,0:T(8,128)(2,1)S(1)}, u32[]{:S(2)}, u32[]{:S(2)}) %collective-permute-start.5) | collective-permute-done | bytes 49184 | tf_op jit(solution)/shard_map/ppermute | solution.py:322
  19.4 2.5 %collective-permute-start.8 = (bf16[24,1024]{1,0:T(8,128)(2,1)S(1)}, bf16[24,1024]{1,0:T(8,128)(2,1)S(1)}, u32[]{:S(2)}, u32[]{:S(2)}) collective-permute-start(bf16[24,1024]{1,0:T(8,128)(2,1)S(1)} %add_convert_fusion.refs_0_), channel_id=1, source_target_pairs={{0,24},{4,28},{8,16},{12,20},{16,8},{20,12},{24,0},{28,4},{1,25},{... | collective-permute-start | bytes 147464 | tf_op jit(solution)/shard_map/ppermute | solution.py:322
  21.9 0.5 %collective-permute-start.7 = (bf16[24,1024]{1,0:T(8,128)(2,1)S(1)}, bf16[24,1024]{1,0:T(8,128)(2,1)S(1)}, u32[]{:S(2)}, u32[]{:S(2)}) collective-permute-start(bf16[24,1024]{1,0:T(8,128)(2,1)S(1)} %add_convert_fusion.refs_0_), channel_id=1, source_target_pairs={{0,16},{4,20},{8,24},{12,28},{16,0},{20,4},{24,8},{28,12},{1,17},{... | collective-permute-start | bytes 147464 | tf_op jit(solution)/shard_map/ppermute | solution.py:322
  22.4 0.6 %collective-permute-start.6 = (bf16[24,1024]{1,0:T(8,128)(2,1)S(1)}, bf16[24,1024]{1,0:T(8,128)(2,1)S(1)}, u32[]{:S(2)}, u32[]{:S(2)}) collective-permute-start(bf16[24,1024]{1,0:T(8,128)(2,1)S(1)} %add_convert_fusion.refs_0_), channel_id=1, source_target_pairs={{0,8},{4,12},{8,0},{12,4},{16,24},{20,28},{24,16},{28,20},{1,9},{5... | collective-permute-start | bytes 147464 | tf_op jit(solution)/shard_map/ppermute | solution.py:322
  22.9 1.5 %collective-permute-done.8.refs_3_ = bf16[24,1024]{1,0:T(8,128)(2,1)S(1)} collective-permute-done((bf16[24,1024]{1,0:T(8,128)(2,1)S(1)}, bf16[24,1024]{1,0:T(8,128)(2,1)S(1)}, u32[]{:S(2)}, u32[]{:S(2)}) %collective-permute-start.8) | collective-permute-done | bytes 49184 | tf_op jit(solution)/shard_map/ppermute | solution.py:322
  24.4 1.5 %collective-permute-done.7.refs_2_ = bf16[24,1024]{1,0:T(8,128)(2,1)S(1)} collective-permute-done((bf16[24,1024]{1,0:T(8,128)(2,1)S(1)}, bf16[24,1024]{1,0:T(8,128)(2,1)S(1)}, u32[]{:S(2)}, u32[]{:S(2)}) %collective-permute-start.7) | collective-permute-done | bytes 49184 | tf_op jit(solution)/shard_map/ppermute | solution.py:322
  25.9 0.5 %collective-permute-done.6.refs_1_ = bf16[24,1024]{1,0:T(8,128)(2,1)S(1)} collective-permute-done((bf16[24,1024]{1,0:T(8,128)(2,1)S(1)}, bf16[24,1024]{1,0:T(8,128)(2,1)S(1)}, u32[]{:S(2)}, u32[]{:S(2)}) %collective-permute-start.6) | collective-permute-done | bytes 49184 | tf_op jit(solution)/shard_map/ppermute | solution.py:322
  26.5 5.5 %shard_map.71 = (bf16[8,4,8,128]{3,2,1,0:T(8,128)(2,1)}, bf16[16,128,256]{2,1,0:T(8,128)(2,1)S(1)}) custom-call(bf16[24,1024]{1,0:T(8,128)(2,1)S(1)} %add_convert_fusion.refs_0_, bf16[24,1024]{1,0:T(8,128)(2,1)S(1)} %collective-permute-done.6.refs_1_, bf16[24,1024]{1,0:T(8,128)(2,1)S(1)} %collective-permute-done.7.refs_2_, ...), custom_call_target="tpu_custom_call" | custom-call | flops 3221225472 | bytes 3112960 | tf_op jit(solution)/shard_map/pallas_call | solution.py:378
  32.0 4.8 %all-to-all-start = ((bf16[32,8,128]{2,1,0:T(8,128)(2,1)}), bf16[32,8,128]{2,1,0:T(8,128)(2,1)S(1)}, u32[]{:S(2)}, u32[]{:S(2)}) async-start(bf16[32,8,128]{2,1,0:T(8,128)(2,1)} %bitcast.11), calls=%async_computation | async-start | bytes 131072 | tf_op jit(solution)/shard_map/all_to_all | solution.py:505
  36.9 1.9 %shard_map.72 = f32[2048,128]{1,0:T(8,128)} custom-call(bf16[32,96]{1,0:T(8,128)(2,1)S(1)} %maximum_select_fusion.after_ref.refs_0_.sent_ref, bf16[32,96]{1,0:T(8,128)(2,1)S(1)} %collective-permute-done.4.refs_1_.got_ref, bf16[2,16,32]{2,1,0:T(8,128)(2,1)S(1)} %bitcast.45, bf16[16,128,256]{2,1,0:T(8,128)(2,1)S(1)} %get-tuple-element.34.g_ref), custom_call_target="tpu_custom_call" | custom-call | flops 536870912 | bytes 1073152 | tf_op jit(solution)/shard_map/pallas_call | solution.py:378
  38.8 5.6 %all-to-all-done = bf16[32,8,128]{2,1,0:T(8,128)(2,1)S(1)} async-done(((bf16[32,8,128]{2,1,0:T(8,128)(2,1)}), bf16[32,8,128]{2,1,0:T(8,128)(2,1)S(1)}, u32[]{:S(2)}, u32[]{:S(2)}) %all-to-all-start) | async-done | bytes 65568 | tf_op jit(solution)/shard_map/all_to_all | solution.py:505
  44.4 0.1 reshape.36
  44.5 0.6 %copy.12 = f32[2,32,2,8]{1,3,2,0:T(8,128)} copy(f32[2,32,2,8]{1,0,2,3:T(2,128)S(1)} %bitcast.52) | data formatting | bytes 8192 | tf_op jit(solution)/shard_map/transpose | solution.py:508
  (9 shorter events, 0.1 us)
Async XLA Ops:
  0.7 0.7 %copy-start.4 = (s32[64,2]{0,1:T(2,128)S(1)}, s32[64,2]{0,1:T(2,128)}, u32[]{:S(2)}) copy-start(s32[64,2]{0,1:T(2,128)} %param.8) | copy-start | bytes 1540
  1.5 1.3 %collective-permute-start = (bf16[32,64]{1,0:T(8,128)(2,1)S(1)}, bf16[32,64]{1,0:T(8,128)(2,1)S(1)}, u32[]{:S(2)}, u32[]{:S(2)}) collective-permute-start(bf16[32,64]{1,0:T(8,128)(2,1)S(1)} %select_convert_fusion), channel_id=1, source_target_pairs={{0,4},{4,0},{8,12},{12,8},{16,20},{20,16},{24,28},{28,24},{1,5},{5... | collective-permute-start | bytes 12296 | tf_op jit(solution)/shard_map/ppermute | solution.py:322
  2.0 0.7 %copy-start = (bf16[2,32,16]{1,2,0:T(8,128)(2,1)S(1)}, bf16[2,32,16]{1,2,0:T(8,128)(2,1)}, u32[]{:S(2)}) copy-start(bf16[2,32,16]{1,2,0:T(8,128)(2,1)} %param.7) | copy-start | bytes 6148
  2.9 8.4 %copy-start.1 = (bf16[2,32,16,1,256]{4,2,3,1,0:T(8,128)(2,1)S(1)}, bf16[2,32,16,1,256]{4,2,3,1,0:T(8,128)(2,1)}, u32[]{:S(2)}) copy-start(bf16[2,32,16,1,256]{4,2,3,1,0:T(8,128)(2,1)} %param.5) | copy-start | bytes 1572868
  2.9 5.5 %collective-permute-start.3 = (bf16[32,64]{1,0:T(8,128)(2,1)S(1)}, bf16[32,64]{1,0:T(8,128)(2,1)S(1)}, u32[]{:S(2)}, u32[]{:S(2)}) collective-permute-start(bf16[32,64]{1,0:T(8,128)(2,1)S(1)} %broadcast_select_fusion.after_ref), channel_id=1, source_target_pairs={{0,24},{1,25},{2,26},{3,27},{4,7},{5,6},{6,5},{7,4},{8,16},{9,17},... | collective-permute-start | bytes 12296 | tf_op jit(solution)/shard_map/ppermute | solution.py:360
  6.8 3.7 %collective-permute-start.2 = (bf16[32,64]{1,0:T(8,128)(2,1)S(1)}, bf16[32,64]{1,0:T(8,128)(2,1)S(1)}, u32[]{:S(2)}, u32[]{:S(2)}) collective-permute-start(bf16[32,64]{1,0:T(8,128)(2,1)S(1)} %broadcast_select_fusion.after_ref), channel_id=1, source_target_pairs={{0,16},{1,17},{2,18},{3,19},{4,6},{5,7},{6,4},{7,5},{8,24},{9,25},... | collective-permute-start | bytes 12296 | tf_op jit(solution)/shard_map/ppermute | solution.py:360
  7.3 3.7 %collective-permute-start.1 = (bf16[32,64]{1,0:T(8,128)(2,1)S(1)}, bf16[32,64]{1,0:T(8,128)(2,1)S(1)}, u32[]{:S(2)}, u32[]{:S(2)}) collective-permute-start(bf16[32,64]{1,0:T(8,128)(2,1)S(1)} %broadcast_select_fusion.after_ref), channel_id=1, source_target_pairs={{0,8},{1,9},{2,10},{3,11},{4,5},{5,4},{6,7},{7,6},{8,0},{9,1},{10,... | collective-permute-start | bytes 12296 | tf_op jit(solution)/shard_map/ppermute | solution.py:360
  11.0 1.2 %collective-permute-start.4 = (bf16[32,96]{1,0:T(8,128)(2,1)S(1)}, bf16[32,96]{1,0:T(8,128)(2,1)S(1)}, u32[]{:S(2)}, u32[]{:S(2)}) collective-permute-start(bf16[32,96]{1,0:T(8,128)(2,1)S(1)} %maximum_select_fusion.after_ref.refs_0_.sent_ref), channel_id=1, source_target_pairs={{0,4},{4,0},{8,12},{12,8},{16,20},{20,16},{24,28},{28,24},{1,5},{5... | collective-permute-start | bytes 18440 | tf_op jit(solution)/shard_map/ppermute | solution.py:322
  11.3 0.7 %copy-start.3 = (bf16[2,64,2,12,1]{1,2,4,3,0:T(2,128)(2,1)S(1)}, bf16[2,64,2,12,1]{1,2,4,3,0:T(2,128)(2,1)}, u32[]{:S(2)}) copy-start(bf16[2,64,2,12,1]{1,2,4,3,0:T(2,128)(2,1)} %param.9) | copy-start | bytes 18436
  11.3 0.9 %copy-start.2 = (bf16[2,12,16,1,256]{4,2,3,1,0:T(8,128)(2,1)S(1)}, bf16[2,12,16,1,256]{4,2,3,1,0:T(8,128)(2,1)}, u32[]{:S(2)}) copy-start(bf16[2,12,16,1,256]{4,2,3,1,0:T(8,128)(2,1)} %param.6) | copy-start | bytes 589828
  18.1 1.3 %collective-permute-start.5 = (bf16[24,1024]{1,0:T(8,128)(2,1)S(1)}, bf16[24,1024]{1,0:T(8,128)(2,1)S(1)}, u32[]{:S(2)}, u32[]{:S(2)}) collective-permute-start(bf16[24,1024]{1,0:T(8,128)(2,1)S(1)} %get-tuple-element.31), channel_id=1, source_target_pairs={{0,4},{4,0},{8,12},{12,8},{16,20},{20,16},{24,28},{28,24},{1,5},{5... | collective-permute-start | bytes 147464 | tf_op jit(solution)/shard_map/ppermute | solution.py:322
  19.4 5.1 %collective-permute-start.8 = (bf16[24,1024]{1,0:T(8,128)(2,1)S(1)}, bf16[24,1024]{1,0:T(8,128)(2,1)S(1)}, u32[]{:S(2)}, u32[]{:S(2)}) collective-permute-start(bf16[24,1024]{1,0:T(8,128)(2,1)S(1)} %add_convert_fusion.refs_0_), channel_id=1, source_target_pairs={{0,24},{4,28},{8,16},{12,20},{16,8},{20,12},{24,0},{28,4},{1,25},{... | collective-permute-start | bytes 147464 | tf_op jit(solution)/shard_map/ppermute | solution.py:322
  21.9 4.1 %collective-permute-start.7 = (bf16[24,1024]{1,0:T(8,128)(2,1)S(1)}, bf16[24,1024]{1,0:T(8,128)(2,1)S(1)}, u32[]{:S(2)}, u32[]{:S(2)}) collective-permute-start(bf16[24,1024]{1,0:T(8,128)(2,1)S(1)} %add_convert_fusion.refs_0_), channel_id=1, source_target_pairs={{0,16},{4,20},{8,24},{12,28},{16,0},{20,4},{24,8},{28,12},{1,17},{... | collective-permute-start | bytes 147464 | tf_op jit(solution)/shard_map/ppermute | solution.py:322
  22.4 4.1 %collective-permute-start.6 = (bf16[24,1024]{1,0:T(8,128)(2,1)S(1)}, bf16[24,1024]{1,0:T(8,128)(2,1)S(1)}, u32[]{:S(2)}, u32[]{:S(2)}) collective-permute-start(bf16[24,1024]{1,0:T(8,128)(2,1)S(1)} %add_convert_fusion.refs_0_), channel_id=1, source_target_pairs={{0,8},{4,12},{8,0},{12,4},{16,24},{20,28},{24,16},{28,20},{1,9},{5... | collective-permute-start | bytes 147464 | tf_op jit(solution)/shard_map/ppermute | solution.py:322
  32.0 12.4 %all-to-all-start = ((bf16[32,8,128]{2,1,0:T(8,128)(2,1)}), bf16[32,8,128]{2,1,0:T(8,128)(2,1)S(1)}, u32[]{:S(2)}, u32[]{:S(2)}) async-start(bf16[32,8,128]{2,1,0:T(8,128)(2,1)} %bitcast.11), calls=%async_computation | async-start | bytes 131072 | tf_op jit(solution)/shard_map/all_to_all | solution.py:505

commit v5 on v4

--- a/solution.py
+++ b/solution.py
@@ -58,7 +58,7 @@
 
 def arrived(sent_ref, got_ref):
     sent, got = sent_ref[...].astype(F32), got_ref[...].astype(F32)
-    even = lax.axis_index("cuts") % 2 == 0
+    even = in_pair()[1] == 0
     return jnp.where(even, sent, got), jnp.where(even, got, sent)
 
 
@@ -68,15 +68,19 @@
     return jnp.concatenate([top, bottom], axis=0).astype(BF16)
 
 
-def own_and_rest(v_ref, others):
+def half_factors(v_ref, others, place):
     _, own, rank = v_ref.shape
+    half = own // 2
     v = v_ref[...].astype(F32)
-    starts = range(0, rank * (lax.axis_size("frame") - 1), rank)
-    rest = [
-        jnp.concatenate([others[p * own : (p + 1) * own, a : a + rank] for a in starts], axis=0)
+    blocks = [(v[0], v[1])]
+    for a in range(0, rank * (lax.axis_size("frame") - 1), rank):
+        blocks.append((others[:own, a : a + rank], others[own : 2 * own, a : a + rank]))
+    return [
+        jnp.concatenate(
+            [jnp.where(place == 0, b[p][:half], b[p][half:]) for b in blocks], axis=0
+        )
         for p in range(2)
     ]
-    return (v[0], v[1]), rest
 
 
 def adjoint_pair(w):
@@ -92,6 +96,10 @@
     return terms[0].astype(F32)
 
 
+def in_pair():
+    return lax.axis_index("cuts") // 2, lax.axis_index("cuts") % 2
+
+
 def frame_of(step, own):
     return ((step // own) ^ lax.axis_index("frame")) * own + step % own
 
@@ -101,7 +109,7 @@
     width, depth, pad = taby_ref.shape[0], tabz_ref.shape[0], coil_ref.shape[2]
     write_dft(taby_ref, width, lax.broadcasted_iota(jnp.int32, (max(TILE, width // TILE), width), 1))
     slice_of = lax.broadcasted_iota(jnp.int32, (max(TILE, depth // TILE), pad), 1) % real
-    write_dft(tabz_ref, depth, slice_of + lax.axis_index("cuts") * real)
+    write_dft(tabz_ref, depth, slice_of + in_pair()[0] * real)
     column = lax.broadcasted_iota(jnp.int32, coil_ref.shape[1:], 1) // real
     row = lax.broadcasted_iota(jnp.int32, coil_ref.shape[1:], 0)
     for part in range(2):
@@ -109,22 +117,37 @@
         coil_ref[part] = place.astype(F32).astype(BF16)
 
 
-def turn_kernel(after_ref, b_ref, b_out, turn_ref):
+def turn_kernel(after_ref, b_ref, b_got_ref, m_ref, m_got_ref, b_out, m_out, turn_ref):
     del after_ref
     images, slab, width = b_ref.shape
     pitch = turn_ref.shape[1] // images
-    for h in range(width // LANES):
-        lanes = slice(h * LANES, (h + 1) * LANES)
-        for n in range(images):
-            turn_ref[h, n * pitch : n * pitch + slab, :] = b_ref[n, :, lanes].astype(F32)
-        for z in range(slab):
-            rows = turn_ref[h, pl.ds(z, images, stride=pitch), :].astype(BF16)
-            for k in range(z, b_out.shape[0], slab):
-                b_out[k, :, lanes] = rows
+    first = in_pair()[1] == 0
+    for n, ref in enumerate((b_ref, b_got_ref)):
+        start = jnp.where(first, n, 1 - n) * slab
+        for h in range(width // LANES):
+            lanes = slice(h * LANES, (h + 1) * LANES)
+            for k in range(images):
+                turn_ref[h, k * pitch : k * pitch + slab, :] = ref[k, :, lanes].astype(F32)
+            for z in range(slab):
+                rows = turn_ref[h, pl.ds(z, images, stride=pitch), :].astype(BF16)
+                for k in range(0, b_out.shape[0], 2 * slab):
+                    b_out[pl.ds(start + z + k, 1), :, lanes] = rows[None]
+    mine, got = m_ref[...].astype(F32), m_got_ref[...].astype(F32)
+    both = [jnp.where(first, mine, got), jnp.where(first, got, mine)]
+    m_out[...] = jnp.concatenate(both, axis=2).astype(BF16)
 
 
 def write_tables(pos, taby_ref, tabz_ref, w_ref, fz_ref):
-    per, frames = pos.shape[0] // 2, pos.shape[1]
+    per, own = pos.shape[0] // 2, pos.shape[1] // lax.axis_size("frame")
+    half = own // 2
+    first_half = in_pair()[1] == 0
+    frames = pos.shape[1] // 2
+
+    def column(row, u):
+        t = u // half * own + u % half
+        rows = slice(row, row + per)
+        return jnp.where(first_half, pos[rows, t : t + 1], pos[rows, t + half : t + half + 1])
+
     at_y = lax.broadcasted_iota(jnp.int32, (per, taby_ref.shape[0]), 1).astype(F32)
     at_z = lax.broadcasted_iota(jnp.int32, (per, tabz_ref.shape[0]), 1).astype(F32)
     group = max(1, 128 // per)
@@ -132,7 +155,7 @@
         hot_y, hot_z = (
             jnp.concatenate(
                 [
-                    jnp.where(iota == pos[first : first + per, t : t + 1], 1.0, 0.0)
+                    jnp.where(iota == column(first, t), 1.0, 0.0)
                     for t in range(g, g + group)
                 ],
                 axis=0,
@@ -162,9 +185,8 @@
     stride = samples_step(x_ref, frames, per)
 
     pos, others = arrived(sent_ref, got_ref)
-    write_tables(pos[: 2 * per, :frames], taby_ref, tabz_ref, w_ref, fz_ref)
-    mine, rest = own_and_rest(v_ref, others)
-    v = factor_matrix(*(jnp.concatenate(both, axis=0) for both in zip(mine, rest)))
+    write_tables(pos[: 2 * per, : 2 * frames], taby_ref, tabz_ref, w_ref, fz_ref)
+    v = factor_matrix(*half_factors(v_ref, others, in_pair()[1]))
     for z in range(slab):
         image = nn(v, b_ref[z])
         for h in range(halves):
@@ -195,7 +217,7 @@
             x_ref[h, pl.ds(t, 2 * per, stride=stride), :lanes] = x[:, h * LANES : h * LANES + lanes]
         return carry
 
-    lax.fori_loop(0, steps, frame, 0, unroll=math.gcd(steps, 32))
+    lax.fori_loop(0, steps, frame, 0, unroll=math.gcd(steps, 16))
     blocks = max(1, min(per, 512 // frames))
 
     def summed(part, first):
@@ -212,13 +234,13 @@
             summed(0, first) + summed(1, first)
         ).astype(BF16)
     size = kd_ref.shape[1]
-    at = pl.ds(pl.multiple_of(lax.axis_index("cuts") * size, LANES), size)
+    at = pl.ds(pl.multiple_of(in_pair()[0] * size, LANES), size)
     pred_ref[:, at] = (pred_ref[:, at].astype(F32) - kd_ref[...].astype(F32)).astype(BF16)
 
 
-def gradient_kernel(own, frames, slab, scale, n_r, *refs):
+def gradient_kernel(own, frames, slab, real, scale, n_r, *refs):
     r_refs, refs = refs[:n_r], refs[n_r:]
-    b_ref, m_ref, w_ref, fz_ref, coil_ref, fg_ref, gz_ref, r_ref, g_ref = refs
+    b_ref, m_ref, w_ref, fz_ref, coil_ref, fg_ref, mine_ref, theirs_ref, r_ref, g_ref = refs
     steps = frames
     width = b_ref.shape[2]
     rank = b_ref.shape[1] // 2
@@ -267,13 +289,15 @@
             g_ref[h, pl.ds(steps + step, slab, stride=pitch), :] = g_im[:, lanes]
         return carry
 
-    lax.fori_loop(0, steps, frame, 0, unroll=math.gcd(steps, 32))
+    lax.fori_loop(0, steps, frame, 0, unroll=math.gcd(steps, 16))
     acc = jnp.zeros((2 * steps, 2 * rank), F32)
-    for z in range(slab):
-        at = pl.ds(z * pitch, 2 * steps)
-        g = jnp.concatenate([g_ref[h, at, :] for h in range(halves)], axis=1).astype(BF16)
-        gz_ref[z] = g
-        acc = acc + nt(g, b_ref[z])
+    for ref, place in ((mine_ref, in_pair()[1]), (theirs_ref, 1 - in_pair()[1])):
+        for n in range(ref.shape[0]):
+            z = n // real * 2 * real + place * real + n % real
+            at = pl.ds(pl.multiple_of(z * pitch, 8), 2 * steps)
+            g = jnp.concatenate([g_ref[h, at, :] for h in range(halves)], axis=1).astype(BF16)
+            ref[n] = g
+            acc = acc + nt(g, b_ref[pl.ds(z, 1)][0])
     top, bottom = acc[:steps], acc[steps:]
     fg = jnp.concatenate(
         [top[:, :rank] + bottom[:, rank:], bottom[:, :rank] - top[:, rank:]], axis=1
@@ -293,13 +317,20 @@
             fg_ref[c, pl.ds(target, 1)] = piece[None]
 
 
-def basis_kernel(sent_ref, got_ref, v_ref, g_ref, grad_ref):
-    slab, _, width = g_ref.shape
-    mine, rest = own_and_rest(v_ref, arrived(sent_ref, got_ref)[1])
-    v = factor_matrix(*(jnp.concatenate(both, axis=0) for both in zip(mine, rest)))
-    halves = width // LANES
+def basis_kernel(sent_ref, got_ref, v_ref, g_ref, g_got_ref, grad_ref):
+    _, others = arrived(sent_ref, got_ref)
+    place = in_pair()[1]
+    pairs_of = [
+        (factor_matrix(*half_factors(v_ref, others, place)), g_ref),
+        (factor_matrix(*half_factors(v_ref, others, 1 - place)), g_got_ref),
+    ]
+    halves = g_ref.shape[2] // LANES
+    slab = grad_ref.shape[0] // (2 * v_ref.shape[2] * halves)
     for z in range(slab):
-        grad = tn(v, g_ref[z])
+        grad = functools.reduce(
+            jnp.add,
+            [tn(v, ref[k]) for v, ref in pairs_of for k in range(z, g_ref.shape[0], slab)],
+        )
         for h in range(halves):
             grad_ref[pl.ds(z * halves + h, grad.shape[0], stride=slab * halves), :] = grad[
                 :, h * LANES : (h + 1) * LANES
@@ -322,8 +353,8 @@
     return lax.ppermute(value, axis, [(i, i ^ distance) for i in range(size)])
 
 
-def shares(value, axis, last=1):
-    steps = stages(lax.axis_size(axis))
+def shares(value, axis, last=1, skip=0):
+    steps = stages(lax.axis_size(axis))[skip:]
     for number, (stride, radix) in enumerate(steps):
         if number + last == len(steps) + 1:
             return value
@@ -390,15 +421,15 @@
     rank, slab, width = basis.shape[1:]
     coils = coil_maps.shape[1]
     columns = lines.shape[1]
-    frames = lines.shape[0]
-    own = factors.shape[2]
+    half = factors.shape[2] // 2
+    frames = lines.shape[0] // 2
     per = columns * n_cuts
     samples = frames * per
     depth = slab * n_cuts
     ky_rows = width // n_cuts
 
-    spread = max(1, TILE // slab)
-    tall = spread * slab
+    spread = max(1, TILE // (2 * slab))
+    tall = spread * 2 * slab
     coil_groups = -(-coils // spread)
     rows = coil_groups * tall
     pad = -(-rows // LANES) * LANES
@@ -407,11 +438,13 @@
     kind = BF16 if max(width, depth) <= 256 else F32
     turned = lines.T
     mine = jnp.stack([cut * ky_rows + turned // depth, turned % depth])
-    owner = jnp.arange(n_cuts, dtype=jnp.int32)[None, :, None, None] == cut
-    placed = jnp.where(owner, mine[:, None], 0).astype(kind).reshape(2 * per, frames)
+    owner = lax.broadcasted_iota(jnp.int32, (2 * per, 2 * frames), 0) // columns % n_cuts == cut
+    every = jnp.broadcast_to(mine[:, None], (2, n_cuts, columns, 2 * frames))
+    placed = jnp.where(owner, every.reshape(2 * per, 2 * frames), 0).astype(kind)
     v_own = factors.transpose(0, 2, 1)
-    m_rows = jnp.pad(coil_maps, ((0, 0), (0, coil_groups * spread - coils), (0, 0), (0, 0)))
-    m_rows = m_rows.reshape(2, rows, width)
+    maps = jnp.pad(coil_maps, ((0, 0), (0, coil_groups * spread - coils), (0, 0), (0, 0)))
+    images_in = basis.reshape(2 * rank, slab, width)
+
     flops = 2 * 2 * per * rows * 2 * width * 8
     halves = width // LANES
     x_shape = jax.ShapeDtypeStruct((pad // LANES, 2 * per * (frames + PITCH), LANES), F32)
@@ -419,9 +452,12 @@
     def images(steps):
         return pltpu.VMEM((halves, tall * (2 * steps + PITCH), LANES), F32)
 
+    _, b, m, k = lax.optimization_barrier((placed, images_in, maps, kdata))
+    b_got, m_got, k_got = (swap(x, "cuts", 1) for x in (b, m, k))
+
     def stage(packet):
-        return call(
-            functools.partial(tables_kernel, slab, coils),
+        tables = call(
+            functools.partial(tables_kernel, 2 * slab, coils),
             (
                 jax.ShapeDtypeStruct((width, 2 * width), BF16),
                 jax.ShapeDtypeStruct((depth, 2 * pad), BF16),
@@ -429,23 +465,30 @@
             ),
             [],
             1024 * 1024 * 1024,
-            packet,
-        )
-
-    sent, got, (taby, tabz, coil_of) = collect(placed, v_own, stage)
-    (b_rows,) = call(
-        turn_kernel,
-        (jax.ShapeDtypeStruct((tall, 2 * rank, width), BF16),),
-        [pltpu.VMEM((halves, 2 * rank * (-(-slab // 8) * 8 + PITCH), LANES), F32)],
-        1024 * 1024 * 1024,
-        sent, basis.reshape(2 * rank, slab, width),
-    )
-    _, kdata = lax.optimization_barrier((sent, kdata))
-    kd = kdata.transpose(0, 3, 2, 1).reshape(2 * coils, columns * frames)
+            b_got,
+        )
+        turned = call(
+            turn_kernel,
+            (
+                jax.ShapeDtypeStruct((tall, 2 * rank, width), BF16),
+                jax.ShapeDtypeStruct((2, maps.shape[1], 2 * slab, width), BF16),
+            ),
+            [pltpu.VMEM((halves, 2 * rank * (-(-slab // 8) * 8 + PITCH), LANES), F32)],
+            1024 * 1024 * 1024,
+            packet, images_in, b_got, maps, m_got,
+        )
+        return tables, turned
+
+    sent, got, ((taby, tabz, coil_of), (b_rows, m_rows)) = collect(placed, v_own, stage)
+    m_rows = m_rows.reshape(2, rows, width)
+    even = lax.axis_index("cuts") % 2 == 0
+    _, mine, k_got = lax.optimization_barrier((sent, kdata, k_got))
+    both = jnp.stack([jnp.where(even, mine, k_got), jnp.where(even, k_got, mine)])
+    both = both.transpose(1, 4, 0, 3, 2).reshape(2 * coils, 2 * columns, n_frame, 2, half)
+    kd = jnp.where(even, both[..., 0, :], both[..., 1, :]).reshape(2 * coils, -1)
     kd = jnp.pad(kd, ((0, coil_rows - 2 * coils), (0, 0)))
-
     predicted, w, fz = call(
-        functools.partial(predict_kernel, own, frames, tall),
+        functools.partial(predict_kernel, half, frames, tall),
         (
             jax.ShapeDtypeStruct((coil_rows, samples), BF16),
             jax.ShapeDtypeStruct((samples, 2 * width), BF16),
@@ -455,14 +498,16 @@
         flops * frames,
         sent, got, v_own, taby, tabz, coil_of, b_rows, m_rows, kd,
     )
-    resid_terms = shares(predicted, "cuts")
+    resid_terms = shares(predicted, "cuts", skip=1)
 
     fold = max(1, LANES // (2 * rank))
-    pieces, g = call(
-        functools.partial(gradient_kernel, own, frames, tall, scale, len(resid_terms)),
+    own_slab = jax.ShapeDtypeStruct((tall // 2, 2 * frames, width), BF16)
+    pieces, g, theirs = call(
+        functools.partial(gradient_kernel, half, frames, tall, slab, scale, len(resid_terms)),
         (
-            jax.ShapeDtypeStruct((n_cuts, n_frame, own // fold, 2 * rank * fold), BF16),
-            jax.ShapeDtypeStruct((tall, 2 * frames, width), BF16),
+            jax.ShapeDtypeStruct((n_cuts, n_frame, half // fold, 2 * rank * fold), F32),
+            own_slab,
+            own_slab,
         ),
         [pltpu.VMEM(x_shape.shape, F32), images(frames)],
         flops * frames,
@@ -470,14 +515,12 @@
     )
     (grad,) = call(
         basis_kernel,
-        (jax.ShapeDtypeStruct((2 * rank * tall * halves, LANES), F32),),
+        (jax.ShapeDtypeStruct((2 * rank * slab * halves, LANES), F32),),
         [],
-        2 * 2 * rank * 2 * frames * tall * width * 8,
-        sent, got, v_own, g,
+        2 * 2 * rank * 4 * frames * slab * width * 8,
+        sent, got, v_own, g, swap(theirs, "cuts", 1),
     )
-    if spread > 1:
-        grad = jnp.sum(grad.reshape(2, rank, spread, slab, width), axis=2)
-    return grad.reshape(2, rank, slab, width), pieces
+    return grad, pieces
 
 
 def pairs(terms):
@@ -500,12 +543,15 @@
         )
         grads.append(grad)
         fg = fg + term
-    basis_grad = grads[0][:, :, :, None] if readout == 1 else jnp.stack(grads, axis=3)
     pieces = fg.reshape((n_cuts * n_frame,) + fg.shape[2:])
     arriving = lax.all_to_all(pieces, ("cuts", "frame"), 0, 0, tiled=True)
-    summed = jnp.sum(arriving.astype(F32), axis=0)
-    folded = summed.reshape(summed.shape[0], -1, 2, rank)
-    return basis_grad, folded.transpose(2, 3, 1, 0).reshape(2, rank, own)
+    arriving, grads = lax.optimization_barrier((arriving, grads))
+    grads = [grad.reshape(2, rank, basis.shape[2], -1) for grad in grads]
+    basis_grad = grads[0][:, :, :, None] if readout == 1 else jnp.stack(grads, axis=3)
+    parts = arriving.astype(F32).reshape((n_cuts // 2, 2, n_frame) + fg.shape[2:])
+    summed = jnp.sum(parts, axis=(0, 2))
+    folded = summed.reshape(2, summed.shape[1], -1, 2, rank)
+    return basis_grad, folded.transpose(3, 4, 0, 2, 1).reshape(2, rank, own)
 
 
 def solution(mesh):

time: 45.4 us -> 44.6 us (0.982)
  waiting for transfers between devices: 13.5 us -> 11.8 us
  starting transfers between devices: 13.9 us -> 14.5 us
    ppermute x6 -> x9, waiting for transfers between devices: 4.77 us -> 3.96 us  [swap(): return lax.ppermute(value, axis, [(i, i ^ distance) for i in range(size)])]
    ppermute x3, waiting for transfers between devices: 3.16 us -> 2.37 us  [collect(): got.append(lax.ppermute(packet, ('cuts', 'frame'), route))]
    ppermute x6 -> x9, starting transfers between devices: 4.59 us -> 4.93 us  [swap(): return lax.ppermute(value, axis, [(i, i ^ distance) for i in range(size)])]
  transfers between devices with their start and end apart: 10 -> 13, of which waited for: 10 -> 8; matrix products, arithmetic and copies ran while one was open for 0% -> 1% of each run, Pallas kernels for 6% -> 7%
where the time goes in v5:
time: 44.6 us; the launch traced here: 44.2 us
  starting transfers between devices  14.5 us (33%)
  Pallas kernels  14.2 us (32%)
  waiting for transfers between devices  11.8 us (26%)
  local copies, waits for them, and re-layouts  2.43 us (5%)
  between operations  0.83 us (2%)
    pallas_call x5, Pallas kernels, call(): pl.pallas_call(kernel, out_shape=outs, scratch_shapes=scratch, compiler_p...  14.2 us
    all_to_all x1, waiting for transfers between devices, body(): arriving = lax.all_to_all(pieces, ('cuts', 'frame'), 0, 0, tiled=True)  5.5 us
    all_to_all x1, starting transfers between devices, body(): arriving = lax.all_to_all(pieces, ('cuts', 'frame'), 0, 0, tiled=True)  5.09 us
    ppermute x9, starting transfers between devices, swap(): return lax.ppermute(value, axis, [(i, i ^ distance) for i in range(size)])  4.93 us
    ppermute x3, starting transfers between devices, collect(): got.append(lax.ppermute(packet, ('cuts', 'frame'), route))  4.52 us
    ppermute x9, waiting for transfers between devices, swap(): return lax.ppermute(value, axis, [(i, i ^ distance) for i in range(size)])  3.96 us
    ppermute x3, waiting for transfers between devices, collect(): got.append(lax.ppermute(packet, ('cuts', 'frame'), route))  2.37 us
    unnamed x10, local copies, waits for them, and re-layouts  1.39 us
  transfers between devices with their start and end apart: 13, of which 8 were waited for; matrix products, arithmetic and copies ran while one was open for 1% of the time, Pallas kernels for 7%

profile of v5, /device:TPU:0, one launch (start us, length us, event | category | flops | bytes accessed | tf_op | source)
XLA Modules:
  0.0 44.2 jit_solution(7364313807481605741)
XLA Ops:
  0.7 0.0 copy-start.4
  0.7 0.7 %copy-done.4 = s32[64,2]{0,1:T(2,128)S(1)} copy-done((s32[64,2]{0,1:T(2,128)S(1)}, s32[64,2]{0,1:T(2,128)}, u32[]{:S(2)}) %copy-start.4) | copy-done | bytes 536
  1.4 0.0 copy-start.3
  1.4 0.1 select_convert_fusion
  1.5 0.5 %collective-permute-start.4 = (bf16[64,16,256]{2,1,0:T(8,128)(2,1)}, bf16[64,16,256]{2,1,0:T(8,128)(2,1)S(1)}, u32[]{:S(2)}, u32[]{:S(2)}) collective-permute-start(bf16[64,16,256]{2,1,0:T(8,128)(2,1)} %bitcast.54), channel_id=1, source_target_pairs={{0,4},{4,0},{8,12},{12,8},{16,20},{20,16},{24,28},{28,24},{1,5},{5... | collective-permute-start | bytes 1572872 | tf_op jit(solution)/shard_map/ppermute | solution.py:353
  2.0 0.1 collective-permute-start
  2.1 0.0 copy-done.3
  2.1 0.5 %collective-permute-start.7 = (bf16[2,64,2,12]{1,2,3,0:T(2,128)(2,1)S(1)}, bf16[2,64,2,12]{1,2,3,0:T(2,128)(2,1)S(1)}, u32[]{:S(2)}, u32[]{:S(2)}) collective-permute-start(bf16[2,64,2,12]{1,2,3,0:T(2,128)(2,1)S(1)} %bitcast.70), channel_id=1, source_target_pairs={{0,4},{4,0},{8,12},{12,8},{16,20},{20,16},{24,28},{28,24},{1,5},{5... | collective-permute-start | bytes 18440 | tf_op jit(solution)/shard_map/ppermute | solution.py:353
  2.5 0.1 collective-permute-start.5
  2.6 0.0 copy-start
  2.6 0.7 %copy-done = bf16[2,32,16]{1,2,0:T(8,128)(2,1)S(1)} copy-done((bf16[2,32,16]{1,2,0:T(8,128)(2,1)S(1)}, bf16[2,32,16]{1,2,0:T(8,128)(2,1)}, u32[]{:S(2)}) %copy-start) | copy-done | bytes 2072
  3.3 0.3 collective-permute-done
  3.6 0.1 add_convert_fusion.1
  3.7 0.0 copy-start.1
  3.7 0.0 copy-start.2
  3.7 3.9 %collective-permute-start.3 = (bf16[32,64]{1,0:T(8,128)(2,1)S(1)}, bf16[32,64]{1,0:T(8,128)(2,1)S(1)}, u32[]{:S(2)}, u32[]{:S(2)}) collective-permute-start(bf16[32,64]{1,0:T(8,128)(2,1)S(1)} %broadcast_select_fusion.2.after_ref), channel_id=1, source_target_pairs={{0,24},{1,25},{2,26},{3,27},{4,7},{5,6},{6,5},{7,4},{8,16},{9,17},... | collective-permute-start | bytes 12296 | tf_op jit(solution)/shard_map/ppermute | solution.py:391
  7.6 0.5 %collective-permute-start.2 = (bf16[32,64]{1,0:T(8,128)(2,1)S(1)}, bf16[32,64]{1,0:T(8,128)(2,1)S(1)}, u32[]{:S(2)}, u32[]{:S(2)}) collective-permute-start(bf16[32,64]{1,0:T(8,128)(2,1)S(1)} %broadcast_select_fusion.2.after_ref), channel_id=1, source_target_pairs={{0,16},{1,17},{2,18},{3,19},{4,6},{5,7},{6,4},{7,5},{8,24},{9,25},... | collective-permute-start | bytes 12296 | tf_op jit(solution)/shard_map/ppermute | solution.py:391
  8.1 0.0 collective-permute-done.4.after_ref.b_got_ref
  8.1 0.1 collective-permute-start.1
  8.2 0.4 shard_map.68
  8.7 0.0 collective-permute-done.5.m_got_ref
  8.7 0.0 copy-done.1
  8.7 0.0 copy-done.2
  8.7 0.7 %shard_map.69 = (bf16[32,64,256]{2,1,0:T(8,128)(2,1)S(1)}, bf16[2,12,32,256]{3,2,1,0:T(8,128)(2,1)S(1)}) custom-call(bf16[32,64]{1,0:T(8,128)(2,1)S(1)} %broadcast_select_fusion.2.after_ref, bf16[64,16,256]{2,1,0:T(8,128)(2,1)S(1)} %bitcast.55, bf16[64,16,256]{2,1,0:T(8,128)(2,1)S(1)} %collective-permute-done.4.after_ref.b_got_ref, ...), custom_call_target="tpu_custom_call" | custom-call | flops 1073741824 | bytes 1449984 | tf_op jit(solution)/shard_map/pallas_call | solution.py:409
  9.4 0.0 collective-permute-done.3
  9.4 1.9 %collective-permute-done.2 = bf16[32,64]{1,0:T(8,128)(2,1)S(1)} collective-permute-done((bf16[32,64]{1,0:T(8,128)(2,1)S(1)}, bf16[32,64]{1,0:T(8,128)(2,1)S(1)}, u32[]{:S(2)}, u32[]{:S(2)}) %collective-permute-start.2) | collective-permute-done | bytes 4128 | tf_op jit(solution)/shard_map/ppermute | solution.py:391
  11.2 0.5 %collective-permute-done.1 = bf16[32,64]{1,0:T(8,128)(2,1)S(1)} collective-permute-done((bf16[32,64]{1,0:T(8,128)(2,1)S(1)}, bf16[32,64]{1,0:T(8,128)(2,1)S(1)}, u32[]{:S(2)}, u32[]{:S(2)}) %collective-permute-start.1) | collective-permute-done | bytes 4128 | tf_op jit(solution)/shard_map/ppermute | solution.py:391
  11.8 0.1 maximum_select_fusion.refs_0_.sent_ref
  11.8 0.3 collective-permute-start.6
  12.1 0.0 collective-permute-done.7
  12.2 0.2 copy.11
  12.3 0.1 reshape.37
  12.5 0.1 copy.12.refs_8_
  12.5 0.5 %collective-permute-done.6.refs_1_.got_ref = bf16[32,96]{1,0:T(8,128)(2,1)S(1)} collective-permute-done((bf16[32,96]{1,0:T(8,128)(2,1)S(1)}, bf16[32,96]{1,0:T(8,128)(2,1)S(1)}, u32[]{:S(2)}, u32[]{:S(2)}) %collective-permute-start.6) | collective-permute-done | bytes 6176 | tf_op jit(solution)/shard_map/ppermute | solution.py:353
  13.0 5.5 %shard_map.70 = (bf16[24,512]{1,0:T(8,128)(2,1)S(1)}, bf16[512,512]{1,0:T(8,128)(2,1)S(1)}, bf16[512,768]{1,0:T(8,128)(2,1)S(1)}) custom-call(bf16[32,96]{1,0:T(8,128)(2,1)S(1)} %maximum_select_fusion.refs_0_.sent_ref, bf16[32,96]{1,0:T(8,128)(2,1)S(1)} %collective-permute-done.6.refs_1_.got_ref, bf16[2,16,32]{2,1,0:T(8,128)(2,1)S(1)} %bitcast.52, ...), custom_call_target="tpu_custom_call" | custom-call | flops 3221225472 | bytes 1982464 | tf_op jit(solution)/shard_map/pallas_call | solution.py:409
  18.6 2.4 %collective-permute-start.10 = (bf16[24,512]{1,0:T(8,128)(2,1)S(1)}, bf16[24,512]{1,0:T(8,128)(2,1)S(1)}, u32[]{:S(2)}, u32[]{:S(2)}) collective-permute-start(bf16[24,512]{1,0:T(8,128)(2,1)S(1)} %get-tuple-element.50.refs_0_), channel_id=1, source_target_pairs={{0,24},{4,28},{8,16},{12,20},{16,8},{20,12},{24,0},{28,4},{1,25},{... | collective-permute-start | bytes 73736 | tf_op jit(solution)/shard_map/ppermute | solution.py:353
  21.0 0.5 %collective-permute-start.9 = (bf16[24,512]{1,0:T(8,128)(2,1)S(1)}, bf16[24,512]{1,0:T(8,128)(2,1)S(1)}, u32[]{:S(2)}, u32[]{:S(2)}) collective-permute-start(bf16[24,512]{1,0:T(8,128)(2,1)S(1)} %get-tuple-element.50.refs_0_), channel_id=1, source_target_pairs={{0,16},{4,20},{8,24},{12,28},{16,0},{20,4},{24,8},{28,12},{1,17},{... | collective-permute-start | bytes 73736 | tf_op jit(solution)/shard_map/ppermute | solution.py:353
  21.5 0.6 %collective-permute-start.8 = (bf16[24,512]{1,0:T(8,128)(2,1)S(1)}, bf16[24,512]{1,0:T(8,128)(2,1)S(1)}, u32[]{:S(2)}, u32[]{:S(2)}) collective-permute-start(bf16[24,512]{1,0:T(8,128)(2,1)S(1)} %get-tuple-element.50.refs_0_), channel_id=1, source_target_pairs={{0,8},{4,12},{8,0},{12,4},{16,24},{20,28},{24,16},{28,20},{1,9},{5... | collective-permute-start | bytes 73736 | tf_op jit(solution)/shard_map/ppermute | solution.py:353
  22.1 1.2 %collective-permute-done.10.refs_3_ = bf16[24,512]{1,0:T(8,128)(2,1)S(1)} collective-permute-done((bf16[24,512]{1,0:T(8,128)(2,1)S(1)}, bf16[24,512]{1,0:T(8,128)(2,1)S(1)}, u32[]{:S(2)}, u32[]{:S(2)}) %collective-permute-start.10) | collective-permute-done | bytes 24608 | tf_op jit(solution)/shard_map/ppermute | solution.py:353
  23.4 1.5 %collective-permute-done.9.refs_2_ = bf16[24,512]{1,0:T(8,128)(2,1)S(1)} collective-permute-done((bf16[24,512]{1,0:T(8,128)(2,1)S(1)}, bf16[24,512]{1,0:T(8,128)(2,1)S(1)}, u32[]{:S(2)}, u32[]{:S(2)}) %collective-permute-start.9) | collective-permute-done | bytes 24608 | tf_op jit(solution)/shard_map/ppermute | solution.py:353
  24.8 0.5 %collective-permute-done.8.refs_1_ = bf16[24,512]{1,0:T(8,128)(2,1)S(1)} collective-permute-done((bf16[24,512]{1,0:T(8,128)(2,1)S(1)}, bf16[24,512]{1,0:T(8,128)(2,1)S(1)}, u32[]{:S(2)}, u32[]{:S(2)}) %collective-permute-start.8) | collective-permute-done | bytes 24608 | tf_op jit(solution)/shard_map/ppermute | solution.py:353
  25.3 5.6 %shard_map.71 = (f32[8,4,4,128]{3,2,1,0:T(4,128)}, bf16[16,64,256]{2,1,0:T(8,128)(2,1)S(1)}, bf16[16,64,256]{2,1,0:T(8,128)(2,1)S(1)}) custom-call(bf16[24,512]{1,0:T(8,128)(2,1)S(1)} %get-tuple-element.50.refs_0_, bf16[24,512]{1,0:T(8,128)(2,1)S(1)} %collective-permute-done.8.refs_1_, bf16[24,512]{1,0:T(8,128)(2,1)S(1)} %collective-permute-done.9.refs_2_, ...), custom_call_target="tpu_custom_call" | custom-call | flops 3221225472 | bytes 2932736 | tf_op jit(solution)/shard_map/pallas_call | solution.py:409
  30.9 0.0 collective-permute-start.11
  30.9 5.1 %all-to-all-start = ((f32[32,4,128]{2,1,0:T(4,128)}), f32[32,4,128]{2,1,0:T(4,128)S(1)}, u32[]{:S(2)}, u32[]{:S(2)}) async-start(f32[32,4,128]{2,1,0:T(4,128)} %bitcast.14), calls=%async_computation | async-start | bytes 131072 | tf_op jit(solution)/shard_map/all_to_all | solution.py:547
  36.0 0.0 collective-permute-done.11.g_got_ref
  36.0 2.0 %shard_map.72 = f32[2048,128]{1,0:T(8,128)} custom-call(bf16[32,96]{1,0:T(8,128)(2,1)S(1)} %maximum_select_fusion.refs_0_.sent_ref, bf16[32,96]{1,0:T(8,128)(2,1)S(1)} %collective-permute-done.6.refs_1_.got_ref, bf16[2,16,32]{2,1,0:T(8,128)(2,1)S(1)} %bitcast.53, bf16[16,64,256]{2,1,0:T(8,128)(2,1)S(1)} %get-tuple-element.54.g_ref, ...), custom_call_target="tpu_custom_call" | custom-call | flops 536870912 | bytes 1073152 | tf_op jit(solution)/shard_map/pallas_call | solution.py:409
  38.0 5.5 %all-to-all-done = f32[32,4,128]{2,1,0:T(4,128)S(1)} async-done(((f32[32,4,128]{2,1,0:T(4,128)}), f32[32,4,128]{2,1,0:T(4,128)S(1)}, u32[]{:S(2)}, u32[]{:S(2)}) %all-to-all-start) | async-done | bytes 65568 | tf_op jit(solution)/shard_map/all_to_all | solution.py:547
  43.5 0.1 reshape.40
  43.6 0.6 %copy.13 = f32[2,32,2,2,4]{1,4,3,2,0:T(4,128)} copy(f32[2,32,2,2,4]{1,0,3,4,2:T(2,128)S(1)} %bitcast.65) | data formatting | bytes 8192 | tf_op jit(solution)/shard_map/transpose | solution.py:554
  (12 shorter events, 0.2 us)
Async XLA Ops:
  0.7 0.7 %copy-start.4 = (s32[64,2]{0,1:T(2,128)S(1)}, s32[64,2]{0,1:T(2,128)}, u32[]{:S(2)}) copy-start(s32[64,2]{0,1:T(2,128)} %param.8) | copy-start | bytes 1540
  1.4 0.7 %copy-start.3 = (bf16[2,64,2,12,1]{1,2,4,3,0:T(2,128)(2,1)S(1)}, bf16[2,64,2,12,1]{1,2,4,3,0:T(2,128)(2,1)}, u32[]{:S(2)}) copy-start(bf16[2,64,2,12,1]{1,2,4,3,0:T(2,128)(2,1)} %param.9) | copy-start | bytes 18436
  1.5 6.6 %collective-permute-start.4 = (bf16[64,16,256]{2,1,0:T(8,128)(2,1)}, bf16[64,16,256]{2,1,0:T(8,128)(2,1)S(1)}, u32[]{:S(2)}, u32[]{:S(2)}) collective-permute-start(bf16[64,16,256]{2,1,0:T(8,128)(2,1)} %bitcast.54), channel_id=1, source_target_pairs={{0,4},{4,0},{8,12},{12,8},{16,20},{20,16},{24,28},{28,24},{1,5},{5... | collective-permute-start | bytes 1572872 | tf_op jit(solution)/shard_map/ppermute | solution.py:353
  2.0 1.6 %collective-permute-start = (bf16[32,64]{1,0:T(8,128)(2,1)S(1)}, bf16[32,64]{1,0:T(8,128)(2,1)S(1)}, u32[]{:S(2)}, u32[]{:S(2)}) collective-permute-start(bf16[32,64]{1,0:T(8,128)(2,1)S(1)} %select_convert_fusion), channel_id=1, source_target_pairs={{0,4},{4,0},{8,12},{12,8},{16,20},{20,16},{24,28},{28,24},{1,5},{5... | collective-permute-start | bytes 12296 | tf_op jit(solution)/shard_map/ppermute | solution.py:353
  2.1 10.0 %collective-permute-start.7 = (bf16[2,64,2,12]{1,2,3,0:T(2,128)(2,1)S(1)}, bf16[2,64,2,12]{1,2,3,0:T(2,128)(2,1)S(1)}, u32[]{:S(2)}, u32[]{:S(2)}) collective-permute-start(bf16[2,64,2,12]{1,2,3,0:T(2,128)(2,1)S(1)} %bitcast.70), channel_id=1, source_target_pairs={{0,4},{4,0},{8,12},{12,8},{16,20},{20,16},{24,28},{28,24},{1,5},{5... | collective-permute-start | bytes 18440 | tf_op jit(solution)/shard_map/ppermute | solution.py:353
  2.5 6.1 %collective-permute-start.5 = (bf16[2,12,16,256]{3,2,1,0:T(8,128)(2,1)}, bf16[2,12,16,256]{3,2,1,0:T(8,128)(2,1)S(1)}, u32[]{:S(2)}, u32[]{:S(2)}) collective-permute-start(bf16[2,12,16,256]{3,2,1,0:T(8,128)(2,1)} %bitcast.56), channel_id=1, source_target_pairs={{0,4},{4,0},{8,12},{12,8},{16,20},{20,16},{24,28},{28,24},{1,5},{5... | collective-permute-start | bytes 589832 | tf_op jit(solution)/shard_map/ppermute | solution.py:353
  2.6 0.7 %copy-start = (bf16[2,32,16]{1,2,0:T(8,128)(2,1)S(1)}, bf16[2,32,16]{1,2,0:T(8,128)(2,1)}, u32[]{:S(2)}) copy-start(bf16[2,32,16]{1,2,0:T(8,128)(2,1)} %param.7) | copy-start | bytes 6148
  3.7 5.0 %copy-start.1 = (bf16[2,32,16,1,256]{4,2,3,1,0:T(8,128)(2,1)S(1)}, bf16[2,32,16,1,256]{4,2,3,1,0:T(8,128)(2,1)}, u32[]{:S(2)}) copy-start(bf16[2,32,16,1,256]{4,2,3,1,0:T(8,128)(2,1)} %param.5) | copy-start | bytes 1572868
  3.7 5.0 %copy-start.2 = (bf16[2,12,16,1,256]{4,2,3,1,0:T(8,128)(2,1)S(1)}, bf16[2,12,16,1,256]{4,2,3,1,0:T(8,128)(2,1)}, u32[]{:S(2)}) copy-start(bf16[2,12,16,1,256]{4,2,3,1,0:T(8,128)(2,1)} %param.6) | copy-start | bytes 589828
  3.7 5.7 %collective-permute-start.3 = (bf16[32,64]{1,0:T(8,128)(2,1)S(1)}, bf16[32,64]{1,0:T(8,128)(2,1)S(1)}, u32[]{:S(2)}, u32[]{:S(2)}) collective-permute-start(bf16[32,64]{1,0:T(8,128)(2,1)S(1)} %broadcast_select_fusion.2.after_ref), channel_id=1, source_target_pairs={{0,24},{1,25},{2,26},{3,27},{4,7},{5,6},{6,5},{7,4},{8,16},{9,17},... | collective-permute-start | bytes 12296 | tf_op jit(solution)/shard_map/ppermute | solution.py:391
  7.6 3.7 %collective-permute-start.2 = (bf16[32,64]{1,0:T(8,128)(2,1)S(1)}, bf16[32,64]{1,0:T(8,128)(2,1)S(1)}, u32[]{:S(2)}, u32[]{:S(2)}) collective-permute-start(bf16[32,64]{1,0:T(8,128)(2,1)S(1)} %broadcast_select_fusion.2.after_ref), channel_id=1, source_target_pairs={{0,16},{1,17},{2,18},{3,19},{4,6},{5,7},{6,4},{7,5},{8,24},{9,25},... | collective-permute-start | bytes 12296 | tf_op jit(solution)/shard_map/ppermute | solution.py:391
  8.1 3.7 %collective-permute-start.1 = (bf16[32,64]{1,0:T(8,128)(2,1)S(1)}, bf16[32,64]{1,0:T(8,128)(2,1)S(1)}, u32[]{:S(2)}, u32[]{:S(2)}) collective-permute-start(bf16[32,64]{1,0:T(8,128)(2,1)S(1)} %broadcast_select_fusion.2.after_ref), channel_id=1, source_target_pairs={{0,8},{1,9},{2,10},{3,11},{4,5},{5,4},{6,7},{7,6},{8,0},{9,1},{10,... | collective-permute-start | bytes 12296 | tf_op jit(solution)/shard_map/ppermute | solution.py:391
  11.8 1.2 %collective-permute-start.6 = (bf16[32,96]{1,0:T(8,128)(2,1)S(1)}, bf16[32,96]{1,0:T(8,128)(2,1)S(1)}, u32[]{:S(2)}, u32[]{:S(2)}) collective-permute-start(bf16[32,96]{1,0:T(8,128)(2,1)S(1)} %maximum_select_fusion.refs_0_.sent_ref), channel_id=1, source_target_pairs={{0,4},{4,0},{8,12},{12,8},{16,20},{20,16},{24,28},{28,24},{1,5},{5... | collective-permute-start | bytes 18440 | tf_op jit(solution)/shard_map/ppermute | solution.py:353
  18.6 4.8 %collective-permute-start.10 = (bf16[24,512]{1,0:T(8,128)(2,1)S(1)}, bf16[24,512]{1,0:T(8,128)(2,1)S(1)}, u32[]{:S(2)}, u32[]{:S(2)}) collective-permute-start(bf16[24,512]{1,0:T(8,128)(2,1)S(1)} %get-tuple-element.50.refs_0_), channel_id=1, source_target_pairs={{0,24},{4,28},{8,16},{12,20},{16,8},{20,12},{24,0},{28,4},{1,25},{... | collective-permute-start | bytes 73736 | tf_op jit(solution)/shard_map/ppermute | solution.py:353
  21.0 3.8 %collective-permute-start.9 = (bf16[24,512]{1,0:T(8,128)(2,1)S(1)}, bf16[24,512]{1,0:T(8,128)(2,1)S(1)}, u32[]{:S(2)}, u32[]{:S(2)}) collective-permute-start(bf16[24,512]{1,0:T(8,128)(2,1)S(1)} %get-tuple-element.50.refs_0_), channel_id=1, source_target_pairs={{0,16},{4,20},{8,24},{12,28},{16,0},{20,4},{24,8},{28,12},{1,17},{... | collective-permute-start | bytes 73736 | tf_op jit(solution)/shard_map/ppermute | solution.py:353
  21.5 3.8 %collective-permute-start.8 = (bf16[24,512]{1,0:T(8,128)(2,1)S(1)}, bf16[24,512]{1,0:T(8,128)(2,1)S(1)}, u32[]{:S(2)}, u32[]{:S(2)}) collective-permute-start(bf16[24,512]{1,0:T(8,128)(2,1)S(1)} %get-tuple-element.50.refs_0_), channel_id=1, source_target_pairs={{0,8},{4,12},{8,0},{12,4},{16,24},{20,28},{24,16},{28,20},{1,9},{5... | collective-permute-start | bytes 73736 | tf_op jit(solution)/shard_map/ppermute | solution.py:353
  30.9 5.1 %collective-permute-start.11 = (bf16[16,64,256]{2,1,0:T(8,128)(2,1)S(1)}, bf16[16,64,256]{2,1,0:T(8,128)(2,1)S(1)}, u32[]{:S(2)}, u32[]{:S(2)}) collective-permute-start(bf16[16,64,256]{2,1,0:T(8,128)(2,1)S(1)} %get-tuple-element.55), channel_id=1, source_target_pairs={{0,4},{4,0},{8,12},{12,8},{16,20},{20,16},{24,28},{28,24},{1,5},{5... | collective-permute-start | bytes 1572872 | tf_op jit(solution)/shard_map/ppermute | solution.py:353
  30.9 12.6 %all-to-all-start = ((f32[32,4,128]{2,1,0:T(4,128)}), f32[32,4,128]{2,1,0:T(4,128)S(1)}, u32[]{:S(2)}, u32[]{:S(2)}) async-start(f32[32,4,128]{2,1,0:T(4,128)} %bitcast.14), calls=%async_computation | async-start | bytes 131072 | tf_op jit(solution)/shard_map/all_to_all | solution.py:547

commit v6 on v5

--- a/solution.py
+++ b/solution.py
@@ -207,7 +207,7 @@
         p_im = (m_re * i_im + m_im * i_re).reshape(rows, width)
         at = pl.ds(pl.multiple_of(t * per, TILE), per)
         lhs = adjoint_pair(w_ref[at, :])
-        y = nt(lhs[:, :width], p_re) + nt(lhs[:, width:], p_im)
+        y = jnp.concatenate([(nt(p_re[k:k+128], lhs[:, :width]) + nt(p_im[k:k+128], lhs[:, width:])).T for k in range(0,rows,128)],axis=1)
         y_re, y_im = y[:per], y[per:]
         f = fz_ref[at, :].astype(F32)
         f_cos, f_sin = f[:, :rows], f[:, pad : pad + rows]

time: 44.6 us -> 44 us (0.987)
  Pallas kernels: 14.2 us -> 13.7 us
    pallas_call x5, Pallas kernels: 14.2 us -> 13.7 us  [call(): pl.pallas_call(kernel, out_shape=outs, scratch_shapes=scratch, compiler_p...]
where the time goes in v6:
time: 44 us; the launch traced here: 43.7 us
  starting transfers between devices  14.5 us (33%)
  Pallas kernels  13.7 us (31%)
  waiting for transfers between devices  11.8 us (27%)
  local copies, waits for them, and re-layouts  2.43 us (6%)
  between operations  0.83 us (2%)
    pallas_call x5, Pallas kernels, call(): pl.pallas_call(kernel, out_shape=outs, scratch_shapes=scratch, compiler_p...  13.7 us
    all_to_all x1, waiting for transfers between devices, body(): arriving = lax.all_to_all(pieces, ('cuts', 'frame'), 0, 0, tiled=True)  5.5 us
    all_to_all x1, starting transfers between devices, body(): arriving = lax.all_to_all(pieces, ('cuts', 'frame'), 0, 0, tiled=True)  5.09 us
    ppermute x9, starting transfers between devices, swap(): return lax.ppermute(value, axis, [(i, i ^ distance) for i in range(size)])  4.93 us
    ppermute x3, starting transfers between devices, collect(): got.append(lax.ppermute(packet, ('cuts', 'frame'), route))  4.52 us
    ppermute x9, waiting for transfers between devices, swap(): return lax.ppermute(value, axis, [(i, i ^ distance) for i in range(size)])  3.96 us
    ppermute x3, waiting for transfers between devices, collect(): got.append(lax.ppermute(packet, ('cuts', 'frame'), route))  2.37 us
    unnamed x10, local copies, waits for them, and re-layouts  1.39 us
  transfers between devices with their start and end apart: 13, of which 8 were waited for; matrix products, arithmetic and copies ran while one was open for 1% of the time, Pallas kernels for 7%

profile of v6, /device:TPU:0, one launch (start us, length us, event | category | flops | bytes accessed | tf_op | source)
XLA Modules:
  0.0 43.7 jit_solution(14876094400271250854)
XLA Ops:
  0.7 0.0 copy-start.4
  0.7 0.7 %copy-done.4 = s32[64,2]{0,1:T(2,128)S(1)} copy-done((s32[64,2]{0,1:T(2,128)S(1)}, s32[64,2]{0,1:T(2,128)}, u32[]{:S(2)}) %copy-start.4) | copy-done | bytes 536
  1.4 0.0 copy-start.3
  1.4 0.1 select_convert_fusion
  1.5 0.5 %collective-permute-start.4 = (bf16[64,16,256]{2,1,0:T(8,128)(2,1)}, bf16[64,16,256]{2,1,0:T(8,128)(2,1)S(1)}, u32[]{:S(2)}, u32[]{:S(2)}) collective-permute-start(bf16[64,16,256]{2,1,0:T(8,128)(2,1)} %bitcast.54), channel_id=1, source_target_pairs={{0,4},{4,0},{8,12},{12,8},{16,20},{20,16},{24,28},{28,24},{1,5},{5... | collective-permute-start | bytes 1572872 | tf_op jit(solution)/shard_map/ppermute | solution.py:353
  2.0 0.1 collective-permute-start
  2.1 0.0 copy-done.3
  2.1 0.5 %collective-permute-start.7 = (bf16[2,64,2,12]{1,2,3,0:T(2,128)(2,1)S(1)}, bf16[2,64,2,12]{1,2,3,0:T(2,128)(2,1)S(1)}, u32[]{:S(2)}, u32[]{:S(2)}) collective-permute-start(bf16[2,64,2,12]{1,2,3,0:T(2,128)(2,1)S(1)} %bitcast.70), channel_id=1, source_target_pairs={{0,4},{4,0},{8,12},{12,8},{16,20},{20,16},{24,28},{28,24},{1,5},{5... | collective-permute-start | bytes 18440 | tf_op jit(solution)/shard_map/ppermute | solution.py:353
  2.5 0.1 collective-permute-start.5
  2.6 0.0 copy-start
  2.6 0.7 %copy-done = bf16[2,32,16]{1,2,0:T(8,128)(2,1)S(1)} copy-done((bf16[2,32,16]{1,2,0:T(8,128)(2,1)S(1)}, bf16[2,32,16]{1,2,0:T(8,128)(2,1)}, u32[]{:S(2)}) %copy-start) | copy-done | bytes 2072
  3.3 0.3 collective-permute-done
  3.6 0.1 add_convert_fusion.1
  3.7 0.0 copy-start.1
  3.7 0.0 copy-start.2
  3.7 3.9 %collective-permute-start.3 = (bf16[32,64]{1,0:T(8,128)(2,1)S(1)}, bf16[32,64]{1,0:T(8,128)(2,1)S(1)}, u32[]{:S(2)}, u32[]{:S(2)}) collective-permute-start(bf16[32,64]{1,0:T(8,128)(2,1)S(1)} %broadcast_select_fusion.2.after_ref), channel_id=1, source_target_pairs={{0,24},{1,25},{2,26},{3,27},{4,7},{5,6},{6,5},{7,4},{8,16},{9,17},... | collective-permute-start | bytes 12296 | tf_op jit(solution)/shard_map/ppermute | solution.py:391
  7.6 0.5 %collective-permute-start.2 = (bf16[32,64]{1,0:T(8,128)(2,1)S(1)}, bf16[32,64]{1,0:T(8,128)(2,1)S(1)}, u32[]{:S(2)}, u32[]{:S(2)}) collective-permute-start(bf16[32,64]{1,0:T(8,128)(2,1)S(1)} %broadcast_select_fusion.2.after_ref), channel_id=1, source_target_pairs={{0,16},{1,17},{2,18},{3,19},{4,6},{5,7},{6,4},{7,5},{8,24},{9,25},... | collective-permute-start | bytes 12296 | tf_op jit(solution)/shard_map/ppermute | solution.py:391
  8.1 0.0 collective-permute-done.4.after_ref.b_got_ref
  8.1 0.1 collective-permute-start.1
  8.2 0.4 shard_map.68
  8.7 0.0 collective-permute-done.5.m_got_ref
  8.7 0.0 copy-done.1
  8.7 0.0 copy-done.2
  8.7 0.7 %shard_map.69 = (bf16[32,64,256]{2,1,0:T(8,128)(2,1)S(1)}, bf16[2,12,32,256]{3,2,1,0:T(8,128)(2,1)S(1)}) custom-call(bf16[32,64]{1,0:T(8,128)(2,1)S(1)} %broadcast_select_fusion.2.after_ref, bf16[64,16,256]{2,1,0:T(8,128)(2,1)S(1)} %bitcast.55, bf16[64,16,256]{2,1,0:T(8,128)(2,1)S(1)} %collective-permute-done.4.after_ref.b_got_ref, ...), custom_call_target="tpu_custom_call" | custom-call | flops 1073741824 | bytes 1449984 | tf_op jit(solution)/shard_map/pallas_call | solution.py:409
  9.4 0.0 collective-permute-done.3
  9.4 1.9 %collective-permute-done.2 = bf16[32,64]{1,0:T(8,128)(2,1)S(1)} collective-permute-done((bf16[32,64]{1,0:T(8,128)(2,1)S(1)}, bf16[32,64]{1,0:T(8,128)(2,1)S(1)}, u32[]{:S(2)}, u32[]{:S(2)}) %collective-permute-start.2) | collective-permute-done | bytes 4128 | tf_op jit(solution)/shard_map/ppermute | solution.py:391
  11.2 0.5 %collective-permute-done.1 = bf16[32,64]{1,0:T(8,128)(2,1)S(1)} collective-permute-done((bf16[32,64]{1,0:T(8,128)(2,1)S(1)}, bf16[32,64]{1,0:T(8,128)(2,1)S(1)}, u32[]{:S(2)}, u32[]{:S(2)}) %collective-permute-start.1) | collective-permute-done | bytes 4128 | tf_op jit(solution)/shard_map/ppermute | solution.py:391
  11.8 0.1 maximum_select_fusion.refs_0_.sent_ref
  11.8 0.3 collective-permute-start.6
  12.1 0.0 collective-permute-done.7
  12.2 0.2 copy.11
  12.3 0.1 reshape.37
  12.5 0.1 copy.12.refs_8_
  12.5 0.5 %collective-permute-done.6.refs_1_.got_ref = bf16[32,96]{1,0:T(8,128)(2,1)S(1)} collective-permute-done((bf16[32,96]{1,0:T(8,128)(2,1)S(1)}, bf16[32,96]{1,0:T(8,128)(2,1)S(1)}, u32[]{:S(2)}, u32[]{:S(2)}) %collective-permute-start.6) | collective-permute-done | bytes 6176 | tf_op jit(solution)/shard_map/ppermute | solution.py:353
  13.0 5.0 %shard_map.70 = (bf16[24,512]{1,0:T(8,128)(2,1)S(1)}, bf16[512,512]{1,0:T(8,128)(2,1)S(1)}, bf16[512,768]{1,0:T(8,128)(2,1)S(1)}) custom-call(bf16[32,96]{1,0:T(8,128)(2,1)S(1)} %maximum_select_fusion.refs_0_.sent_ref, bf16[32,96]{1,0:T(8,128)(2,1)S(1)} %collective-permute-done.6.refs_1_.got_ref, bf16[2,16,32]{2,1,0:T(8,128)(2,1)S(1)} %bitcast.52, ...), custom_call_target="tpu_custom_call" | custom-call | flops 3221225472 | bytes 1982464 | tf_op jit(solution)/shard_map/pallas_call | solution.py:409
  18.0 2.4 %collective-permute-start.10 = (bf16[24,512]{1,0:T(8,128)(2,1)S(1)}, bf16[24,512]{1,0:T(8,128)(2,1)S(1)}, u32[]{:S(2)}, u32[]{:S(2)}) collective-permute-start(bf16[24,512]{1,0:T(8,128)(2,1)S(1)} %get-tuple-element.50.refs_0_), channel_id=1, source_target_pairs={{0,24},{4,28},{8,16},{12,20},{16,8},{20,12},{24,0},{28,4},{1,25},{... | collective-permute-start | bytes 73736 | tf_op jit(solution)/shard_map/ppermute | solution.py:353
  20.5 0.5 %collective-permute-start.9 = (bf16[24,512]{1,0:T(8,128)(2,1)S(1)}, bf16[24,512]{1,0:T(8,128)(2,1)S(1)}, u32[]{:S(2)}, u32[]{:S(2)}) collective-permute-start(bf16[24,512]{1,0:T(8,128)(2,1)S(1)} %get-tuple-element.50.refs_0_), channel_id=1, source_target_pairs={{0,16},{4,20},{8,24},{12,28},{16,0},{20,4},{24,8},{28,12},{1,17},{... | collective-permute-start | bytes 73736 | tf_op jit(solution)/shard_map/ppermute | solution.py:353
  21.0 0.6 %collective-permute-start.8 = (bf16[24,512]{1,0:T(8,128)(2,1)S(1)}, bf16[24,512]{1,0:T(8,128)(2,1)S(1)}, u32[]{:S(2)}, u32[]{:S(2)}) collective-permute-start(bf16[24,512]{1,0:T(8,128)(2,1)S(1)} %get-tuple-element.50.refs_0_), channel_id=1, source_target_pairs={{0,8},{4,12},{8,0},{12,4},{16,24},{20,28},{24,16},{28,20},{1,9},{5... | collective-permute-start | bytes 73736 | tf_op jit(solution)/shard_map/ppermute | solution.py:353
  21.6 1.2 %collective-permute-done.10.refs_3_ = bf16[24,512]{1,0:T(8,128)(2,1)S(1)} collective-permute-done((bf16[24,512]{1,0:T(8,128)(2,1)S(1)}, bf16[24,512]{1,0:T(8,128)(2,1)S(1)}, u32[]{:S(2)}, u32[]{:S(2)}) %collective-permute-start.10) | collective-permute-done | bytes 24608 | tf_op jit(solution)/shard_map/ppermute | solution.py:353
  22.8 1.5 %collective-permute-done.9.refs_2_ = bf16[24,512]{1,0:T(8,128)(2,1)S(1)} collective-permute-done((bf16[24,512]{1,0:T(8,128)(2,1)S(1)}, bf16[24,512]{1,0:T(8,128)(2,1)S(1)}, u32[]{:S(2)}, u32[]{:S(2)}) %collective-permute-start.9) | collective-permute-done | bytes 24608 | tf_op jit(solution)/shard_map/ppermute | solution.py:353
  24.3 0.5 %collective-permute-done.8.refs_1_ = bf16[24,512]{1,0:T(8,128)(2,1)S(1)} collective-permute-done((bf16[24,512]{1,0:T(8,128)(2,1)S(1)}, bf16[24,512]{1,0:T(8,128)(2,1)S(1)}, u32[]{:S(2)}, u32[]{:S(2)}) %collective-permute-start.8) | collective-permute-done | bytes 24608 | tf_op jit(solution)/shard_map/ppermute | solution.py:353
  24.8 5.6 %shard_map.71 = (f32[8,4,4,128]{3,2,1,0:T(4,128)}, bf16[16,64,256]{2,1,0:T(8,128)(2,1)S(1)}, bf16[16,64,256]{2,1,0:T(8,128)(2,1)S(1)}) custom-call(bf16[24,512]{1,0:T(8,128)(2,1)S(1)} %get-tuple-element.50.refs_0_, bf16[24,512]{1,0:T(8,128)(2,1)S(1)} %collective-permute-done.8.refs_1_, bf16[24,512]{1,0:T(8,128)(2,1)S(1)} %collective-permute-done.9.refs_2_, ...), custom_call_target="tpu_custom_call" | custom-call | flops 3221225472 | bytes 2932736 | tf_op jit(solution)/shard_map/pallas_call | solution.py:409
  30.4 0.0 collective-permute-start.11
  30.4 5.1 %all-to-all-start = ((f32[32,4,128]{2,1,0:T(4,128)}), f32[32,4,128]{2,1,0:T(4,128)S(1)}, u32[]{:S(2)}, u32[]{:S(2)}) async-start(f32[32,4,128]{2,1,0:T(4,128)} %bitcast.14), calls=%async_computation | async-start | bytes 131072 | tf_op jit(solution)/shard_map/all_to_all | solution.py:547
  35.5 0.0 collective-permute-done.11.g_got_ref
  35.5 2.0 %shard_map.72 = f32[2048,128]{1,0:T(8,128)} custom-call(bf16[32,96]{1,0:T(8,128)(2,1)S(1)} %maximum_select_fusion.refs_0_.sent_ref, bf16[32,96]{1,0:T(8,128)(2,1)S(1)} %collective-permute-done.6.refs_1_.got_ref, bf16[2,16,32]{2,1,0:T(8,128)(2,1)S(1)} %bitcast.53, bf16[16,64,256]{2,1,0:T(8,128)(2,1)S(1)} %get-tuple-element.54.g_ref, ...), custom_call_target="tpu_custom_call" | custom-call | flops 536870912 | bytes 1073152 | tf_op jit(solution)/shard_map/pallas_call | solution.py:409
  37.5 5.5 %all-to-all-done = f32[32,4,128]{2,1,0:T(4,128)S(1)} async-done(((f32[32,4,128]{2,1,0:T(4,128)}), f32[32,4,128]{2,1,0:T(4,128)S(1)}, u32[]{:S(2)}, u32[]{:S(2)}) %all-to-all-start) | async-done | bytes 65568 | tf_op jit(solution)/shard_map/all_to_all | solution.py:547
  43.0 0.1 reshape.40
  43.1 0.6 %copy.13 = f32[2,32,2,2,4]{1,4,3,2,0:T(4,128)} copy(f32[2,32,2,2,4]{1,0,3,4,2:T(2,128)S(1)} %bitcast.65) | data formatting | bytes 8192 | tf_op jit(solution)/shard_map/transpose | solution.py:554
  (12 shorter events, 0.2 us)
Async XLA Ops:
  0.7 0.7 %copy-start.4 = (s32[64,2]{0,1:T(2,128)S(1)}, s32[64,2]{0,1:T(2,128)}, u32[]{:S(2)}) copy-start(s32[64,2]{0,1:T(2,128)} %param.8) | copy-start | bytes 1540
  1.4 0.7 %copy-start.3 = (bf16[2,64,2,12,1]{1,2,4,3,0:T(2,128)(2,1)S(1)}, bf16[2,64,2,12,1]{1,2,4,3,0:T(2,128)(2,1)}, u32[]{:S(2)}) copy-start(bf16[2,64,2,12,1]{1,2,4,3,0:T(2,128)(2,1)} %param.9) | copy-start | bytes 18436
  1.5 6.6 %collective-permute-start.4 = (bf16[64,16,256]{2,1,0:T(8,128)(2,1)}, bf16[64,16,256]{2,1,0:T(8,128)(2,1)S(1)}, u32[]{:S(2)}, u32[]{:S(2)}) collective-permute-start(bf16[64,16,256]{2,1,0:T(8,128)(2,1)} %bitcast.54), channel_id=1, source_target_pairs={{0,4},{4,0},{8,12},{12,8},{16,20},{20,16},{24,28},{28,24},{1,5},{5... | collective-permute-start | bytes 1572872 | tf_op jit(solution)/shard_map/ppermute | solution.py:353
  2.0 1.6 %collective-permute-start = (bf16[32,64]{1,0:T(8,128)(2,1)S(1)}, bf16[32,64]{1,0:T(8,128)(2,1)S(1)}, u32[]{:S(2)}, u32[]{:S(2)}) collective-permute-start(bf16[32,64]{1,0:T(8,128)(2,1)S(1)} %select_convert_fusion), channel_id=1, source_target_pairs={{0,4},{4,0},{8,12},{12,8},{16,20},{20,16},{24,28},{28,24},{1,5},{5... | collective-permute-start | bytes 12296 | tf_op jit(solution)/shard_map/ppermute | solution.py:353
  2.1 10.0 %collective-permute-start.7 = (bf16[2,64,2,12]{1,2,3,0:T(2,128)(2,1)S(1)}, bf16[2,64,2,12]{1,2,3,0:T(2,128)(2,1)S(1)}, u32[]{:S(2)}, u32[]{:S(2)}) collective-permute-start(bf16[2,64,2,12]{1,2,3,0:T(2,128)(2,1)S(1)} %bitcast.70), channel_id=1, source_target_pairs={{0,4},{4,0},{8,12},{12,8},{16,20},{20,16},{24,28},{28,24},{1,5},{5... | collective-permute-start | bytes 18440 | tf_op jit(solution)/shard_map/ppermute | solution.py:353
  2.5 6.1 %collective-permute-start.5 = (bf16[2,12,16,256]{3,2,1,0:T(8,128)(2,1)}, bf16[2,12,16,256]{3,2,1,0:T(8,128)(2,1)S(1)}, u32[]{:S(2)}, u32[]{:S(2)}) collective-permute-start(bf16[2,12,16,256]{3,2,1,0:T(8,128)(2,1)} %bitcast.56), channel_id=1, source_target_pairs={{0,4},{4,0},{8,12},{12,8},{16,20},{20,16},{24,28},{28,24},{1,5},{5... | collective-permute-start | bytes 589832 | tf_op jit(solution)/shard_map/ppermute | solution.py:353
  2.6 0.7 %copy-start = (bf16[2,32,16]{1,2,0:T(8,128)(2,1)S(1)}, bf16[2,32,16]{1,2,0:T(8,128)(2,1)}, u32[]{:S(2)}) copy-start(bf16[2,32,16]{1,2,0:T(8,128)(2,1)} %param.7) | copy-start | bytes 6148
  3.7 5.0 %copy-start.1 = (bf16[2,32,16,1,256]{4,2,3,1,0:T(8,128)(2,1)S(1)}, bf16[2,32,16,1,256]{4,2,3,1,0:T(8,128)(2,1)}, u32[]{:S(2)}) copy-start(bf16[2,32,16,1,256]{4,2,3,1,0:T(8,128)(2,1)} %param.5) | copy-start | bytes 1572868
  3.7 5.0 %copy-start.2 = (bf16[2,12,16,1,256]{4,2,3,1,0:T(8,128)(2,1)S(1)}, bf16[2,12,16,1,256]{4,2,3,1,0:T(8,128)(2,1)}, u32[]{:S(2)}) copy-start(bf16[2,12,16,1,256]{4,2,3,1,0:T(8,128)(2,1)} %param.6) | copy-start | bytes 589828
  3.7 5.7 %collective-permute-start.3 = (bf16[32,64]{1,0:T(8,128)(2,1)S(1)}, bf16[32,64]{1,0:T(8,128)(2,1)S(1)}, u32[]{:S(2)}, u32[]{:S(2)}) collective-permute-start(bf16[32,64]{1,0:T(8,128)(2,1)S(1)} %broadcast_select_fusion.2.after_ref), channel_id=1, source_target_pairs={{0,24},{1,25},{2,26},{3,27},{4,7},{5,6},{6,5},{7,4},{8,16},{9,17},... | collective-permute-start | bytes 12296 | tf_op jit(solution)/shard_map/ppermute | solution.py:391
  7.6 3.7 %collective-permute-start.2 = (bf16[32,64]{1,0:T(8,128)(2,1)S(1)}, bf16[32,64]{1,0:T(8,128)(2,1)S(1)}, u32[]{:S(2)}, u32[]{:S(2)}) collective-permute-start(bf16[32,64]{1,0:T(8,128)(2,1)S(1)} %broadcast_select_fusion.2.after_ref), channel_id=1, source_target_pairs={{0,16},{1,17},{2,18},{3,19},{4,6},{5,7},{6,4},{7,5},{8,24},{9,25},... | collective-permute-start | bytes 12296 | tf_op jit(solution)/shard_map/ppermute | solution.py:391
  8.1 3.7 %collective-permute-start.1 = (bf16[32,64]{1,0:T(8,128)(2,1)S(1)}, bf16[32,64]{1,0:T(8,128)(2,1)S(1)}, u32[]{:S(2)}, u32[]{:S(2)}) collective-permute-start(bf16[32,64]{1,0:T(8,128)(2,1)S(1)} %broadcast_select_fusion.2.after_ref), channel_id=1, source_target_pairs={{0,8},{1,9},{2,10},{3,11},{4,5},{5,4},{6,7},{7,6},{8,0},{9,1},{10,... | collective-permute-start | bytes 12296 | tf_op jit(solution)/shard_map/ppermute | solution.py:391
  11.8 1.2 %collective-permute-start.6 = (bf16[32,96]{1,0:T(8,128)(2,1)S(1)}, bf16[32,96]{1,0:T(8,128)(2,1)S(1)}, u32[]{:S(2)}, u32[]{:S(2)}) collective-permute-start(bf16[32,96]{1,0:T(8,128)(2,1)S(1)} %maximum_select_fusion.refs_0_.sent_ref), channel_id=1, source_target_pairs={{0,4},{4,0},{8,12},{12,8},{16,20},{20,16},{24,28},{28,24},{1,5},{5... | collective-permute-start | bytes 18440 | tf_op jit(solution)/shard_map/ppermute | solution.py:353
  18.0 4.8 %collective-permute-start.10 = (bf16[24,512]{1,0:T(8,128)(2,1)S(1)}, bf16[24,512]{1,0:T(8,128)(2,1)S(1)}, u32[]{:S(2)}, u32[]{:S(2)}) collective-permute-start(bf16[24,512]{1,0:T(8,128)(2,1)S(1)} %get-tuple-element.50.refs_0_), channel_id=1, source_target_pairs={{0,24},{4,28},{8,16},{12,20},{16,8},{20,12},{24,0},{28,4},{1,25},{... | collective-permute-start | bytes 73736 | tf_op jit(solution)/shard_map/ppermute | solution.py:353
  20.5 3.8 %collective-permute-start.9 = (bf16[24,512]{1,0:T(8,128)(2,1)S(1)}, bf16[24,512]{1,0:T(8,128)(2,1)S(1)}, u32[]{:S(2)}, u32[]{:S(2)}) collective-permute-start(bf16[24,512]{1,0:T(8,128)(2,1)S(1)} %get-tuple-element.50.refs_0_), channel_id=1, source_target_pairs={{0,16},{4,20},{8,24},{12,28},{16,0},{20,4},{24,8},{28,12},{1,17},{... | collective-permute-start | bytes 73736 | tf_op jit(solution)/shard_map/ppermute | solution.py:353
  21.0 3.8 %collective-permute-start.8 = (bf16[24,512]{1,0:T(8,128)(2,1)S(1)}, bf16[24,512]{1,0:T(8,128)(2,1)S(1)}, u32[]{:S(2)}, u32[]{:S(2)}) collective-permute-start(bf16[24,512]{1,0:T(8,128)(2,1)S(1)} %get-tuple-element.50.refs_0_), channel_id=1, source_target_pairs={{0,8},{4,12},{8,0},{12,4},{16,24},{20,28},{24,16},{28,20},{1,9},{5... | collective-permute-start | bytes 73736 | tf_op jit(solution)/shard_map/ppermute | solution.py:353
  30.4 5.1 %collective-permute-start.11 = (bf16[16,64,256]{2,1,0:T(8,128)(2,1)S(1)}, bf16[16,64,256]{2,1,0:T(8,128)(2,1)S(1)}, u32[]{:S(2)}, u32[]{:S(2)}) collective-permute-start(bf16[16,64,256]{2,1,0:T(8,128)(2,1)S(1)} %get-tuple-element.55), channel_id=1, source_target_pairs={{0,4},{4,0},{8,12},{12,8},{16,20},{20,16},{24,28},{28,24},{1,5},{5... | collective-permute-start | bytes 1572872 | tf_op jit(solution)/shard_map/ppermute | solution.py:353
  30.4 12.6 %all-to-all-start = ((f32[32,4,128]{2,1,0:T(4,128)}), f32[32,4,128]{2,1,0:T(4,128)S(1)}, u32[]{:S(2)}, u32[]{:S(2)}) async-start(f32[32,4,128]{2,1,0:T(4,128)} %bitcast.14), calls=%async_computation | async-start | bytes 131072 | tf_op jit(solution)/shard_map/all_to_all | solution.py:547

commit v7 on v6

--- a/solution.py
+++ b/solution.py
@@ -120,7 +120,7 @@
 def turn_kernel(after_ref, b_ref, b_got_ref, m_ref, m_got_ref, b_out, m_out, turn_ref):
     del after_ref
     images, slab, width = b_ref.shape
-    pitch = turn_ref.shape[1] // images
+    pitch = -(-slab // 8) * 8 + PITCH
     first = in_pair()[1] == 0
     for n, ref in enumerate((b_ref, b_got_ref)):
         start = jnp.where(first, n, 1 - n) * slab
@@ -167,10 +167,6 @@
         fz_ref[rows, :] = nn(hot_z, tabz_ref[...]).astype(BF16)
 
 
-def samples_step(x_ref, frames, per):
-    return x_ref.shape[1] // (2 * per)
-
-
 def predict_kernel(own, frames, slab, *refs):
     sent_ref, got_ref, v_ref, taby_ref, tabz_ref, coil_ref, b_ref, m_ref, kd_ref = refs[:9]
     pred_ref, w_ref, fz_ref, x_ref, i_ref = refs[9:]
@@ -182,7 +178,7 @@
     coils = rows // slab
     halves = width // LANES
     pitch = 2 * steps + PITCH
-    stride = samples_step(x_ref, frames, per)
+    stride = frames + PITCH
 
     pos, others = arrived(sent_ref, got_ref)
     write_tables(pos[: 2 * per, : 2 * frames], taby_ref, tabz_ref, w_ref, fz_ref)
@@ -250,7 +246,7 @@
     coils = rows // slab
     halves = width // LANES
     pitch = 2 * steps + PITCH
-    stride = samples_step(r_ref, frames, per)
+    stride = frames + PITCH
 
     resid = total(r_refs).astype(BF16)
     blocks = max(1, min(per, 512 // frames))
@@ -317,7 +313,7 @@
             fg_ref[c, pl.ds(target, 1)] = piece[None]
 
 
-def basis_kernel(sent_ref, got_ref, v_ref, g_ref, g_got_ref, grad_ref):
+def basis_kernel(sent_ref, got_ref, v_ref, g_ref, g_got_ref, grad_ref, rows_ref):
     _, others = arrived(sent_ref, got_ref)
     place = in_pair()[1]
     pairs_of = [
@@ -325,16 +321,22 @@
         (factor_matrix(*half_factors(v_ref, others, 1 - place)), g_got_ref),
     ]
     halves = g_ref.shape[2] // LANES
-    slab = grad_ref.shape[0] // (2 * v_ref.shape[2] * halves)
+    images = 2 * v_ref.shape[2]
+    slab = grad_ref.shape[0] // (images * halves)
+    pitch = slab * halves + PITCH
     for z in range(slab):
         grad = functools.reduce(
             jnp.add,
             [tn(v, ref[k]) for v, ref in pairs_of for k in range(z, g_ref.shape[0], slab)],
         )
         for h in range(halves):
-            grad_ref[pl.ds(z * halves + h, grad.shape[0], stride=slab * halves), :] = grad[
+            rows_ref[pl.ds(z * halves + h, images, stride=pitch), :] = grad[
                 :, h * LANES : (h + 1) * LANES
             ]
+    for n in range(images):
+        grad_ref[n * slab * halves : (n + 1) * slab * halves, :] = rows_ref[
+            n * pitch : n * pitch + slab * halves, :
+        ]
 
 
 def stages(size):
@@ -447,10 +449,10 @@
 
     flops = 2 * 2 * per * rows * 2 * width * 8
     halves = width // LANES
-    x_shape = jax.ShapeDtypeStruct((pad // LANES, 2 * per * (frames + PITCH), LANES), F32)
+    x_shape = jax.ShapeDtypeStruct((pad // LANES, (2 * per + 1) * (frames + PITCH), LANES), F32)
 
     def images(steps):
-        return pltpu.VMEM((halves, tall * (2 * steps + PITCH), LANES), F32)
+        return pltpu.VMEM((halves, (tall + 1) * (2 * steps + PITCH), LANES), F32)
 
     _, b, m, k = lax.optimization_barrier((placed, images_in, maps, kdata))
     b_got, m_got, k_got = (swap(x, "cuts", 1) for x in (b, m, k))
@@ -473,7 +475,7 @@
                 jax.ShapeDtypeStruct((tall, 2 * rank, width), BF16),
                 jax.ShapeDtypeStruct((2, maps.shape[1], 2 * slab, width), BF16),
             ),
-            [pltpu.VMEM((halves, 2 * rank * (-(-slab // 8) * 8 + PITCH), LANES), F32)],
+            [pltpu.VMEM((halves, (2 * rank + 1) * (-(-slab // 8) * 8 + PITCH), LANES), F32)],
             1024 * 1024 * 1024,
             packet, images_in, b_got, maps, m_got,
         )
@@ -516,7 +518,7 @@
     (grad,) = call(
         basis_kernel,
         (jax.ShapeDtypeStruct((2 * rank * slab * halves, LANES), F32),),
-        [],
+        [pltpu.VMEM(((2 * rank + 1) * (slab * halves + PITCH), LANES), F32)],
         2 * 2 * rank * 4 * frames * slab * width * 8,
         sent, got, v_own, g, swap(theirs, "cuts", 1),
     )

time: 44 us -> 44.1 us (level)
  transfers between devices with their start and end apart: 13 -> 13, of which waited for: 8 -> 8; matrix products, arithmetic and copies ran while one was open for 1% -> 1% of each run, Pallas kernels for 7% -> 6%
where the time goes in v7:
time: 44.1 us; the launch traced here: 43.7 us
  starting transfers between devices  14.6 us (33%)
  Pallas kernels  13.3 us (30%)
  waiting for transfers between devices  12.1 us (27%)
  local copies, waits for them, and re-layouts  2.43 us (6%)
  between operations  0.83 us (2%)
    pallas_call x5, Pallas kernels, call(): pl.pallas_call(kernel, out_shape=outs, scratch_shapes=scratch, compiler_p...  13.3 us
    all_to_all x1, waiting for transfers between devices, body(): arriving = lax.all_to_all(pieces, ('cuts', 'frame'), 0, 0, tiled=True)  5.82 us
    all_to_all x1, starting transfers between devices, body(): arriving = lax.all_to_all(pieces, ('cuts', 'frame'), 0, 0, tiled=True)  5.11 us
    ppermute x9, starting transfers between devices, swap(): return lax.ppermute(value, axis, [(i, i ^ distance) for i in range(size)])  4.93 us
    ppermute x3, starting transfers between devices, collect(): got.append(lax.ppermute(packet, ('cuts', 'frame'), route))  4.52 us
    ppermute x9, waiting for transfers between devices, swap(): return lax.ppermute(value, axis, [(i, i ^ distance) for i in range(size)])  3.95 us
    ppermute x3, waiting for transfers between devices, collect(): got.append(lax.ppermute(packet, ('cuts', 'frame'), route))  2.37 us
    unnamed x10, local copies, waits for them, and re-layouts  1.39 us
  transfers between devices with their start and end apart: 13, of which 8 were waited for; matrix products, arithmetic and copies ran while one was open for 1% of the time, Pallas kernels for 6%

profile of v7, /device:TPU:0, one launch (start us, length us, event | category | flops | bytes accessed | tf_op | source)
XLA Modules:
  0.0 43.7 jit_solution(9009749584738958497)
XLA Ops:
  0.7 0.0 copy-start.4
  0.7 0.7 %copy-done.4 = s32[64,2]{0,1:T(2,128)S(1)} copy-done((s32[64,2]{0,1:T(2,128)S(1)}, s32[64,2]{0,1:T(2,128)}, u32[]{:S(2)}) %copy-start.4) | copy-done | bytes 536
  1.4 0.0 copy-start.3
  1.4 0.1 select_convert_fusion
  1.5 0.5 %collective-permute-start.4 = (bf16[64,16,256]{2,1,0:T(8,128)(2,1)}, bf16[64,16,256]{2,1,0:T(8,128)(2,1)S(1)}, u32[]{:S(2)}, u32[]{:S(2)}) collective-permute-start(bf16[64,16,256]{2,1,0:T(8,128)(2,1)} %bitcast.54), channel_id=1, source_target_pairs={{0,4},{4,0},{8,12},{12,8},{16,20},{20,16},{24,28},{28,24},{1,5},{5... | collective-permute-start | bytes 1572872 | tf_op jit(solution)/shard_map/ppermute | solution.py:355
  2.0 0.1 collective-permute-start
  2.1 0.0 copy-done.3
  2.1 0.5 %collective-permute-start.7 = (bf16[2,64,2,12]{1,2,3,0:T(2,128)(2,1)S(1)}, bf16[2,64,2,12]{1,2,3,0:T(2,128)(2,1)S(1)}, u32[]{:S(2)}, u32[]{:S(2)}) collective-permute-start(bf16[2,64,2,12]{1,2,3,0:T(2,128)(2,1)S(1)} %bitcast.70), channel_id=1, source_target_pairs={{0,4},{4,0},{8,12},{12,8},{16,20},{20,16},{24,28},{28,24},{1,5},{5... | collective-permute-start | bytes 18440 | tf_op jit(solution)/shard_map/ppermute | solution.py:355
  2.5 0.1 collective-permute-start.5
  2.6 0.0 copy-start
  2.6 0.7 %copy-done = bf16[2,32,16]{1,2,0:T(8,128)(2,1)S(1)} copy-done((bf16[2,32,16]{1,2,0:T(8,128)(2,1)S(1)}, bf16[2,32,16]{1,2,0:T(8,128)(2,1)}, u32[]{:S(2)}) %copy-start) | copy-done | bytes 2072
  3.3 0.3 collective-permute-done
  3.6 0.1 add_convert_fusion.1
  3.7 0.0 copy-start.1
  3.7 0.0 copy-start.2
  3.7 3.9 %collective-permute-start.3 = (bf16[32,64]{1,0:T(8,128)(2,1)S(1)}, bf16[32,64]{1,0:T(8,128)(2,1)S(1)}, u32[]{:S(2)}, u32[]{:S(2)}) collective-permute-start(bf16[32,64]{1,0:T(8,128)(2,1)S(1)} %broadcast_select_fusion.2.after_ref), channel_id=1, source_target_pairs={{0,24},{1,25},{2,26},{3,27},{4,7},{5,6},{6,5},{7,4},{8,16},{9,17},... | collective-permute-start | bytes 12296 | tf_op jit(solution)/shard_map/ppermute | solution.py:393
  7.6 0.5 %collective-permute-start.2 = (bf16[32,64]{1,0:T(8,128)(2,1)S(1)}, bf16[32,64]{1,0:T(8,128)(2,1)S(1)}, u32[]{:S(2)}, u32[]{:S(2)}) collective-permute-start(bf16[32,64]{1,0:T(8,128)(2,1)S(1)} %broadcast_select_fusion.2.after_ref), channel_id=1, source_target_pairs={{0,16},{1,17},{2,18},{3,19},{4,6},{5,7},{6,4},{7,5},{8,24},{9,25},... | collective-permute-start | bytes 12296 | tf_op jit(solution)/shard_map/ppermute | solution.py:393
  8.1 0.0 collective-permute-done.4.after_ref.b_got_ref
  8.1 0.1 collective-permute-start.1
  8.2 0.4 shard_map.68
  8.7 0.0 collective-permute-done.5.m_got_ref
  8.7 0.0 copy-done.1
  8.7 0.0 copy-done.2
  8.7 0.7 %shard_map.69 = (bf16[32,64,256]{2,1,0:T(8,128)(2,1)S(1)}, bf16[2,12,32,256]{3,2,1,0:T(8,128)(2,1)S(1)}) custom-call(bf16[32,64]{1,0:T(8,128)(2,1)S(1)} %broadcast_select_fusion.2.after_ref, bf16[64,16,256]{2,1,0:T(8,128)(2,1)S(1)} %bitcast.55, bf16[64,16,256]{2,1,0:T(8,128)(2,1)S(1)} %collective-permute-done.4.after_ref.b_got_ref, ...), custom_call_target="tpu_custom_call" | custom-call | flops 1073741824 | bytes 1449984 | tf_op jit(solution)/shard_map/pallas_call | solution.py:411
  9.4 0.0 collective-permute-done.3
  9.4 1.9 %collective-permute-done.2 = bf16[32,64]{1,0:T(8,128)(2,1)S(1)} collective-permute-done((bf16[32,64]{1,0:T(8,128)(2,1)S(1)}, bf16[32,64]{1,0:T(8,128)(2,1)S(1)}, u32[]{:S(2)}, u32[]{:S(2)}) %collective-permute-start.2) | collective-permute-done | bytes 4128 | tf_op jit(solution)/shard_map/ppermute | solution.py:393
  11.2 0.5 %collective-permute-done.1 = bf16[32,64]{1,0:T(8,128)(2,1)S(1)} collective-permute-done((bf16[32,64]{1,0:T(8,128)(2,1)S(1)}, bf16[32,64]{1,0:T(8,128)(2,1)S(1)}, u32[]{:S(2)}, u32[]{:S(2)}) %collective-permute-start.1) | collective-permute-done | bytes 4128 | tf_op jit(solution)/shard_map/ppermute | solution.py:393
  11.8 0.1 maximum_select_fusion.refs_0_.sent_ref
  11.8 0.3 collective-permute-start.6
  12.1 0.0 collective-permute-done.7
  12.2 0.2 copy.11
  12.3 0.1 reshape.37
  12.5 0.1 copy.12.refs_8_
  12.5 0.5 %collective-permute-done.6.refs_1_.got_ref = bf16[32,96]{1,0:T(8,128)(2,1)S(1)} collective-permute-done((bf16[32,96]{1,0:T(8,128)(2,1)S(1)}, bf16[32,96]{1,0:T(8,128)(2,1)S(1)}, u32[]{:S(2)}, u32[]{:S(2)}) %collective-permute-start.6) | collective-permute-done | bytes 6176 | tf_op jit(solution)/shard_map/ppermute | solution.py:355
  13.0 5.0 %shard_map.70 = (bf16[24,512]{1,0:T(8,128)(2,1)S(1)}, bf16[512,512]{1,0:T(8,128)(2,1)S(1)}, bf16[512,768]{1,0:T(8,128)(2,1)S(1)}) custom-call(bf16[32,96]{1,0:T(8,128)(2,1)S(1)} %maximum_select_fusion.refs_0_.sent_ref, bf16[32,96]{1,0:T(8,128)(2,1)S(1)} %collective-permute-done.6.refs_1_.got_ref, bf16[2,16,32]{2,1,0:T(8,128)(2,1)S(1)} %bitcast.52, ...), custom_call_target="tpu_custom_call" | custom-call | flops 3221225472 | bytes 1982464 | tf_op jit(solution)/shard_map/pallas_call | solution.py:411
  18.1 2.4 %collective-permute-start.10 = (bf16[24,512]{1,0:T(8,128)(2,1)S(1)}, bf16[24,512]{1,0:T(8,128)(2,1)S(1)}, u32[]{:S(2)}, u32[]{:S(2)}) collective-permute-start(bf16[24,512]{1,0:T(8,128)(2,1)S(1)} %get-tuple-element.50.refs_0_), channel_id=1, source_target_pairs={{0,24},{4,28},{8,16},{12,20},{16,8},{20,12},{24,0},{28,4},{1,25},{... | collective-permute-start | bytes 73736 | tf_op jit(solution)/shard_map/ppermute | solution.py:355
  20.5 0.5 %collective-permute-start.9 = (bf16[24,512]{1,0:T(8,128)(2,1)S(1)}, bf16[24,512]{1,0:T(8,128)(2,1)S(1)}, u32[]{:S(2)}, u32[]{:S(2)}) collective-permute-start(bf16[24,512]{1,0:T(8,128)(2,1)S(1)} %get-tuple-element.50.refs_0_), channel_id=1, source_target_pairs={{0,16},{4,20},{8,24},{12,28},{16,0},{20,4},{24,8},{28,12},{1,17},{... | collective-permute-start | bytes 73736 | tf_op jit(solution)/shard_map/ppermute | solution.py:355
  21.0 0.6 %collective-permute-start.8 = (bf16[24,512]{1,0:T(8,128)(2,1)S(1)}, bf16[24,512]{1,0:T(8,128)(2,1)S(1)}, u32[]{:S(2)}, u32[]{:S(2)}) collective-permute-start(bf16[24,512]{1,0:T(8,128)(2,1)S(1)} %get-tuple-element.50.refs_0_), channel_id=1, source_target_pairs={{0,8},{4,12},{8,0},{12,4},{16,24},{20,28},{24,16},{28,20},{1,9},{5... | collective-permute-start | bytes 73736 | tf_op jit(solution)/shard_map/ppermute | solution.py:355
  21.6 1.2 %collective-permute-done.10.refs_3_ = bf16[24,512]{1,0:T(8,128)(2,1)S(1)} collective-permute-done((bf16[24,512]{1,0:T(8,128)(2,1)S(1)}, bf16[24,512]{1,0:T(8,128)(2,1)S(1)}, u32[]{:S(2)}, u32[]{:S(2)}) %collective-permute-start.10) | collective-permute-done | bytes 24608 | tf_op jit(solution)/shard_map/ppermute | solution.py:355
  22.8 1.5 %collective-permute-done.9.refs_2_ = bf16[24,512]{1,0:T(8,128)(2,1)S(1)} collective-permute-done((bf16[24,512]{1,0:T(8,128)(2,1)S(1)}, bf16[24,512]{1,0:T(8,128)(2,1)S(1)}, u32[]{:S(2)}, u32[]{:S(2)}) %collective-permute-start.9) | collective-permute-done | bytes 24608 | tf_op jit(solution)/shard_map/ppermute | solution.py:355
  24.3 0.5 %collective-permute-done.8.refs_1_ = bf16[24,512]{1,0:T(8,128)(2,1)S(1)} collective-permute-done((bf16[24,512]{1,0:T(8,128)(2,1)S(1)}, bf16[24,512]{1,0:T(8,128)(2,1)S(1)}, u32[]{:S(2)}, u32[]{:S(2)}) %collective-permute-start.8) | collective-permute-done | bytes 24608 | tf_op jit(solution)/shard_map/ppermute | solution.py:355
  24.8 5.6 %shard_map.71 = (f32[8,4,4,128]{3,2,1,0:T(4,128)}, bf16[16,64,256]{2,1,0:T(8,128)(2,1)S(1)}, bf16[16,64,256]{2,1,0:T(8,128)(2,1)S(1)}) custom-call(bf16[24,512]{1,0:T(8,128)(2,1)S(1)} %get-tuple-element.50.refs_0_, bf16[24,512]{1,0:T(8,128)(2,1)S(1)} %collective-permute-done.8.refs_1_, bf16[24,512]{1,0:T(8,128)(2,1)S(1)} %collective-permute-done.9.refs_2_, ...), custom_call_target="tpu_custom_call" | custom-call | flops 3221225472 | bytes 2932736 | tf_op jit(solution)/shard_map/pallas_call | solution.py:411
  30.4 0.0 collective-permute-start.11
  30.4 5.1 %all-to-all-start = ((f32[32,4,128]{2,1,0:T(4,128)}), f32[32,4,128]{2,1,0:T(4,128)S(1)}, u32[]{:S(2)}, u32[]{:S(2)}) async-start(f32[32,4,128]{2,1,0:T(4,128)} %bitcast.14), calls=%async_computation | async-start | bytes 131072 | tf_op jit(solution)/shard_map/all_to_all | solution.py:549
  35.5 0.0 collective-permute-done.11.g_got_ref
  35.5 1.7 %shard_map.72 = f32[2048,128]{1,0:T(8,128)} custom-call(bf16[32,96]{1,0:T(8,128)(2,1)S(1)} %maximum_select_fusion.refs_0_.sent_ref, bf16[32,96]{1,0:T(8,128)(2,1)S(1)} %collective-permute-done.6.refs_1_.got_ref, bf16[2,16,32]{2,1,0:T(8,128)(2,1)S(1)} %bitcast.53, bf16[16,64,256]{2,1,0:T(8,128)(2,1)S(1)} %get-tuple-element.54.g_ref, ...), custom_call_target="tpu_custom_call" | custom-call | flops 536870912 | bytes 1073152 | tf_op jit(solution)/shard_map/pallas_call | solution.py:411
  37.2 5.8 %all-to-all-done = f32[32,4,128]{2,1,0:T(4,128)S(1)} async-done(((f32[32,4,128]{2,1,0:T(4,128)}), f32[32,4,128]{2,1,0:T(4,128)S(1)}, u32[]{:S(2)}, u32[]{:S(2)}) %all-to-all-start) | async-done | bytes 65568 | tf_op jit(solution)/shard_map/all_to_all | solution.py:549
  43.0 0.1 reshape.40
  43.1 0.6 %copy.13 = f32[2,32,2,2,4]{1,4,3,2,0:T(4,128)} copy(f32[2,32,2,2,4]{1,0,3,4,2:T(2,128)S(1)} %bitcast.65) | data formatting | bytes 8192 | tf_op jit(solution)/shard_map/transpose | solution.py:556
  (12 shorter events, 0.2 us)
Async XLA Ops:
  0.7 0.7 %copy-start.4 = (s32[64,2]{0,1:T(2,128)S(1)}, s32[64,2]{0,1:T(2,128)}, u32[]{:S(2)}) copy-start(s32[64,2]{0,1:T(2,128)} %param.8) | copy-start | bytes 1540
  1.4 0.7 %copy-start.3 = (bf16[2,64,2,12,1]{1,2,4,3,0:T(2,128)(2,1)S(1)}, bf16[2,64,2,12,1]{1,2,4,3,0:T(2,128)(2,1)}, u32[]{:S(2)}) copy-start(bf16[2,64,2,12,1]{1,2,4,3,0:T(2,128)(2,1)} %param.9) | copy-start | bytes 18436
  1.5 6.6 %collective-permute-start.4 = (bf16[64,16,256]{2,1,0:T(8,128)(2,1)}, bf16[64,16,256]{2,1,0:T(8,128)(2,1)S(1)}, u32[]{:S(2)}, u32[]{:S(2)}) collective-permute-start(bf16[64,16,256]{2,1,0:T(8,128)(2,1)} %bitcast.54), channel_id=1, source_target_pairs={{0,4},{4,0},{8,12},{12,8},{16,20},{20,16},{24,28},{28,24},{1,5},{5... | collective-permute-start | bytes 1572872 | tf_op jit(solution)/shard_map/ppermute | solution.py:355
  2.0 1.6 %collective-permute-start = (bf16[32,64]{1,0:T(8,128)(2,1)S(1)}, bf16[32,64]{1,0:T(8,128)(2,1)S(1)}, u32[]{:S(2)}, u32[]{:S(2)}) collective-permute-start(bf16[32,64]{1,0:T(8,128)(2,1)S(1)} %select_convert_fusion), channel_id=1, source_target_pairs={{0,4},{4,0},{8,12},{12,8},{16,20},{20,16},{24,28},{28,24},{1,5},{5... | collective-permute-start | bytes 12296 | tf_op jit(solution)/shard_map/ppermute | solution.py:355
  2.1 10.0 %collective-permute-start.7 = (bf16[2,64,2,12]{1,2,3,0:T(2,128)(2,1)S(1)}, bf16[2,64,2,12]{1,2,3,0:T(2,128)(2,1)S(1)}, u32[]{:S(2)}, u32[]{:S(2)}) collective-permute-start(bf16[2,64,2,12]{1,2,3,0:T(2,128)(2,1)S(1)} %bitcast.70), channel_id=1, source_target_pairs={{0,4},{4,0},{8,12},{12,8},{16,20},{20,16},{24,28},{28,24},{1,5},{5... | collective-permute-start | bytes 18440 | tf_op jit(solution)/shard_map/ppermute | solution.py:355
  2.5 6.1 %collective-permute-start.5 = (bf16[2,12,16,256]{3,2,1,0:T(8,128)(2,1)}, bf16[2,12,16,256]{3,2,1,0:T(8,128)(2,1)S(1)}, u32[]{:S(2)}, u32[]{:S(2)}) collective-permute-start(bf16[2,12,16,256]{3,2,1,0:T(8,128)(2,1)} %bitcast.56), channel_id=1, source_target_pairs={{0,4},{4,0},{8,12},{12,8},{16,20},{20,16},{24,28},{28,24},{1,5},{5... | collective-permute-start | bytes 589832 | tf_op jit(solution)/shard_map/ppermute | solution.py:355
  2.6 0.7 %copy-start = (bf16[2,32,16]{1,2,0:T(8,128)(2,1)S(1)}, bf16[2,32,16]{1,2,0:T(8,128)(2,1)}, u32[]{:S(2)}) copy-start(bf16[2,32,16]{1,2,0:T(8,128)(2,1)} %param.7) | copy-start | bytes 6148
  3.7 5.0 %copy-start.1 = (bf16[2,32,16,1,256]{4,2,3,1,0:T(8,128)(2,1)S(1)}, bf16[2,32,16,1,256]{4,2,3,1,0:T(8,128)(2,1)}, u32[]{:S(2)}) copy-start(bf16[2,32,16,1,256]{4,2,3,1,0:T(8,128)(2,1)} %param.5) | copy-start | bytes 1572868
  3.7 5.0 %copy-start.2 = (bf16[2,12,16,1,256]{4,2,3,1,0:T(8,128)(2,1)S(1)}, bf16[2,12,16,1,256]{4,2,3,1,0:T(8,128)(2,1)}, u32[]{:S(2)}) copy-start(bf16[2,12,16,1,256]{4,2,3,1,0:T(8,128)(2,1)} %param.6) | copy-start | bytes 589828
  3.7 5.7 %collective-permute-start.3 = (bf16[32,64]{1,0:T(8,128)(2,1)S(1)}, bf16[32,64]{1,0:T(8,128)(2,1)S(1)}, u32[]{:S(2)}, u32[]{:S(2)}) collective-permute-start(bf16[32,64]{1,0:T(8,128)(2,1)S(1)} %broadcast_select_fusion.2.after_ref), channel_id=1, source_target_pairs={{0,24},{1,25},{2,26},{3,27},{4,7},{5,6},{6,5},{7,4},{8,16},{9,17},... | collective-permute-start | bytes 12296 | tf_op jit(solution)/shard_map/ppermute | solution.py:393
  7.6 3.7 %collective-permute-start.2 = (bf16[32,64]{1,0:T(8,128)(2,1)S(1)}, bf16[32,64]{1,0:T(8,128)(2,1)S(1)}, u32[]{:S(2)}, u32[]{:S(2)}) collective-permute-start(bf16[32,64]{1,0:T(8,128)(2,1)S(1)} %broadcast_select_fusion.2.after_ref), channel_id=1, source_target_pairs={{0,16},{1,17},{2,18},{3,19},{4,6},{5,7},{6,4},{7,5},{8,24},{9,25},... | collective-permute-start | bytes 12296 | tf_op jit(solution)/shard_map/ppermute | solution.py:393
  8.1 3.7 %collective-permute-start.1 = (bf16[32,64]{1,0:T(8,128)(2,1)S(1)}, bf16[32,64]{1,0:T(8,128)(2,1)S(1)}, u32[]{:S(2)}, u32[]{:S(2)}) collective-permute-start(bf16[32,64]{1,0:T(8,128)(2,1)S(1)} %broadcast_select_fusion.2.after_ref), channel_id=1, source_target_pairs={{0,8},{1,9},{2,10},{3,11},{4,5},{5,4},{6,7},{7,6},{8,0},{9,1},{10,... | collective-permute-start | bytes 12296 | tf_op jit(solution)/shard_map/ppermute | solution.py:393
  11.8 1.2 %collective-permute-start.6 = (bf16[32,96]{1,0:T(8,128)(2,1)S(1)}, bf16[32,96]{1,0:T(8,128)(2,1)S(1)}, u32[]{:S(2)}, u32[]{:S(2)}) collective-permute-start(bf16[32,96]{1,0:T(8,128)(2,1)S(1)} %maximum_select_fusion.refs_0_.sent_ref), channel_id=1, source_target_pairs={{0,4},{4,0},{8,12},{12,8},{16,20},{20,16},{24,28},{28,24},{1,5},{5... | collective-permute-start | bytes 18440 | tf_op jit(solution)/shard_map/ppermute | solution.py:355
  18.1 4.8 %collective-permute-start.10 = (bf16[24,512]{1,0:T(8,128)(2,1)S(1)}, bf16[24,512]{1,0:T(8,128)(2,1)S(1)}, u32[]{:S(2)}, u32[]{:S(2)}) collective-permute-start(bf16[24,512]{1,0:T(8,128)(2,1)S(1)} %get-tuple-element.50.refs_0_), channel_id=1, source_target_pairs={{0,24},{4,28},{8,16},{12,20},{16,8},{20,12},{24,0},{28,4},{1,25},{... | collective-permute-start | bytes 73736 | tf_op jit(solution)/shard_map/ppermute | solution.py:355
  20.5 3.8 %collective-permute-start.9 = (bf16[24,512]{1,0:T(8,128)(2,1)S(1)}, bf16[24,512]{1,0:T(8,128)(2,1)S(1)}, u32[]{:S(2)}, u32[]{:S(2)}) collective-permute-start(bf16[24,512]{1,0:T(8,128)(2,1)S(1)} %get-tuple-element.50.refs_0_), channel_id=1, source_target_pairs={{0,16},{4,20},{8,24},{12,28},{16,0},{20,4},{24,8},{28,12},{1,17},{... | collective-permute-start | bytes 73736 | tf_op jit(solution)/shard_map/ppermute | solution.py:355
  21.0 3.8 %collective-permute-start.8 = (bf16[24,512]{1,0:T(8,128)(2,1)S(1)}, bf16[24,512]{1,0:T(8,128)(2,1)S(1)}, u32[]{:S(2)}, u32[]{:S(2)}) collective-permute-start(bf16[24,512]{1,0:T(8,128)(2,1)S(1)} %get-tuple-element.50.refs_0_), channel_id=1, source_target_pairs={{0,8},{4,12},{8,0},{12,4},{16,24},{20,28},{24,16},{28,20},{1,9},{5... | collective-permute-start | bytes 73736 | tf_op jit(solution)/shard_map/ppermute | solution.py:355
  30.4 5.1 %collective-permute-start.11 = (bf16[16,64,256]{2,1,0:T(8,128)(2,1)S(1)}, bf16[16,64,256]{2,1,0:T(8,128)(2,1)S(1)}, u32[]{:S(2)}, u32[]{:S(2)}) collective-permute-start(bf16[16,64,256]{2,1,0:T(8,128)(2,1)S(1)} %get-tuple-element.55), channel_id=1, source_target_pairs={{0,4},{4,0},{8,12},{12,8},{16,20},{20,16},{24,28},{28,24},{1,5},{5... | collective-permute-start | bytes 1572872 | tf_op jit(solution)/shard_map/ppermute | solution.py:355
  30.4 12.6 %all-to-all-start = ((f32[32,4,128]{2,1,0:T(4,128)}), f32[32,4,128]{2,1,0:T(4,128)S(1)}, u32[]{:S(2)}, u32[]{:S(2)}) async-start(f32[32,4,128]{2,1,0:T(4,128)} %bitcast.14), calls=%async_computation | async-start | bytes 131072 | tf_op jit(solution)/shard_map/all_to_all | solution.py:549

commit v8 on v7

--- a/solution.py
+++ b/solution.py
@@ -507,7 +507,7 @@
     pieces, g, theirs = call(
         functools.partial(gradient_kernel, half, frames, tall, slab, scale, len(resid_terms)),
         (
-            jax.ShapeDtypeStruct((n_cuts, n_frame, half // fold, 2 * rank * fold), F32),
+            jax.ShapeDtypeStruct((n_cuts, n_frame, half // fold, 2 * rank * fold), BF16),
             own_slab,
             own_slab,
         ),

time: 44.1 us -> 43.8 us (level)
  no operation moved by 1% of the time
where the time goes in v8:
time: 43.8 us; the launch traced here: 43.5 us
  starting transfers between devices  14.6 us (33%)
  Pallas kernels  13.3 us (30%)
  waiting for transfers between devices  11.9 us (27%)
  local copies, waits for them, and re-layouts  2.43 us (6%)
  between operations  0.83 us (2%)
    pallas_call x5, Pallas kernels, call(): pl.pallas_call(kernel, out_shape=outs, scratch_shapes=scratch, compiler_p...  13.3 us
    all_to_all x1, waiting for transfers between devices, body(): arriving = lax.all_to_all(pieces, ('cuts', 'frame'), 0, 0, tiled=True)  5.62 us
    all_to_all x1, starting transfers between devices, body(): arriving = lax.all_to_all(pieces, ('cuts', 'frame'), 0, 0, tiled=True)  5.11 us
    ppermute x9, starting transfers between devices, swap(): return lax.ppermute(value, axis, [(i, i ^ distance) for i in range(size)])  4.93 us
    ppermute x3, starting transfers between devices, collect(): got.append(lax.ppermute(packet, ('cuts', 'frame'), route))  4.52 us
    ppermute x9, waiting for transfers between devices, swap(): return lax.ppermute(value, axis, [(i, i ^ distance) for i in range(size)])  3.95 us
    ppermute x3, waiting for transfers between devices, collect(): got.append(lax.ppermute(packet, ('cuts', 'frame'), route))  2.37 us
    unnamed x10, local copies, waits for them, and re-layouts  1.39 us
  transfers between devices with their start and end apart: 13, of which 8 were waited for; matrix products, arithmetic and copies ran while one was open for 1% of the time, Pallas kernels for 6%

profile of v8, /device:TPU:0, one launch (start us, length us, event | category | flops | bytes accessed | tf_op | source)
XLA Modules:
  0.0 43.5 jit_solution(16687369621295815372)
XLA Ops:
  0.7 0.0 copy-start.4
  0.7 0.7 %copy-done.4 = s32[64,2]{0,1:T(2,128)S(1)} copy-done((s32[64,2]{0,1:T(2,128)S(1)}, s32[64,2]{0,1:T(2,128)}, u32[]{:S(2)}) %copy-start.4) | copy-done | bytes 536
  1.4 0.0 copy-start.3
  1.4 0.1 select_convert_fusion
  1.5 0.5 %collective-permute-start.4 = (bf16[64,16,256]{2,1,0:T(8,128)(2,1)}, bf16[64,16,256]{2,1,0:T(8,128)(2,1)S(1)}, u32[]{:S(2)}, u32[]{:S(2)}) collective-permute-start(bf16[64,16,256]{2,1,0:T(8,128)(2,1)} %bitcast.55), channel_id=1, source_target_pairs={{0,4},{4,0},{8,12},{12,8},{16,20},{20,16},{24,28},{28,24},{1,5},{5... | collective-permute-start | bytes 1572872 | tf_op jit(solution)/shard_map/ppermute | solution.py:355
  2.0 0.1 collective-permute-start
  2.1 0.0 copy-done.3
  2.1 0.5 %collective-permute-start.7 = (bf16[2,64,2,12]{1,2,3,0:T(2,128)(2,1)S(1)}, bf16[2,64,2,12]{1,2,3,0:T(2,128)(2,1)S(1)}, u32[]{:S(2)}, u32[]{:S(2)}) collective-permute-start(bf16[2,64,2,12]{1,2,3,0:T(2,128)(2,1)S(1)} %bitcast.71), channel_id=1, source_target_pairs={{0,4},{4,0},{8,12},{12,8},{16,20},{20,16},{24,28},{28,24},{1,5},{5... | collective-permute-start | bytes 18440 | tf_op jit(solution)/shard_map/ppermute | solution.py:355
  2.5 0.1 collective-permute-start.5
  2.6 0.0 copy-start
  2.6 0.7 %copy-done = bf16[2,32,16]{1,2,0:T(8,128)(2,1)S(1)} copy-done((bf16[2,32,16]{1,2,0:T(8,128)(2,1)S(1)}, bf16[2,32,16]{1,2,0:T(8,128)(2,1)}, u32[]{:S(2)}) %copy-start) | copy-done | bytes 2072
  3.3 0.3 collective-permute-done
  3.6 0.1 add_convert_fusion.1
  3.7 0.0 copy-start.1
  3.7 0.0 copy-start.2
  3.7 3.9 %collective-permute-start.3 = (bf16[32,64]{1,0:T(8,128)(2,1)S(1)}, bf16[32,64]{1,0:T(8,128)(2,1)S(1)}, u32[]{:S(2)}, u32[]{:S(2)}) collective-permute-start(bf16[32,64]{1,0:T(8,128)(2,1)S(1)} %broadcast_select_fusion.2.after_ref), channel_id=1, source_target_pairs={{0,24},{1,25},{2,26},{3,27},{4,7},{5,6},{6,5},{7,4},{8,16},{9,17},... | collective-permute-start | bytes 12296 | tf_op jit(solution)/shard_map/ppermute | solution.py:393
  7.6 0.5 %collective-permute-start.2 = (bf16[32,64]{1,0:T(8,128)(2,1)S(1)}, bf16[32,64]{1,0:T(8,128)(2,1)S(1)}, u32[]{:S(2)}, u32[]{:S(2)}) collective-permute-start(bf16[32,64]{1,0:T(8,128)(2,1)S(1)} %broadcast_select_fusion.2.after_ref), channel_id=1, source_target_pairs={{0,16},{1,17},{2,18},{3,19},{4,6},{5,7},{6,4},{7,5},{8,24},{9,25},... | collective-permute-start | bytes 12296 | tf_op jit(solution)/shard_map/ppermute | solution.py:393
  8.1 0.0 collective-permute-done.4.after_ref.b_got_ref
  8.1 0.1 collective-permute-start.1
  8.2 0.4 shard_map.68
  8.7 0.0 collective-permute-done.5.m_got_ref
  8.7 0.0 copy-done.1
  8.7 0.0 copy-done.2
  8.7 0.7 %shard_map.69 = (bf16[32,64,256]{2,1,0:T(8,128)(2,1)S(1)}, bf16[2,12,32,256]{3,2,1,0:T(8,128)(2,1)S(1)}) custom-call(bf16[32,64]{1,0:T(8,128)(2,1)S(1)} %broadcast_select_fusion.2.after_ref, bf16[64,16,256]{2,1,0:T(8,128)(2,1)S(1)} %bitcast.56, bf16[64,16,256]{2,1,0:T(8,128)(2,1)S(1)} %collective-permute-done.4.after_ref.b_got_ref, ...), custom_call_target="tpu_custom_call" | custom-call | flops 1073741824 | bytes 1449984 | tf_op jit(solution)/shard_map/pallas_call | solution.py:411
  9.4 0.0 collective-permute-done.3
  9.4 1.9 %collective-permute-done.2 = bf16[32,64]{1,0:T(8,128)(2,1)S(1)} collective-permute-done((bf16[32,64]{1,0:T(8,128)(2,1)S(1)}, bf16[32,64]{1,0:T(8,128)(2,1)S(1)}, u32[]{:S(2)}, u32[]{:S(2)}) %collective-permute-start.2) | collective-permute-done | bytes 4128 | tf_op jit(solution)/shard_map/ppermute | solution.py:393
  11.2 0.5 %collective-permute-done.1 = bf16[32,64]{1,0:T(8,128)(2,1)S(1)} collective-permute-done((bf16[32,64]{1,0:T(8,128)(2,1)S(1)}, bf16[32,64]{1,0:T(8,128)(2,1)S(1)}, u32[]{:S(2)}, u32[]{:S(2)}) %collective-permute-start.1) | collective-permute-done | bytes 4128 | tf_op jit(solution)/shard_map/ppermute | solution.py:393
  11.8 0.1 maximum_select_fusion.refs_0_.sent_ref
  11.8 0.3 collective-permute-start.6
  12.1 0.0 collective-permute-done.7
  12.2 0.2 copy.11
  12.3 0.1 reshape.40
  12.5 0.1 copy.12.refs_8_
  12.5 0.5 %collective-permute-done.6.refs_1_.got_ref = bf16[32,96]{1,0:T(8,128)(2,1)S(1)} collective-permute-done((bf16[32,96]{1,0:T(8,128)(2,1)S(1)}, bf16[32,96]{1,0:T(8,128)(2,1)S(1)}, u32[]{:S(2)}, u32[]{:S(2)}) %collective-permute-start.6) | collective-permute-done | bytes 6176 | tf_op jit(solution)/shard_map/ppermute | solution.py:355
  13.0 5.0 %shard_map.70 = (bf16[24,512]{1,0:T(8,128)(2,1)S(1)}, bf16[512,512]{1,0:T(8,128)(2,1)S(1)}, bf16[512,768]{1,0:T(8,128)(2,1)S(1)}) custom-call(bf16[32,96]{1,0:T(8,128)(2,1)S(1)} %maximum_select_fusion.refs_0_.sent_ref, bf16[32,96]{1,0:T(8,128)(2,1)S(1)} %collective-permute-done.6.refs_1_.got_ref, bf16[2,16,32]{2,1,0:T(8,128)(2,1)S(1)} %bitcast.53, ...), custom_call_target="tpu_custom_call" | custom-call | flops 3221225472 | bytes 1982464 | tf_op jit(solution)/shard_map/pallas_call | solution.py:411
  18.1 2.4 %collective-permute-start.10 = (bf16[24,512]{1,0:T(8,128)(2,1)S(1)}, bf16[24,512]{1,0:T(8,128)(2,1)S(1)}, u32[]{:S(2)}, u32[]{:S(2)}) collective-permute-start(bf16[24,512]{1,0:T(8,128)(2,1)S(1)} %get-tuple-element.50.refs_0_), channel_id=1, source_target_pairs={{0,24},{4,28},{8,16},{12,20},{16,8},{20,12},{24,0},{28,4},{1,25},{... | collective-permute-start | bytes 73736 | tf_op jit(solution)/shard_map/ppermute | solution.py:355
  20.5 0.5 %collective-permute-start.9 = (bf16[24,512]{1,0:T(8,128)(2,1)S(1)}, bf16[24,512]{1,0:T(8,128)(2,1)S(1)}, u32[]{:S(2)}, u32[]{:S(2)}) collective-permute-start(bf16[24,512]{1,0:T(8,128)(2,1)S(1)} %get-tuple-element.50.refs_0_), channel_id=1, source_target_pairs={{0,16},{4,20},{8,24},{12,28},{16,0},{20,4},{24,8},{28,12},{1,17},{... | collective-permute-start | bytes 73736 | tf_op jit(solution)/shard_map/ppermute | solution.py:355
  21.0 0.6 %collective-permute-start.8 = (bf16[24,512]{1,0:T(8,128)(2,1)S(1)}, bf16[24,512]{1,0:T(8,128)(2,1)S(1)}, u32[]{:S(2)}, u32[]{:S(2)}) collective-permute-start(bf16[24,512]{1,0:T(8,128)(2,1)S(1)} %get-tuple-element.50.refs_0_), channel_id=1, source_target_pairs={{0,8},{4,12},{8,0},{12,4},{16,24},{20,28},{24,16},{28,20},{1,9},{5... | collective-permute-start | bytes 73736 | tf_op jit(solution)/shard_map/ppermute | solution.py:355
  21.6 1.2 %collective-permute-done.10.refs_3_ = bf16[24,512]{1,0:T(8,128)(2,1)S(1)} collective-permute-done((bf16[24,512]{1,0:T(8,128)(2,1)S(1)}, bf16[24,512]{1,0:T(8,128)(2,1)S(1)}, u32[]{:S(2)}, u32[]{:S(2)}) %collective-permute-start.10) | collective-permute-done | bytes 24608 | tf_op jit(solution)/shard_map/ppermute | solution.py:355
  22.8 1.5 %collective-permute-done.9.refs_2_ = bf16[24,512]{1,0:T(8,128)(2,1)S(1)} collective-permute-done((bf16[24,512]{1,0:T(8,128)(2,1)S(1)}, bf16[24,512]{1,0:T(8,128)(2,1)S(1)}, u32[]{:S(2)}, u32[]{:S(2)}) %collective-permute-start.9) | collective-permute-done | bytes 24608 | tf_op jit(solution)/shard_map/ppermute | solution.py:355
  24.3 0.5 %collective-permute-done.8.refs_1_ = bf16[24,512]{1,0:T(8,128)(2,1)S(1)} collective-permute-done((bf16[24,512]{1,0:T(8,128)(2,1)S(1)}, bf16[24,512]{1,0:T(8,128)(2,1)S(1)}, u32[]{:S(2)}, u32[]{:S(2)}) %collective-permute-start.8) | collective-permute-done | bytes 24608 | tf_op jit(solution)/shard_map/ppermute | solution.py:355
  24.8 5.5 %shard_map.71 = (bf16[8,4,4,128]{3,2,1,0:T(4,128)(2,1)}, bf16[16,64,256]{2,1,0:T(8,128)(2,1)S(1)}, bf16[16,64,256]{2,1,0:T(8,128)(2,1)S(1)}) custom-call(bf16[24,512]{1,0:T(8,128)(2,1)S(1)} %get-tuple-element.50.refs_0_, bf16[24,512]{1,0:T(8,128)(2,1)S(1)} %collective-permute-done.8.refs_1_, bf16[24,512]{1,0:T(8,128)(2,1)S(1)} %collective-permute-done.9.refs_2_, ...), custom_call_target="tpu_custom_call" | custom-call | flops 3221225472 | bytes 2932736 | tf_op jit(solution)/shard_map/pallas_call | solution.py:411
  30.4 0.0 collective-permute-start.11
  30.4 5.1 %all-to-all-start = ((bf16[32,4,128]{2,1,0:T(4,128)(2,1)}), bf16[32,4,128]{2,1,0:T(4,128)(2,1)S(1)}, u32[]{:S(2)}, u32[]{:S(2)}) async-start(bf16[32,4,128]{2,1,0:T(4,128)(2,1)} %bitcast.14), calls=%async_computation | async-start | bytes 65536 | tf_op jit(solution)/shard_map/all_to_all | solution.py:549
  35.5 0.0 collective-permute-done.11.g_got_ref
  35.5 1.7 %shard_map.72 = f32[2048,128]{1,0:T(8,128)} custom-call(bf16[32,96]{1,0:T(8,128)(2,1)S(1)} %maximum_select_fusion.refs_0_.sent_ref, bf16[32,96]{1,0:T(8,128)(2,1)S(1)} %collective-permute-done.6.refs_1_.got_ref, bf16[2,16,32]{2,1,0:T(8,128)(2,1)S(1)} %bitcast.54, bf16[16,64,256]{2,1,0:T(8,128)(2,1)S(1)} %get-tuple-element.54.g_ref, ...), custom_call_target="tpu_custom_call" | custom-call | flops 536870912 | bytes 1073152 | tf_op jit(solution)/shard_map/pallas_call | solution.py:411
  37.1 5.6 %all-to-all-done = bf16[32,4,128]{2,1,0:T(4,128)(2,1)S(1)} async-done(((bf16[32,4,128]{2,1,0:T(4,128)(2,1)}), bf16[32,4,128]{2,1,0:T(4,128)(2,1)S(1)}, u32[]{:S(2)}, u32[]{:S(2)}) %all-to-all-start) | async-done | bytes 32800 | tf_op jit(solution)/shard_map/all_to_all | solution.py:549
  42.8 0.1 reshape.44
  42.9 0.6 %copy.13 = f32[2,32,2,2,4]{1,4,3,2,0:T(4,128)} copy(f32[2,32,2,2,4]{1,0,3,4,2:T(2,128)S(1)} %bitcast.66) | data formatting | bytes 8192 | tf_op jit(solution)/shard_map/transpose | solution.py:556
  (12 shorter events, 0.2 us)
Async XLA Ops:
  0.7 0.7 %copy-start.4 = (s32[64,2]{0,1:T(2,128)S(1)}, s32[64,2]{0,1:T(2,128)}, u32[]{:S(2)}) copy-start(s32[64,2]{0,1:T(2,128)} %param.8) | copy-start | bytes 1540
  1.4 0.7 %copy-start.3 = (bf16[2,64,2,12,1]{1,2,4,3,0:T(2,128)(2,1)S(1)}, bf16[2,64,2,12,1]{1,2,4,3,0:T(2,128)(2,1)}, u32[]{:S(2)}) copy-start(bf16[2,64,2,12,1]{1,2,4,3,0:T(2,128)(2,1)} %param.9) | copy-start | bytes 18436
  1.5 6.6 %collective-permute-start.4 = (bf16[64,16,256]{2,1,0:T(8,128)(2,1)}, bf16[64,16,256]{2,1,0:T(8,128)(2,1)S(1)}, u32[]{:S(2)}, u32[]{:S(2)}) collective-permute-start(bf16[64,16,256]{2,1,0:T(8,128)(2,1)} %bitcast.55), channel_id=1, source_target_pairs={{0,4},{4,0},{8,12},{12,8},{16,20},{20,16},{24,28},{28,24},{1,5},{5... | collective-permute-start | bytes 1572872 | tf_op jit(solution)/shard_map/ppermute | solution.py:355
  2.0 1.6 %collective-permute-start = (bf16[32,64]{1,0:T(8,128)(2,1)S(1)}, bf16[32,64]{1,0:T(8,128)(2,1)S(1)}, u32[]{:S(2)}, u32[]{:S(2)}) collective-permute-start(bf16[32,64]{1,0:T(8,128)(2,1)S(1)} %select_convert_fusion), channel_id=1, source_target_pairs={{0,4},{4,0},{8,12},{12,8},{16,20},{20,16},{24,28},{28,24},{1,5},{5... | collective-permute-start | bytes 12296 | tf_op jit(solution)/shard_map/ppermute | solution.py:355
  2.1 10.0 %collective-permute-start.7 = (bf16[2,64,2,12]{1,2,3,0:T(2,128)(2,1)S(1)}, bf16[2,64,2,12]{1,2,3,0:T(2,128)(2,1)S(1)}, u32[]{:S(2)}, u32[]{:S(2)}) collective-permute-start(bf16[2,64,2,12]{1,2,3,0:T(2,128)(2,1)S(1)} %bitcast.71), channel_id=1, source_target_pairs={{0,4},{4,0},{8,12},{12,8},{16,20},{20,16},{24,28},{28,24},{1,5},{5... | collective-permute-start | bytes 18440 | tf_op jit(solution)/shard_map/ppermute | solution.py:355
  2.5 6.1 %collective-permute-start.5 = (bf16[2,12,16,256]{3,2,1,0:T(8,128)(2,1)}, bf16[2,12,16,256]{3,2,1,0:T(8,128)(2,1)S(1)}, u32[]{:S(2)}, u32[]{:S(2)}) collective-permute-start(bf16[2,12,16,256]{3,2,1,0:T(8,128)(2,1)} %bitcast.57), channel_id=1, source_target_pairs={{0,4},{4,0},{8,12},{12,8},{16,20},{20,16},{24,28},{28,24},{1,5},{5... | collective-permute-start | bytes 589832 | tf_op jit(solution)/shard_map/ppermute | solution.py:355
  2.6 0.7 %copy-start = (bf16[2,32,16]{1,2,0:T(8,128)(2,1)S(1)}, bf16[2,32,16]{1,2,0:T(8,128)(2,1)}, u32[]{:S(2)}) copy-start(bf16[2,32,16]{1,2,0:T(8,128)(2,1)} %param.7) | copy-start | bytes 6148
  3.7 5.0 %copy-start.1 = (bf16[2,32,16,1,256]{4,2,3,1,0:T(8,128)(2,1)S(1)}, bf16[2,32,16,1,256]{4,2,3,1,0:T(8,128)(2,1)}, u32[]{:S(2)}) copy-start(bf16[2,32,16,1,256]{4,2,3,1,0:T(8,128)(2,1)} %param.5) | copy-start | bytes 1572868
  3.7 5.0 %copy-start.2 = (bf16[2,12,16,1,256]{4,2,3,1,0:T(8,128)(2,1)S(1)}, bf16[2,12,16,1,256]{4,2,3,1,0:T(8,128)(2,1)}, u32[]{:S(2)}) copy-start(bf16[2,12,16,1,256]{4,2,3,1,0:T(8,128)(2,1)} %param.6) | copy-start | bytes 589828
  3.7 5.7 %collective-permute-start.3 = (bf16[32,64]{1,0:T(8,128)(2,1)S(1)}, bf16[32,64]{1,0:T(8,128)(2,1)S(1)}, u32[]{:S(2)}, u32[]{:S(2)}) collective-permute-start(bf16[32,64]{1,0:T(8,128)(2,1)S(1)} %broadcast_select_fusion.2.after_ref), channel_id=1, source_target_pairs={{0,24},{1,25},{2,26},{3,27},{4,7},{5,6},{6,5},{7,4},{8,16},{9,17},... | collective-permute-start | bytes 12296 | tf_op jit(solution)/shard_map/ppermute | solution.py:393
  7.6 3.7 %collective-permute-start.2 = (bf16[32,64]{1,0:T(8,128)(2,1)S(1)}, bf16[32,64]{1,0:T(8,128)(2,1)S(1)}, u32[]{:S(2)}, u32[]{:S(2)}) collective-permute-start(bf16[32,64]{1,0:T(8,128)(2,1)S(1)} %broadcast_select_fusion.2.after_ref), channel_id=1, source_target_pairs={{0,16},{1,17},{2,18},{3,19},{4,6},{5,7},{6,4},{7,5},{8,24},{9,25},... | collective-permute-start | bytes 12296 | tf_op jit(solution)/shard_map/ppermute | solution.py:393
  8.1 3.7 %collective-permute-start.1 = (bf16[32,64]{1,0:T(8,128)(2,1)S(1)}, bf16[32,64]{1,0:T(8,128)(2,1)S(1)}, u32[]{:S(2)}, u32[]{:S(2)}) collective-permute-start(bf16[32,64]{1,0:T(8,128)(2,1)S(1)} %broadcast_select_fusion.2.after_ref), channel_id=1, source_target_pairs={{0,8},{1,9},{2,10},{3,11},{4,5},{5,4},{6,7},{7,6},{8,0},{9,1},{10,... | collective-permute-start | bytes 12296 | tf_op jit(solution)/shard_map/ppermute | solution.py:393
  11.8 1.2 %collective-permute-start.6 = (bf16[32,96]{1,0:T(8,128)(2,1)S(1)}, bf16[32,96]{1,0:T(8,128)(2,1)S(1)}, u32[]{:S(2)}, u32[]{:S(2)}) collective-permute-start(bf16[32,96]{1,0:T(8,128)(2,1)S(1)} %maximum_select_fusion.refs_0_.sent_ref), channel_id=1, source_target_pairs={{0,4},{4,0},{8,12},{12,8},{16,20},{20,16},{24,28},{28,24},{1,5},{5... | collective-permute-start | bytes 18440 | tf_op jit(solution)/shard_map/ppermute | solution.py:355
  18.1 4.8 %collective-permute-start.10 = (bf16[24,512]{1,0:T(8,128)(2,1)S(1)}, bf16[24,512]{1,0:T(8,128)(2,1)S(1)}, u32[]{:S(2)}, u32[]{:S(2)}) collective-permute-start(bf16[24,512]{1,0:T(8,128)(2,1)S(1)} %get-tuple-element.50.refs_0_), channel_id=1, source_target_pairs={{0,24},{4,28},{8,16},{12,20},{16,8},{20,12},{24,0},{28,4},{1,25},{... | collective-permute-start | bytes 73736 | tf_op jit(solution)/shard_map/ppermute | solution.py:355
  20.5 3.8 %collective-permute-start.9 = (bf16[24,512]{1,0:T(8,128)(2,1)S(1)}, bf16[24,512]{1,0:T(8,128)(2,1)S(1)}, u32[]{:S(2)}, u32[]{:S(2)}) collective-permute-start(bf16[24,512]{1,0:T(8,128)(2,1)S(1)} %get-tuple-element.50.refs_0_), channel_id=1, source_target_pairs={{0,16},{4,20},{8,24},{12,28},{16,0},{20,4},{24,8},{28,12},{1,17},{... | collective-permute-start | bytes 73736 | tf_op jit(solution)/shard_map/ppermute | solution.py:355
  21.0 3.8 %collective-permute-start.8 = (bf16[24,512]{1,0:T(8,128)(2,1)S(1)}, bf16[24,512]{1,0:T(8,128)(2,1)S(1)}, u32[]{:S(2)}, u32[]{:S(2)}) collective-permute-start(bf16[24,512]{1,0:T(8,128)(2,1)S(1)} %get-tuple-element.50.refs_0_), channel_id=1, source_target_pairs={{0,8},{4,12},{8,0},{12,4},{16,24},{20,28},{24,16},{28,20},{1,9},{5... | collective-permute-start | bytes 73736 | tf_op jit(solution)/shard_map/ppermute | solution.py:355
  30.4 5.1 %collective-permute-start.11 = (bf16[16,64,256]{2,1,0:T(8,128)(2,1)S(1)}, bf16[16,64,256]{2,1,0:T(8,128)(2,1)S(1)}, u32[]{:S(2)}, u32[]{:S(2)}) collective-permute-start(bf16[16,64,256]{2,1,0:T(8,128)(2,1)S(1)} %get-tuple-element.55), channel_id=1, source_target_pairs={{0,4},{4,0},{8,12},{12,8},{16,20},{20,16},{24,28},{28,24},{1,5},{5... | collective-permute-start | bytes 1572872 | tf_op jit(solution)/shard_map/ppermute | solution.py:355
  30.4 12.4 %all-to-all-start = ((bf16[32,4,128]{2,1,0:T(4,128)(2,1)}), bf16[32,4,128]{2,1,0:T(4,128)(2,1)S(1)}, u32[]{:S(2)}, u32[]{:S(2)}) async-start(bf16[32,4,128]{2,1,0:T(4,128)(2,1)} %bitcast.14), calls=%async_computation | async-start | bytes 65536 | tf_op jit(solution)/shard_map/all_to_all | solution.py:549

commit v9 on v8

--- a/solution.py
+++ b/solution.py
@@ -360,7 +360,7 @@
     for number, (stride, radix) in enumerate(steps):
         if number + last == len(steps) + 1:
             return value
-        terms = [value] + [swap(value, axis, stride * d) for d in range(1, radix)]
+        terms = [value] + [swap(value, axis, stride * d) for d in range(radix - 1, 0, -1)][::-1]
         if number + 1 < len(steps):
             value = pairs([term.astype(F32) for term in terms]).astype(value.dtype)
     return terms

time: 43.8 us -> 43.8 us (level)
  no operation moved by 1% of the time
where the time goes in v9:
time: 43.8 us; the launch traced here: 43.5 us
  starting transfers between devices  14.6 us (33%)
  Pallas kernels  13.3 us (30%)
  waiting for transfers between devices  11.9 us (27%)
  local copies, waits for them, and re-layouts  2.43 us (6%)
  between operations  0.83 us (2%)
    pallas_call x5, Pallas kernels, call(): pl.pallas_call(kernel, out_shape=outs, scratch_shapes=scratch, compiler_p...  13.3 us
    all_to_all x1, waiting for transfers between devices, body(): arriving = lax.all_to_all(pieces, ('cuts', 'frame'), 0, 0, tiled=True)  5.62 us
    all_to_all x1, starting transfers between devices, body(): arriving = lax.all_to_all(pieces, ('cuts', 'frame'), 0, 0, tiled=True)  5.11 us
    ppermute x9, starting transfers between devices, swap(): return lax.ppermute(value, axis, [(i, i ^ distance) for i in range(size)])  4.93 us
    ppermute x3, starting transfers between devices, collect(): got.append(lax.ppermute(packet, ('cuts', 'frame'), route))  4.52 us
    ppermute x9, waiting for transfers between devices, swap(): return lax.ppermute(value, axis, [(i, i ^ distance) for i in range(size)])  3.95 us
    ppermute x3, waiting for transfers between devices, collect(): got.append(lax.ppermute(packet, ('cuts', 'frame'), route))  2.37 us
    unnamed x10, local copies, waits for them, and re-layouts  1.39 us
  transfers between devices with their start and end apart: 13, of which 8 were waited for; matrix products, arithmetic and copies ran while one was open for 1% of the time, Pallas kernels for 6%

profile of v9, /device:TPU:0, one launch (start us, length us, event | category | flops | bytes accessed | tf_op | source)
XLA Modules:
  0.0 43.5 jit_solution(16687369621295815372)
XLA Ops:
  0.7 0.0 copy-start.4
  0.7 0.7 %copy-done.4 = s32[64,2]{0,1:T(2,128)S(1)} copy-done((s32[64,2]{0,1:T(2,128)S(1)}, s32[64,2]{0,1:T(2,128)}, u32[]{:S(2)}) %copy-start.4) | copy-done | bytes 536
  1.4 0.0 copy-start.3
  1.4 0.1 select_convert_fusion
  1.5 0.5 %collective-permute-start.4 = (bf16[64,16,256]{2,1,0:T(8,128)(2,1)}, bf16[64,16,256]{2,1,0:T(8,128)(2,1)S(1)}, u32[]{:S(2)}, u32[]{:S(2)}) collective-permute-start(bf16[64,16,256]{2,1,0:T(8,128)(2,1)} %bitcast.55), channel_id=1, source_target_pairs={{0,4},{4,0},{8,12},{12,8},{16,20},{20,16},{24,28},{28,24},{1,5},{5... | collective-permute-start | bytes 1572872 | tf_op jit(solution)/shard_map/ppermute | solution.py:355
  2.0 0.1 collective-permute-start
  2.1 0.0 copy-done.3
  2.1 0.5 %collective-permute-start.7 = (bf16[2,64,2,12]{1,2,3,0:T(2,128)(2,1)S(1)}, bf16[2,64,2,12]{1,2,3,0:T(2,128)(2,1)S(1)}, u32[]{:S(2)}, u32[]{:S(2)}) collective-permute-start(bf16[2,64,2,12]{1,2,3,0:T(2,128)(2,1)S(1)} %bitcast.71), channel_id=1, source_target_pairs={{0,4},{4,0},{8,12},{12,8},{16,20},{20,16},{24,28},{28,24},{1,5},{5... | collective-permute-start | bytes 18440 | tf_op jit(solution)/shard_map/ppermute | solution.py:355
  2.5 0.1 collective-permute-start.5
  2.6 0.0 copy-start
  2.6 0.7 %copy-done = bf16[2,32,16]{1,2,0:T(8,128)(2,1)S(1)} copy-done((bf16[2,32,16]{1,2,0:T(8,128)(2,1)S(1)}, bf16[2,32,16]{1,2,0:T(8,128)(2,1)}, u32[]{:S(2)}) %copy-start) | copy-done | bytes 2072
  3.3 0.3 collective-permute-done
  3.6 0.1 add_convert_fusion.1
  3.7 0.0 copy-start.1
  3.7 0.0 copy-start.2
  3.7 3.9 %collective-permute-start.3 = (bf16[32,64]{1,0:T(8,128)(2,1)S(1)}, bf16[32,64]{1,0:T(8,128)(2,1)S(1)}, u32[]{:S(2)}, u32[]{:S(2)}) collective-permute-start(bf16[32,64]{1,0:T(8,128)(2,1)S(1)} %broadcast_select_fusion.2.after_ref), channel_id=1, source_target_pairs={{0,24},{1,25},{2,26},{3,27},{4,7},{5,6},{6,5},{7,4},{8,16},{9,17},... | collective-permute-start | bytes 12296 | tf_op jit(solution)/shard_map/ppermute | solution.py:393
  7.6 0.5 %collective-permute-start.2 = (bf16[32,64]{1,0:T(8,128)(2,1)S(1)}, bf16[32,64]{1,0:T(8,128)(2,1)S(1)}, u32[]{:S(2)}, u32[]{:S(2)}) collective-permute-start(bf16[32,64]{1,0:T(8,128)(2,1)S(1)} %broadcast_select_fusion.2.after_ref), channel_id=1, source_target_pairs={{0,16},{1,17},{2,18},{3,19},{4,6},{5,7},{6,4},{7,5},{8,24},{9,25},... | collective-permute-start | bytes 12296 | tf_op jit(solution)/shard_map/ppermute | solution.py:393
  8.1 0.0 collective-permute-done.4.after_ref.b_got_ref
  8.1 0.1 collective-permute-start.1
  8.2 0.4 shard_map.68
  8.7 0.0 collective-permute-done.5.m_got_ref
  8.7 0.0 copy-done.1
  8.7 0.0 copy-done.2
  8.7 0.7 %shard_map.69 = (bf16[32,64,256]{2,1,0:T(8,128)(2,1)S(1)}, bf16[2,12,32,256]{3,2,1,0:T(8,128)(2,1)S(1)}) custom-call(bf16[32,64]{1,0:T(8,128)(2,1)S(1)} %broadcast_select_fusion.2.after_ref, bf16[64,16,256]{2,1,0:T(8,128)(2,1)S(1)} %bitcast.56, bf16[64,16,256]{2,1,0:T(8,128)(2,1)S(1)} %collective-permute-done.4.after_ref.b_got_ref, ...), custom_call_target="tpu_custom_call" | custom-call | flops 1073741824 | bytes 1449984 | tf_op jit(solution)/shard_map/pallas_call | solution.py:411
  9.4 0.0 collective-permute-done.3
  9.4 1.9 %collective-permute-done.2 = bf16[32,64]{1,0:T(8,128)(2,1)S(1)} collective-permute-done((bf16[32,64]{1,0:T(8,128)(2,1)S(1)}, bf16[32,64]{1,0:T(8,128)(2,1)S(1)}, u32[]{:S(2)}, u32[]{:S(2)}) %collective-permute-start.2) | collective-permute-done | bytes 4128 | tf_op jit(solution)/shard_map/ppermute | solution.py:393
  11.2 0.5 %collective-permute-done.1 = bf16[32,64]{1,0:T(8,128)(2,1)S(1)} collective-permute-done((bf16[32,64]{1,0:T(8,128)(2,1)S(1)}, bf16[32,64]{1,0:T(8,128)(2,1)S(1)}, u32[]{:S(2)}, u32[]{:S(2)}) %collective-permute-start.1) | collective-permute-done | bytes 4128 | tf_op jit(solution)/shard_map/ppermute | solution.py:393
  11.8 0.1 maximum_select_fusion.refs_0_.sent_ref
  11.8 0.3 collective-permute-start.6
  12.1 0.0 collective-permute-done.7
  12.2 0.2 copy.11
  12.3 0.1 reshape.40
  12.5 0.1 copy.12.refs_8_
  12.5 0.5 %collective-permute-done.6.refs_1_.got_ref = bf16[32,96]{1,0:T(8,128)(2,1)S(1)} collective-permute-done((bf16[32,96]{1,0:T(8,128)(2,1)S(1)}, bf16[32,96]{1,0:T(8,128)(2,1)S(1)}, u32[]{:S(2)}, u32[]{:S(2)}) %collective-permute-start.6) | collective-permute-done | bytes 6176 | tf_op jit(solution)/shard_map/ppermute | solution.py:355
  13.0 5.0 %shard_map.70 = (bf16[24,512]{1,0:T(8,128)(2,1)S(1)}, bf16[512,512]{1,0:T(8,128)(2,1)S(1)}, bf16[512,768]{1,0:T(8,128)(2,1)S(1)}) custom-call(bf16[32,96]{1,0:T(8,128)(2,1)S(1)} %maximum_select_fusion.refs_0_.sent_ref, bf16[32,96]{1,0:T(8,128)(2,1)S(1)} %collective-permute-done.6.refs_1_.got_ref, bf16[2,16,32]{2,1,0:T(8,128)(2,1)S(1)} %bitcast.53, ...), custom_call_target="tpu_custom_call" | custom-call | flops 3221225472 | bytes 1982464 | tf_op jit(solution)/shard_map/pallas_call | solution.py:411
  18.1 2.4 %collective-permute-start.10 = (bf16[24,512]{1,0:T(8,128)(2,1)S(1)}, bf16[24,512]{1,0:T(8,128)(2,1)S(1)}, u32[]{:S(2)}, u32[]{:S(2)}) collective-permute-start(bf16[24,512]{1,0:T(8,128)(2,1)S(1)} %get-tuple-element.50.refs_0_), channel_id=1, source_target_pairs={{0,24},{4,28},{8,16},{12,20},{16,8},{20,12},{24,0},{28,4},{1,25},{... | collective-permute-start | bytes 73736 | tf_op jit(solution)/shard_map/ppermute | solution.py:355
  20.5 0.5 %collective-permute-start.9 = (bf16[24,512]{1,0:T(8,128)(2,1)S(1)}, bf16[24,512]{1,0:T(8,128)(2,1)S(1)}, u32[]{:S(2)}, u32[]{:S(2)}) collective-permute-start(bf16[24,512]{1,0:T(8,128)(2,1)S(1)} %get-tuple-element.50.refs_0_), channel_id=1, source_target_pairs={{0,16},{4,20},{8,24},{12,28},{16,0},{20,4},{24,8},{28,12},{1,17},{... | collective-permute-start | bytes 73736 | tf_op jit(solution)/shard_map/ppermute | solution.py:355
  21.0 0.6 %collective-permute-start.8 = (bf16[24,512]{1,0:T(8,128)(2,1)S(1)}, bf16[24,512]{1,0:T(8,128)(2,1)S(1)}, u32[]{:S(2)}, u32[]{:S(2)}) collective-permute-start(bf16[24,512]{1,0:T(8,128)(2,1)S(1)} %get-tuple-element.50.refs_0_), channel_id=1, source_target_pairs={{0,8},{4,12},{8,0},{12,4},{16,24},{20,28},{24,16},{28,20},{1,9},{5... | collective-permute-start | bytes 73736 | tf_op jit(solution)/shard_map/ppermute | solution.py:355
  21.6 1.2 %collective-permute-done.10.refs_3_ = bf16[24,512]{1,0:T(8,128)(2,1)S(1)} collective-permute-done((bf16[24,512]{1,0:T(8,128)(2,1)S(1)}, bf16[24,512]{1,0:T(8,128)(2,1)S(1)}, u32[]{:S(2)}, u32[]{:S(2)}) %collective-permute-start.10) | collective-permute-done | bytes 24608 | tf_op jit(solution)/shard_map/ppermute | solution.py:355
  22.8 1.5 %collective-permute-done.9.refs_2_ = bf16[24,512]{1,0:T(8,128)(2,1)S(1)} collective-permute-done((bf16[24,512]{1,0:T(8,128)(2,1)S(1)}, bf16[24,512]{1,0:T(8,128)(2,1)S(1)}, u32[]{:S(2)}, u32[]{:S(2)}) %collective-permute-start.9) | collective-permute-done | bytes 24608 | tf_op jit(solution)/shard_map/ppermute | solution.py:355
  24.3 0.5 %collective-permute-done.8.refs_1_ = bf16[24,512]{1,0:T(8,128)(2,1)S(1)} collective-permute-done((bf16[24,512]{1,0:T(8,128)(2,1)S(1)}, bf16[24,512]{1,0:T(8,128)(2,1)S(1)}, u32[]{:S(2)}, u32[]{:S(2)}) %collective-permute-start.8) | collective-permute-done | bytes 24608 | tf_op jit(solution)/shard_map/ppermute | solution.py:355
  24.8 5.5 %shard_map.71 = (bf16[8,4,4,128]{3,2,1,0:T(4,128)(2,1)}, bf16[16,64,256]{2,1,0:T(8,128)(2,1)S(1)}, bf16[16,64,256]{2,1,0:T(8,128)(2,1)S(1)}) custom-call(bf16[24,512]{1,0:T(8,128)(2,1)S(1)} %get-tuple-element.50.refs_0_, bf16[24,512]{1,0:T(8,128)(2,1)S(1)} %collective-permute-done.8.refs_1_, bf16[24,512]{1,0:T(8,128)(2,1)S(1)} %collective-permute-done.9.refs_2_, ...), custom_call_target="tpu_custom_call" | custom-call | flops 3221225472 | bytes 2932736 | tf_op jit(solution)/shard_map/pallas_call | solution.py:411
  30.4 0.0 collective-permute-start.11
  30.4 5.1 %all-to-all-start = ((bf16[32,4,128]{2,1,0:T(4,128)(2,1)}), bf16[32,4,128]{2,1,0:T(4,128)(2,1)S(1)}, u32[]{:S(2)}, u32[]{:S(2)}) async-start(bf16[32,4,128]{2,1,0:T(4,128)(2,1)} %bitcast.14), calls=%async_computation | async-start | bytes 65536 | tf_op jit(solution)/shard_map/all_to_all | solution.py:549
  35.5 0.0 collective-permute-done.11.g_got_ref
  35.5 1.7 %shard_map.72 = f32[2048,128]{1,0:T(8,128)} custom-call(bf16[32,96]{1,0:T(8,128)(2,1)S(1)} %maximum_select_fusion.refs_0_.sent_ref, bf16[32,96]{1,0:T(8,128)(2,1)S(1)} %collective-permute-done.6.refs_1_.got_ref, bf16[2,16,32]{2,1,0:T(8,128)(2,1)S(1)} %bitcast.54, bf16[16,64,256]{2,1,0:T(8,128)(2,1)S(1)} %get-tuple-element.54.g_ref, ...), custom_call_target="tpu_custom_call" | custom-call | flops 536870912 | bytes 1073152 | tf_op jit(solution)/shard_map/pallas_call | solution.py:411
  37.1 5.6 %all-to-all-done = bf16[32,4,128]{2,1,0:T(4,128)(2,1)S(1)} async-done(((bf16[32,4,128]{2,1,0:T(4,128)(2,1)}), bf16[32,4,128]{2,1,0:T(4,128)(2,1)S(1)}, u32[]{:S(2)}, u32[]{:S(2)}) %all-to-all-start) | async-done | bytes 32800 | tf_op jit(solution)/shard_map/all_to_all | solution.py:549
  42.8 0.1 reshape.44
  42.9 0.6 %copy.13 = f32[2,32,2,2,4]{1,4,3,2,0:T(4,128)} copy(f32[2,32,2,2,4]{1,0,3,4,2:T(2,128)S(1)} %bitcast.66) | data formatting | bytes 8192 | tf_op jit(solution)/shard_map/transpose | solution.py:556
  (12 shorter events, 0.2 us)
Async XLA Ops:
  0.7 0.7 %copy-start.4 = (s32[64,2]{0,1:T(2,128)S(1)}, s32[64,2]{0,1:T(2,128)}, u32[]{:S(2)}) copy-start(s32[64,2]{0,1:T(2,128)} %param.8) | copy-start | bytes 1540
  1.4 0.7 %copy-start.3 = (bf16[2,64,2,12,1]{1,2,4,3,0:T(2,128)(2,1)S(1)}, bf16[2,64,2,12,1]{1,2,4,3,0:T(2,128)(2,1)}, u32[]{:S(2)}) copy-start(bf16[2,64,2,12,1]{1,2,4,3,0:T(2,128)(2,1)} %param.9) | copy-start | bytes 18436
  1.5 6.6 %collective-permute-start.4 = (bf16[64,16,256]{2,1,0:T(8,128)(2,1)}, bf16[64,16,256]{2,1,0:T(8,128)(2,1)S(1)}, u32[]{:S(2)}, u32[]{:S(2)}) collective-permute-start(bf16[64,16,256]{2,1,0:T(8,128)(2,1)} %bitcast.55), channel_id=1, source_target_pairs={{0,4},{4,0},{8,12},{12,8},{16,20},{20,16},{24,28},{28,24},{1,5},{5... | collective-permute-start | bytes 1572872 | tf_op jit(solution)/shard_map/ppermute | solution.py:355
  2.0 1.6 %collective-permute-start = (bf16[32,64]{1,0:T(8,128)(2,1)S(1)}, bf16[32,64]{1,0:T(8,128)(2,1)S(1)}, u32[]{:S(2)}, u32[]{:S(2)}) collective-permute-start(bf16[32,64]{1,0:T(8,128)(2,1)S(1)} %select_convert_fusion), channel_id=1, source_target_pairs={{0,4},{4,0},{8,12},{12,8},{16,20},{20,16},{24,28},{28,24},{1,5},{5... | collective-permute-start | bytes 12296 | tf_op jit(solution)/shard_map/ppermute | solution.py:355
  2.1 10.0 %collective-permute-start.7 = (bf16[2,64,2,12]{1,2,3,0:T(2,128)(2,1)S(1)}, bf16[2,64,2,12]{1,2,3,0:T(2,128)(2,1)S(1)}, u32[]{:S(2)}, u32[]{:S(2)}) collective-permute-start(bf16[2,64,2,12]{1,2,3,0:T(2,128)(2,1)S(1)} %bitcast.71), channel_id=1, source_target_pairs={{0,4},{4,0},{8,12},{12,8},{16,20},{20,16},{24,28},{28,24},{1,5},{5... | collective-permute-start | bytes 18440 | tf_op jit(solution)/shard_map/ppermute | solution.py:355
  2.5 6.1 %collective-permute-start.5 = (bf16[2,12,16,256]{3,2,1,0:T(8,128)(2,1)}, bf16[2,12,16,256]{3,2,1,0:T(8,128)(2,1)S(1)}, u32[]{:S(2)}, u32[]{:S(2)}) collective-permute-start(bf16[2,12,16,256]{3,2,1,0:T(8,128)(2,1)} %bitcast.57), channel_id=1, source_target_pairs={{0,4},{4,0},{8,12},{12,8},{16,20},{20,16},{24,28},{28,24},{1,5},{5... | collective-permute-start | bytes 589832 | tf_op jit(solution)/shard_map/ppermute | solution.py:355
  2.6 0.7 %copy-start = (bf16[2,32,16]{1,2,0:T(8,128)(2,1)S(1)}, bf16[2,32,16]{1,2,0:T(8,128)(2,1)}, u32[]{:S(2)}) copy-start(bf16[2,32,16]{1,2,0:T(8,128)(2,1)} %param.7) | copy-start | bytes 6148
  3.7 5.0 %copy-start.1 = (bf16[2,32,16,1,256]{4,2,3,1,0:T(8,128)(2,1)S(1)}, bf16[2,32,16,1,256]{4,2,3,1,0:T(8,128)(2,1)}, u32[]{:S(2)}) copy-start(bf16[2,32,16,1,256]{4,2,3,1,0:T(8,128)(2,1)} %param.5) | copy-start | bytes 1572868
  3.7 5.0 %copy-start.2 = (bf16[2,12,16,1,256]{4,2,3,1,0:T(8,128)(2,1)S(1)}, bf16[2,12,16,1,256]{4,2,3,1,0:T(8,128)(2,1)}, u32[]{:S(2)}) copy-start(bf16[2,12,16,1,256]{4,2,3,1,0:T(8,128)(2,1)} %param.6) | copy-start | bytes 589828
  3.7 5.7 %collective-permute-start.3 = (bf16[32,64]{1,0:T(8,128)(2,1)S(1)}, bf16[32,64]{1,0:T(8,128)(2,1)S(1)}, u32[]{:S(2)}, u32[]{:S(2)}) collective-permute-start(bf16[32,64]{1,0:T(8,128)(2,1)S(1)} %broadcast_select_fusion.2.after_ref), channel_id=1, source_target_pairs={{0,24},{1,25},{2,26},{3,27},{4,7},{5,6},{6,5},{7,4},{8,16},{9,17},... | collective-permute-start | bytes 12296 | tf_op jit(solution)/shard_map/ppermute | solution.py:393
  7.6 3.7 %collective-permute-start.2 = (bf16[32,64]{1,0:T(8,128)(2,1)S(1)}, bf16[32,64]{1,0:T(8,128)(2,1)S(1)}, u32[]{:S(2)}, u32[]{:S(2)}) collective-permute-start(bf16[32,64]{1,0:T(8,128)(2,1)S(1)} %broadcast_select_fusion.2.after_ref), channel_id=1, source_target_pairs={{0,16},{1,17},{2,18},{3,19},{4,6},{5,7},{6,4},{7,5},{8,24},{9,25},... | collective-permute-start | bytes 12296 | tf_op jit(solution)/shard_map/ppermute | solution.py:393
  8.1 3.7 %collective-permute-start.1 = (bf16[32,64]{1,0:T(8,128)(2,1)S(1)}, bf16[32,64]{1,0:T(8,128)(2,1)S(1)}, u32[]{:S(2)}, u32[]{:S(2)}) collective-permute-start(bf16[32,64]{1,0:T(8,128)(2,1)S(1)} %broadcast_select_fusion.2.after_ref), channel_id=1, source_target_pairs={{0,8},{1,9},{2,10},{3,11},{4,5},{5,4},{6,7},{7,6},{8,0},{9,1},{10,... | collective-permute-start | bytes 12296 | tf_op jit(solution)/shard_map/ppermute | solution.py:393
  11.8 1.2 %collective-permute-start.6 = (bf16[32,96]{1,0:T(8,128)(2,1)S(1)}, bf16[32,96]{1,0:T(8,128)(2,1)S(1)}, u32[]{:S(2)}, u32[]{:S(2)}) collective-permute-start(bf16[32,96]{1,0:T(8,128)(2,1)S(1)} %maximum_select_fusion.refs_0_.sent_ref), channel_id=1, source_target_pairs={{0,4},{4,0},{8,12},{12,8},{16,20},{20,16},{24,28},{28,24},{1,5},{5... | collective-permute-start | bytes 18440 | tf_op jit(solution)/shard_map/ppermute | solution.py:355
  18.1 4.8 %collective-permute-start.10 = (bf16[24,512]{1,0:T(8,128)(2,1)S(1)}, bf16[24,512]{1,0:T(8,128)(2,1)S(1)}, u32[]{:S(2)}, u32[]{:S(2)}) collective-permute-start(bf16[24,512]{1,0:T(8,128)(2,1)S(1)} %get-tuple-element.50.refs_0_), channel_id=1, source_target_pairs={{0,24},{4,28},{8,16},{12,20},{16,8},{20,12},{24,0},{28,4},{1,25},{... | collective-permute-start | bytes 73736 | tf_op jit(solution)/shard_map/ppermute | solution.py:355
  20.5 3.8 %collective-permute-start.9 = (bf16[24,512]{1,0:T(8,128)(2,1)S(1)}, bf16[24,512]{1,0:T(8,128)(2,1)S(1)}, u32[]{:S(2)}, u32[]{:S(2)}) collective-permute-start(bf16[24,512]{1,0:T(8,128)(2,1)S(1)} %get-tuple-element.50.refs_0_), channel_id=1, source_target_pairs={{0,16},{4,20},{8,24},{12,28},{16,0},{20,4},{24,8},{28,12},{1,17},{... | collective-permute-start | bytes 73736 | tf_op jit(solution)/shard_map/ppermute | solution.py:355
  21.0 3.8 %collective-permute-start.8 = (bf16[24,512]{1,0:T(8,128)(2,1)S(1)}, bf16[24,512]{1,0:T(8,128)(2,1)S(1)}, u32[]{:S(2)}, u32[]{:S(2)}) collective-permute-start(bf16[24,512]{1,0:T(8,128)(2,1)S(1)} %get-tuple-element.50.refs_0_), channel_id=1, source_target_pairs={{0,8},{4,12},{8,0},{12,4},{16,24},{20,28},{24,16},{28,20},{1,9},{5... | collective-permute-start | bytes 73736 | tf_op jit(solution)/shard_map/ppermute | solution.py:355
  30.4 5.1 %collective-permute-start.11 = (bf16[16,64,256]{2,1,0:T(8,128)(2,1)S(1)}, bf16[16,64,256]{2,1,0:T(8,128)(2,1)S(1)}, u32[]{:S(2)}, u32[]{:S(2)}) collective-permute-start(bf16[16,64,256]{2,1,0:T(8,128)(2,1)S(1)} %get-tuple-element.55), channel_id=1, source_target_pairs={{0,4},{4,0},{8,12},{12,8},{16,20},{20,16},{24,28},{28,24},{1,5},{5... | collective-permute-start | bytes 1572872 | tf_op jit(solution)/shard_map/ppermute | solution.py:355
  30.4 12.4 %all-to-all-start = ((bf16[32,4,128]{2,1,0:T(4,128)(2,1)}), bf16[32,4,128]{2,1,0:T(4,128)(2,1)S(1)}, u32[]{:S(2)}, u32[]{:S(2)}) async-start(bf16[32,4,128]{2,1,0:T(4,128)(2,1)} %bitcast.14), calls=%async_computation | async-start | bytes 65536 | tf_op jit(solution)/shard_map/all_to_all | solution.py:549
